TPU v7x, 32 devices: a whole 2x2x4 slice. The times are simulated.
32 devices in a mesh: ctx: 8 (over z, core), exp: 4 (over y, x).
Axes of the slice: x: 2, y: 2, z: 4, core: 2. Of those that a mesh axis runs over, the one named last changes fastest.
Arguments:
- queries: bfloat16 [768, 6144], P('ctx', 'exp'), may hold values from -10 to 10
- rotated_keys: bfloat16 [768, 1024], P('ctx', 'exp'), may hold values from -10 to 10
- values: bfloat16 [768, 1024], P('ctx', 'exp'), may hold values from -6 to 6
- residual: bfloat16 [768, 6144], P('ctx', 'exp'), may hold values from -45 to 45
- span_order: int32 [8], replicated, may hold values from 0 to 7, each once
- norm_gain: bfloat16 [6144], replicated, may hold values from 0.25 to 1.75
- router_weight: bfloat16 [6144, 4], replicated, may hold values from -0.078125 to 0.078125
- expert_ids: int32 [768, 2], P(('ctx', 'exp')), may hold values from 0 to 3, all different within a row; in each aligned block of 24 rows (0 to 23, 24 to 47, ...) at most 18 rows name the same one
- gate_weight: bfloat16 [4, 6144, 8192], P('exp', None, 'ctx'), may hold values from -0.078125 to 0.078125
- up_weight: bfloat16 [4, 6144, 8192], P('exp', None, 'ctx'), may hold values from -0.078125 to 0.078125
- down_weight: bfloat16 [4, 8192, 6144], P('exp', 'ctx'), may hold values from -0.0625 to 0.0625
Outputs:
- layer_out: bfloat16 [768, 6144], P('ctx', 'exp')
Inputs may be any that keep to these rules, and one draw needn't show every extreme that they name: `expert_ids`: each row names two different experts. In each aligned block of 24 rows, no expert is named by more than 18 rows, a bound that some block reaches.
All inputs are finite; a program needn't handle non-finite values.
Results may differ from a plain program's by a relative error of at most 0.012.
Values may be sent and summed in bfloat16 or wider, within the bound.
No kernel may reach another device: no remote copies, remote signals or barrier semaphores. Data moves between devices by JAX's collectives and lax.ppermute only.
A program may use at most 128 MiB of HBM per device.

v0:
```python
import math

import jax
import jax.numpy as jnp
from jax import lax
from jax.sharding import PartitionSpec as P

HEAD_WIDTH = 128


def slot_tables(id_pairs, n_experts, capacity):
    width_a = id_pairs.shape[-2] * id_pairs.shape[-1]
    flat_ids = id_pairs.reshape(id_pairs.shape[:-2] + (width_a,))
    expert_hot = (flat_ids[..., None] == jnp.arange(n_experts, dtype=jnp.int32)).astype(jnp.int32)
    earlier = jnp.cumsum(expert_hot, axis=-2) - expert_hot
    slot_index = jnp.sum(earlier * expert_hot, axis=-1)
    slot_hot = (slot_index[..., None] == jnp.arange(capacity, dtype=jnp.int32)).astype(jnp.float32)
    slot_table = expert_hot.astype(jnp.float32)[..., :, :, None] * slot_hot[..., :, None, :]
    return jnp.moveaxis(slot_table, -3, -1)


def body(
    queries,
    rotated_keys,
    values,
    residual,
    span_order,
    norm_gain,
    router_weight,
    expert_ids,
    gate_weight,
    up_weight,
    down_weight,
):
    tok_ctx = queries.shape[0]
    n_exp = lax.axis_size("exp")
    kv_local = rotated_keys.shape[1] // HEAD_WIDTH
    query_group_width = queries.shape[1] // HEAD_WIDTH // kv_local
    ctx_index = lax.axis_index("ctx")
    span_ids = jnp.arange(span_order.shape[0], dtype=jnp.int32)
    own_span = jnp.sum(jnp.where(span_ids == ctx_index, span_order, 0))
    query_pos = own_span * tok_ctx + jnp.arange(tok_ctx, dtype=jnp.int32)
    query_head_rows = queries.reshape(tok_ctx, kv_local, query_group_width, HEAD_WIDTH)
    logit_scale_factor = 1.0 / math.sqrt(HEAD_WIDTH)
    running_max = jnp.full((kv_local, query_group_width, tok_ctx), -1e30, jnp.float32)
    key_piece = lax.all_gather(rotated_keys, "ctx", axis=0, tiled=True)
    value_piece = lax.all_gather(values, "ctx", axis=0, tiled=True)
    row_count = key_piece.shape[0]
    key_rows = jnp.arange(row_count, dtype=jnp.int32)
    key_span = key_rows // tok_ctx
    key_start = jnp.sum(
        jnp.where(key_span[:, None] == span_ids[None, :], span_order[None, :], 0), axis=1
    )
    key_pos = key_start * tok_ctx + key_rows % tok_ctx
    visible = key_pos[None, :] <= query_pos[:, None]
    key_head_rows = key_piece.reshape(row_count, kv_local, HEAD_WIDTH)
    value_head_rows = value_piece.reshape(row_count, kv_local, HEAD_WIDTH)
    attention_logits = (
        jnp.einsum(
            "tkgd,skd->kgts", query_head_rows, key_head_rows, preferred_element_type=jnp.float32
        )
        * logit_scale_factor
    )
    masked = jnp.where(visible, attention_logits, -jnp.inf)
    new_max = jnp.maximum(running_max, jnp.max(masked, axis=-1))
    weights = jnp.where(visible, jnp.exp(attention_logits - new_max[..., None]), 0.0)
    new_sum = jnp.sum(weights, axis=-1)
    new_acc = jnp.einsum(
        "kgts,skd->kgtd",
        weights.astype(jnp.bfloat16),
        value_head_rows,
        preferred_element_type=jnp.float32,
    )
    attended = (
        (new_acc / new_sum[..., None])
        .transpose(2, 0, 1, 3)
        .reshape(tok_ctx, kv_local * query_group_width * HEAD_WIDTH)
    )
    hidden = (residual.astype(jnp.float32) + attended).astype(jnp.bfloat16)
    tok_sub = tok_ctx // n_exp
    experts_n = n_exp * gate_weight.shape[0]
    capacity = max(2, min(tok_sub, 3 * tok_sub // experts_n))
    d_model = norm_gain.shape[0]
    gate_local = gate_weight[0]
    up_local = up_weight[0]
    down_local = down_weight[0]
    expert_range = jnp.arange(experts_n, dtype=jnp.int32)
    token_rows = lax.all_to_all(hidden, "exp", split_axis=0, concat_axis=1, tiled=True)
    token_f = token_rows.astype(jnp.float32)
    mean_sq = jnp.mean(token_f * token_f, axis=-1, keepdims=True)
    normed = (token_f * lax.rsqrt(mean_sq + 1e-05) * norm_gain.astype(jnp.float32)).astype(
        jnp.bfloat16
    )
    logits = jnp.dot(normed, router_weight, preferred_element_type=jnp.float32)
    tables = slot_tables(expert_ids, experts_n, capacity)
    token_tables = jnp.sum(tables.reshape(experts_n, capacity, tok_sub, 2), axis=-1)
    buffer = jnp.einsum(
        "ect,td->ecd", token_tables.astype(jnp.bfloat16), normed, preferred_element_type=jnp.float32
    ).astype(jnp.bfloat16)
    received = lax.all_to_all(buffer, "exp", split_axis=0, concat_axis=0, tiled=True)
    block_count, slot_count, feat_count = received.shape
    row_count = block_count * slot_count
    flat_rows = received.reshape(row_count, feat_count)
    row_piece = lax.all_gather(flat_rows, "ctx", axis=0, tiled=True)
    gate_val = jnp.dot(row_piece, gate_local, preferred_element_type=jnp.float32)
    up_val = jnp.dot(row_piece, up_local, preferred_element_type=jnp.float32)
    activation = (jax.nn.silu(gate_val) * up_val).astype(jnp.bfloat16)
    summed = lax.psum_scatter(
        jnp.dot(activation, down_local, preferred_element_type=jnp.float32).astype(jnp.bfloat16),
        "ctx",
        scatter_dimension=0,
        tiled=True,
    )
    local_out = summed.reshape(block_count, slot_count, feat_count)
    picked_y = lax.all_to_all(local_out, "exp", split_axis=0, concat_axis=0, tiled=True)
    picked = jnp.einsum(
        "eca,ecd->ad", tables.astype(jnp.bfloat16), picked_y, preferred_element_type=jnp.float32
    ).reshape(tok_sub, 2, d_model)
    id_hot = (expert_ids[..., None] == expert_range).astype(jnp.float32)
    chosen = jnp.sum(logits[:, None, :] * id_hot, axis=-1)
    mix_weight = jax.nn.sigmoid(chosen - chosen[:, ::-1])
    merged = (token_f + jnp.sum(mix_weight[..., None] * picked, axis=1)).astype(jnp.bfloat16)
    layer_out = lax.all_to_all(merged, "exp", split_axis=1, concat_axis=0, tiled=True)
    return layer_out


def solution(mesh):
    return jax.shard_map(
        body,
        mesh=mesh,
        in_specs=(
            P("ctx", "exp"),
            P("ctx", "exp"),
            P("ctx", "exp"),
            P("ctx", "exp"),
            P(),
            P(),
            P(),
            P(("ctx", "exp"), None),
            P("exp", None, "ctx"),
            P("exp", None, "ctx"),
            P("exp", "ctx", None),
        ),
        out_specs=P("ctx", "exp"),
        check_vma=False,
    )
```

profile of v0, /device:TPU:9, one launch (start us, length us, event | category | flops | bytes accessed | tf_op | source)
XLA Modules:
  0.0 296.2 jit_solution(2498283641194504753)
XLA Ops:
  6.6 0.7 select_reduce_fusion.1
  7.3 1.3 fusion.45
  9.3 15.5 %all_gather.9 = bf16[768,256]{1,0:T(8,128)(2,1)S(1)} all-gather(bf16[96,256]{1,0:T(8,128)(2,1)} %param.12), channel_id=1, replica_groups=mesh['ctx'=8,'exp'=4] {'ctx'}, dimensions={0}, use_global_device_ids=true | all-gather | bytes 442368 | tf_op jit(solution)/shard_map/all_gather | solution.py:46
  24.7 0.2 copy.76
  24.9 1.3 reshape.136
  26.2 0.1 broadcast_compare_fusion
  26.3 2.4 fusion.9
  28.8 14.5 %all_gather.10 = bf16[768,256]{1,0:T(8,128)(2,1)S(1)} all-gather(bf16[96,256]{1,0:T(8,128)(2,1)S(1)} %copy-done.3), channel_id=1, replica_groups=mesh['ctx'=8,'exp'=4] {'ctx'}, dimensions={0}, use_global_device_ids=true | all-gather | bytes 442368 | tf_op jit(solution)/shard_map/all_gather | solution.py:47
  43.3 0.2 copy.79
  43.5 3.2 %fusion.12 = f32[2,6,96]{2,1,0:T(8,128)S(1)} fusion(f32[2,768,96,6]{1,2,3,0:T(8,128)} %get-tuple-element.6, f32[2,6,96]{2,1,0:T(8,128)S(1)} %broadcast_maximum_fusion, pred[96,768]{1,0:T(8,128)(4,1)S(1)} %broadcast_compare_fusion), kind=kLoop, calls=%fused_computation.14 | loop fusion | flops 3537792 | bytes 3621888 | tf_op jit(solution)/shard_map/reduce_sum | solution.py:67
  46.6 1.0 fusion.22
  47.6 0.4 copy.81
  48.0 0.1 reshape.138
  48.2 0.8 add_convert_fusion
  48.9 3.5 %all-to-all-start = ((bf16[4,24,1536]{2,1,0:T(8,128)(2,1)}), bf16[4,24,1536]{2,1,0:T(8,128)(2,1)S(1)}, u32[]{:S(2)}, u32[]{:S(2)}) async-start(bf16[4,24,1536]{2,1,0:T(8,128)(2,1)} %bitcast.7), calls=%async_computation | async-start | bytes 589824 | tf_op jit(solution)/shard_map/all_to_all | solution.py:88
  52.4 0.0 all-gather.2.cloned.1.call-start
  52.4 0.1 copy.84
  52.5 0.1 eq.102
  52.6 0.1 fusion.34
  52.7 0.1 reduce_window_sum.11
  52.8 0.2 select_reduce_fusion
  53.0 0.1 eq.115
  53.1 0.1 copy.85
  53.2 4.3 %all-to-all-done = bf16[4,24,1536]{2,1,0:T(8,128)(2,1)S(1)} async-done(((bf16[4,24,1536]{2,1,0:T(8,128)(2,1)}), bf16[4,24,1536]{2,1,0:T(8,128)(2,1)S(1)}, u32[]{:S(2)}, u32[]{:S(2)}) %all-to-all-start) | async-done | bytes 294944 | tf_op jit(solution)/shard_map/all_to_all | solution.py:88
  57.7 0.2 fusion.27
  57.9 0.5 convolution_convert_fusion
  58.4 16.0 %all_to_all.39 = bf16[4,18,6144]{2,1,0:T(8,128)(2,1)S(1)} all-to-all(bf16[4,18,6144]{2,1,0:T(8,128)(2,1)S(1)} %convolution_convert_fusion), channel_id=1, replica_groups=mesh['ctx'=8,'exp'=4] {'exp'}, dimensions={0} | all-to-all | bytes 1769472 | tf_op jit(solution)/shard_map/all_to_all | solution.py:100
  74.4 1.2 reshape.139
  75.6 0.0 all-gather.2.cloned.1.call-update
  75.7 0.2 reduce-scatter.2.cloned.1.call-start
  75.9 70.8 %all-gather.2.cloned.1.call-done = bf16[576,6144]{1,0:T(8,128)(2,1)} async-done(((bf16[72,6144]{1,0:T(8,128)(2,1)}), bf16[576,6144]{1,0:T(8,128)(2,1)}) %all-gather.2.cloned.1.call-update) | async-done | bytes 7077904 | tf_op jit(solution)/shard_map/all_gather | solution.py:104
  146.7 12.6 %fusion.2 = f32[576,1024]{1,0:T(8,128)S(1)} fusion(bf16[576,6144]{1,0:T(8,128)(2,1)} %all-gather.2.cloned.1.call-done, bf16[1,6144,1024]{2,1,0:T(8,128)(2,1)} %param.20), kind=kOutput, calls=%fused_computation.2 | convolution fusion | flops 7247757312 | bytes 22020096 | tf_op jit(solution)/shard_map/dot_general | solution.py:106
  159.3 0.0 slice-start.2
  159.3 11.1 %multiply_convert_fusion = bf16[576,1024]{1,0:T(8,128)(2,1)S(1)} fusion(f32[576,1024]{1,0:T(8,128)S(1)} %fusion.2, bf16[576,6144]{1,0:T(8,128)(2,1)S(1)} %copy-done.6, bf16[1,6144,1024]{2,1,0:T(8,128)(2,1)} %param.19), kind=kOutput, calls=%fused_computation.16 | convolution fusion | flops 7251296256 | bytes 23199744 | tf_op jit(solution)/shard_map/dot_general | solution.py:105
  170.5 9.3 %fusion.6 = bf16[576,6144]{1,0:T(8,128)(2,1)} fusion(bf16[576,1024]{1,0:T(8,128)(2,1)S(1)} %multiply_convert_fusion, bf16[1,1024,6144]{2,1,0:T(8,128)(2,1)S(1)} %bitcast.86), kind=kOutput, calls=%fused_computation.6 | convolution fusion | flops 7251296256 | bytes 20840448 | tf_op jit(solution)/shard_map/dot_general | solution.py:109
  179.8 0.0 reduce-scatter.2.cloned.1.call-update
  179.9 76.5 %reduce-scatter.2.cloned.1.call-done = bf16[72,6144]{1,0:T(8,128)(2,1)} async-done(((bf16[576,6144]{1,0:T(8,128)(2,1)}), bf16[72,6144]{1,0:T(8,128)(2,1)}) %reduce-scatter.2.cloned.1.call-update) | async-done | bytes 884752 | tf_op jit(solution)/shard_map/reduce_scatter | solution.py:108
  256.4 2.5 reshape.140
  258.9 3.5 %all-to-all-start.2 = ((bf16[4,18,6144]{2,1,0:T(8,128)(2,1)}), bf16[4,18,6144]{2,1,0:T(8,128)(2,1)S(1)}, u32[]{:S(2)}, u32[]{:S(2)}) async-start(bf16[4,18,6144]{2,1,0:T(8,128)(2,1)} %reshape.140), calls=%async_computation.3 | async-start | bytes 2359296 | tf_op jit(solution)/shard_map/all_to_all | solution.py:115
  262.4 0.3 fusion.48
  262.8 0.1 copy.83
  262.9 15.1 %all-to-all-done.2 = bf16[4,18,6144]{2,1,0:T(8,128)(2,1)S(1)} async-done(((bf16[4,18,6144]{2,1,0:T(8,128)(2,1)}), bf16[4,18,6144]{2,1,0:T(8,128)(2,1)S(1)}, u32[]{:S(2)}, u32[]{:S(2)}) %all-to-all-start.2) | async-done | bytes 884768 | tf_op jit(solution)/shard_map/all_to_all | solution.py:115
  277.9 0.4 convolution_bitcast_fusion
  278.3 0.7 reshape.141
  279.0 1.6 multiply_reduce_fusion
  280.6 0.1 fusion.28
  280.7 7.9 %all_to_all.40 = bf16[24,4,1536]{2,0,1:T(8,128)(2,1)S(1)} all-to-all(bf16[24,4,1536]{2,0,1:T(8,128)(2,1)S(1)} %fusion.28), channel_id=1, replica_groups=mesh['ctx'=8,'exp'=4] {'exp'}, dimensions={1} | all-to-all | bytes 589824 | tf_op jit(solution)/shard_map/all_to_all | solution.py:123
  288.6 0.7 copy.104
  (36 shorter events, 0.3 us)
Async XLA Ops:
  6.5 255.9 %copy-start = (bf16[6144,4]{0,1:T(4,128)(2,1)S(1)}, bf16[6144,4]{0,1:T(4,128)(2,1)}, u32[]{:S(2)}) copy-start(bf16[6144,4]{0,1:T(4,128)(2,1)} %param.17) | copy-start | bytes 147460
  6.5 22.2 %copy-start.3 = (bf16[96,256]{1,0:T(8,128)(2,1)S(1)}, bf16[96,256]{1,0:T(8,128)(2,1)}, u32[]{:S(2)}) copy-start(bf16[96,256]{1,0:T(8,128)(2,1)} %param.13) | copy-start | bytes 147460
  43.4 3.2 %copy-start.1 = (f32[2,768,96,6]{1,2,3,0:T(8,128)S(1)}, f32[2,768,96,6]{1,2,3,0:T(8,128)}, u32[]{:S(2)}) copy-start(f32[2,768,96,6]{1,2,3,0:T(8,128)} %get-tuple-element.6) | copy-start | bytes 10616836
  46.6 1.5 copy-start.2
  47.6 4.8 %copy-start.5 = (s32[24,2]{0,1:T(2,128)S(1)}, s32[24,2]{0,1:T(2,128)}, u32[]{:S(2)}) copy-start(s32[24,2]{0,1:T(2,128)} %param.18) | copy-start | bytes 580
  47.6 5.6 %copy-start.4 = (bf16[6144]{0:T(1024)(128)(2,1)S(1)}, bf16[6144]{0:T(1024)(128)(2,1)}, u32[]{:S(2)}) copy-start(bf16[6144]{0:T(1024)(128)(2,1)} %param.16) | copy-start | bytes 36868
  48.9 8.6 %all-to-all-start = ((bf16[4,24,1536]{2,1,0:T(8,128)(2,1)}), bf16[4,24,1536]{2,1,0:T(8,128)(2,1)S(1)}, u32[]{:S(2)}, u32[]{:S(2)}) async-start(bf16[4,24,1536]{2,1,0:T(8,128)(2,1)} %bitcast.7), calls=%async_computation | async-start | bytes 589824 | tf_op jit(solution)/shard_map/all_to_all | solution.py:88
  52.4 94.3 %all-gather.2.cloned.1.call-start = ((), (), s32[]{:S(2)}) async-start(), calls=%async_computation.5 | async-start | bytes 7962624 | tf_op jit(solution)/shard_map/all_gather | solution.py:104
  75.7 180.7 %reduce-scatter.2.cloned.1.call-start = ((), (), s32[]{:S(2)}) async-start(), calls=%async_computation.6 | async-start | bytes 7962624 | tf_op jit(solution)/shard_map/reduce_scatter | solution.py:108
  146.7 12.6 %copy-start.6 = (bf16[576,6144]{1,0:T(8,128)(2,1)S(1)}, bf16[576,6144]{1,0:T(8,128)(2,1)}, u32[]{:S(2)}) copy-start(bf16[576,6144]{1,0:T(8,128)(2,1)} %all-gather.2.cloned.1.call-done) | copy-start | bytes 21233668
  146.7 23.8 %slice-start = ((s8[12582912]{0:T(1024)(128)(4,1)}), s8[4194304]{0:T(1024)(128)(4,1)S(1)}, s32[]{:S(2)}) async-start(s8[12582912]{0:T(1024)(128)(4,1)} %bitcast.85), calls=%async_computation.7 | async-start | bytes 8388608
  146.7 23.8 %slice-start.1 = ((s8[12582912]{0:T(1024)(128)(4,1)}), s8[4194304]{0:T(1024)(128)(4,1)S(1)}, s32[]{:S(2)}) async-start(s8[12582912]{0:T(1024)(128)(4,1)} %bitcast.85), calls=%async_computation.8 | async-start | bytes 8388608
  159.3 11.2 %slice-start.2 = ((s8[12582912]{0:T(1024)(128)(4,1)}), s8[4194304]{0:T(1024)(128)(4,1)S(1)}, s32[]{:S(2)}) async-start(s8[12582912]{0:T(1024)(128)(4,1)} %bitcast.85), calls=%async_computation.9 | async-start | bytes 8388608
  258.9 19.1 %all-to-all-start.2 = ((bf16[4,18,6144]{2,1,0:T(8,128)(2,1)}), bf16[4,18,6144]{2,1,0:T(8,128)(2,1)S(1)}, u32[]{:S(2)}, u32[]{:S(2)}) async-start(bf16[4,18,6144]{2,1,0:T(8,128)(2,1)} %reshape.140), calls=%async_computation.3 | async-start | bytes 2359296 | tf_op jit(solution)/shard_map/all_to_all | solution.py:115
Sparse Core Ops, SparseCore 0:
  75.8 70.8 all-gather.1
  180.0 76.3 reduce-scatter.1
where the time goes:
time: 298 us; the launch traced here: 296 us
  waiting for transfers between devices  167 us (56%)
  blocking collectives  53.9 us (18%)
  matrix products  37.6 us (13%)
  between operations  14.4 us (5%)
  other arithmetic  8.44 us (3%)
  local copies, waits for them, and re-layouts  7.79 us (3%)
  starting transfers between devices  7.25 us (2%)
    reduce_scatter x1, waiting for transfers between devices, body(): lax.psum_scatter(jnp.dot(activation, down_local, preferred_element_type=j...  76.5 us
    all_gather x1, waiting for transfers between devices, body(): row_piece = lax.all_gather(flat_rows, 'ctx', axis=0, tiled=True)  70.8 us
    all_to_all x1, blocking collectives, body(): lax.all_to_all(buffer, 'exp', split_axis=0, concat_axis=0, tiled=True)  16 us
    all_gather x1, blocking collectives, body(): key_piece = lax.all_gather(rotated_keys, 'ctx', axis=0, tiled=True)  15.5 us
    all_to_all x1, waiting for transfers between devices, body(): lax.all_to_all(local_out, 'exp', split_axis=0, concat_axis=0, tiled=True)  15.1 us
    all_gather x1, blocking collectives, body(): value_piece = lax.all_gather(values, 'ctx', axis=0, tiled=True)  14.5 us
    dot_general x1, matrix products, body(): up_val = jnp.dot(row_piece, up_local, preferred_element_type=jnp.float32)  12.6 us
    dot_general x1, matrix products, body(): jnp.dot(row_piece, gate_local, preferred_element_type=jnp.float32)  11.1 us
  transfers between devices with their start and end apart: 4, of which 4 were waited for; matrix products, arithmetic and copies ran while one was open for 0% of the time, Pallas kernels for 0%

commit v1 on v0

v1 whole, which is shorter than its diff:
```python
import functools
import math

import jax
import jax.numpy as jnp
from jax import lax
from jax.experimental import pallas as pl
from jax.experimental.pallas import tpu as pltpu
from jax.sharding import PartitionSpec as P

HEAD_WIDTH = 128
TILE = 16
LANES = 128
F32, BF16 = jnp.float32, jnp.bfloat16
MIB = 2**20
VMEM = pl.BlockSpec(memory_space=pltpu.VMEM)
ANY = pl.BlockSpec(memory_space=pl.ANY)
SMEM = pl.BlockSpec(memory_space=pltpu.SMEM)


def call(kernel, inputs, specs, shapes, limit, scratch=(), flops=0, moved=0, after=()):
    n = len(inputs)

    def ordered(*refs):
        kernel(*refs[:n], *refs[n + len(after) :])

    return pl.pallas_call(
        ordered,
        in_specs=list(specs) + [ANY] * len(after),
        out_specs=[VMEM] * len(shapes),
        out_shape=[jax.ShapeDtypeStruct(s, d) for s, d in shapes],
        scratch_shapes=list(scratch),
        compiler_params=pltpu.CompilerParams(vmem_limit_bytes=limit * MIB),
        cost_estimate=pl.CostEstimate(flops=flops, bytes_accessed=moved, transcendentals=0),
    )(*inputs, *after)


def pack_kernel(
    where_ref, ids_ref, k_ref, v_ref, q_ref, res_ref, out_ref, row_ref, q_out, res_out, ids_vmem, sems
):
    kv = k_ref.shape[1]
    sub = ids_ref.shape[1]
    copies = [
        pltpu.make_async_copy(ids_ref, ids_vmem, sems.at[0]),
        pltpu.make_async_copy(k_ref, out_ref.at[:, :kv], sems.at[1]),
        pltpu.make_async_copy(v_ref, out_ref.at[:, kv:], sems.at[2]),
        pltpu.make_async_copy(q_ref, q_out, sems.at[3]),
        pltpu.make_async_copy(res_ref, res_out, sems.at[4]),
    ]
    for copy in copies:
        copy.start()
    copies[0].wait()
    row = lax.broadcasted_iota(jnp.int32, (TILE, sub), 0)
    two = jnp.where(row == 0, ids_vmem[0:1, :], jnp.where(row == 1, ids_vmem[1:2, :], 0))
    token = lax.broadcasted_iota(jnp.int32, (sub, LANES), 0) + where_ref[1] * sub
    lane = lax.broadcasted_iota(jnp.int32, (sub, LANES), 1)
    place = (token == lane).astype(F32)
    row_ref[...] = jnp.dot(two.astype(F32), place, preferred_element_type=F32).astype(BF16)
    for copy in copies[1:]:
        copy.wait()


def join_kernel(n, *refs):
    spans, rows, (out_ref, row_ref) = refs[:n], refs[n:-2], refs[-2:]
    tok = spans[0].shape[0]
    for d in range(n):
        out_ref[d * tok : (d + 1) * tok, :] = spans[d][...]
    total = rows[0][...].astype(F32)
    for other in rows[1:]:
        total += other[...].astype(F32)
    row_ref[...] = total.astype(BF16)


def attention_kernel(n, where_ref, q_ref, res_ref, near_ref, far_ref, row_ref, hid_ref):
    tok, width = q_ref.shape
    kv = near_ref.shape[1] // 2
    heads = kv // HEAD_WIDTH
    group = width // kv
    ctx = where_ref[0]
    chip, core = ctx // 2, ctx % 2
    own = where_ref[2 + ctx] * tok
    ahead = lax.broadcasted_iota(jnp.int32, (tok, tok), 0) - lax.broadcasted_iota(
        jnp.int32, (tok, tok), 1
    )
    pieces = []
    for side in (core, 1 - core):
        for d in range(n):
            span = 2 * ((chip + d) % n) + side
            pieces.append(jnp.where(ahead >= where_ref[2 + span] * tok - own, 0.0, -1e30))
    bias = jnp.concatenate(pieces, axis=1)
    bias = jnp.concatenate([bias] * group, axis=0)
    for h in range(heads):
        cols = slice(h * HEAD_WIDTH, (h + 1) * HEAD_WIDTH)
        vals = slice(kv + h * HEAD_WIDTH, kv + (h + 1) * HEAD_WIDTH)
        key = jnp.concatenate([near_ref[:, cols], far_ref[:, cols]], axis=0)
        value = jnp.concatenate([near_ref[:, vals], far_ref[:, vals]], axis=0)
        base = h * group * HEAD_WIDTH
        q = jnp.concatenate(
            [q_ref[:, base + g * HEAD_WIDTH : base + (g + 1) * HEAD_WIDTH] for g in range(group)],
            axis=0,
        )
        s = lax.dot_general(q, key, (((1,), (1,)), ((), ())), preferred_element_type=F32)
        s = s * (1.0 / math.sqrt(HEAD_WIDTH)) + bias
        w = jnp.exp(s - jnp.max(s, axis=1, keepdims=True))
        total = jnp.sum(w, axis=1, keepdims=True)
        att = jnp.dot(w.astype(BF16), value, preferred_element_type=F32) / total
        for g in range(group):
            at = slice(base + g * HEAD_WIDTH, base + (g + 1) * HEAD_WIDTH)
            rows = att[g * tok : (g + 1) * tok]
            hid_ref[:tok, at] = (res_ref[:, at].astype(F32) + rows).astype(BF16)
    hid_ref[tok:, :] = jnp.zeros((TILE, width), BF16)
    hid_ref[tok:, :LANES] = row_ref[...]


def pick_kernel(n_exp, slots, tok, n, where_ref, *refs):
    blocks, refs = refs[:n], refs[n:]
    outs, takes, others = refs[:n_exp], refs[n_exp : n_exp + n], refs[n_exp + n :]
    exp = where_ref[1]
    earlier = (
        lax.broadcasted_iota(jnp.int32, (LANES, LANES), 0)
        < lax.broadcasted_iota(jnp.int32, (LANES, LANES), 1)
    ).astype(BF16)
    row = lax.broadcasted_iota(jnp.int32, (TILE, LANES), 0)
    lane = lax.broadcasted_iota(jnp.int32, (TILE, LANES), 1)
    slot = lax.broadcasted_iota(jnp.int32, (slots, LANES), 0).astype(F32)
    target = (exp ^ row).astype(F32)
    chosen = []
    for i in range(n):
        both = blocks[i][tok:, :LANES].astype(F32)
        first, second = both[0:1, :], both[1:2, :]
        sent = jnp.where(((first == target) | (second == target)) & (lane < tok), 1.0, 0.0)
        rank = jnp.dot(sent.astype(BF16), earlier, preferred_element_type=F32)
        chosen.append([])
        for k in range(n_exp):
            one = jnp.where(slot == rank[k : k + 1, :], sent[k : k + 1, :], 0.0)
            take = one[:, :tok].astype(BF16)
            takes[i][k] = take
            chosen[i].append(take)
            if k == 0:
                other = jnp.sum(one * (first + second), axis=1, keepdims=True) - exp.astype(F32)
                others[i][...] = jnp.broadcast_to(other, (slots, LANES))
    for k in range(n_exp):
        rows = [
            jnp.dot(chosen[i][k], blocks[i][:tok, :], preferred_element_type=F32)
            for i in range(n)
        ]
        outs[k][...] = (rows[0] if n == 1 else jnp.concatenate(rows, axis=0)).astype(BF16)


def norm_kernel(n_exp, n, parts, where_ref, gain_ref, router_ref, *refs):
    others, pieces, (out_ref, mix_ref) = refs[:n], refs[n:-2], refs[-2:]
    exp = where_ref[1]
    width = pieces[0].shape[1]
    rows = out_ref.shape[0]

    def load(k):
        held = [pieces[p * n_exp + k][...].astype(F32) for p in range(parts)]
        return held[0] if parts == 1 else jnp.concatenate(held, axis=0)

    square = jnp.zeros((rows, 1), F32)
    for k in range(n_exp):
        x = load(k)
        square += jnp.sum(x * x, axis=1, keepdims=True)
    scale = lax.rsqrt(square * (1.0 / (n_exp * width)) + 1e-05)
    logits = jnp.zeros((rows, router_ref.shape[0]), F32)
    for k in range(n_exp):
        at = pl.ds(pl.multiple_of((exp ^ k) * width, width), width)
        normed = (load(k) * scale * gain_ref[:, at].astype(F32)).astype(BF16)
        out_ref[:, at] = normed
        logits += lax.dot_general(
            normed, router_ref[:, at], (((1,), (1,)), ((), ())), preferred_element_type=F32
        )
    col = lax.broadcasted_iota(jnp.int32, logits.shape, 1)
    other = jnp.concatenate([o[...] for o in others], axis=0)[:, :1]
    own = jnp.sum(jnp.where(col == exp, logits, 0.0), axis=1, keepdims=True)
    rival = jnp.sum(jnp.where(col.astype(F32) == other, logits, 0.0), axis=1, keepdims=True)
    mix = 1.0 / (1.0 + jnp.exp(rival - own))
    mix_ref[...] = jnp.broadcast_to(mix, (rows, LANES))


def up_kernel(n, near_ref, far_ref, g_ref, u_ref, act_ref, x_ref, acc, buf, sems):
    rows = near_ref.shape[0]
    depth = g_ref.shape[1] // n
    slots = buf.shape[0]

    def copy(j):
        part = (g_ref, u_ref)[j // n].at[0, (j % n) * depth : (j % n + 1) * depth, :]
        return pltpu.make_async_copy(part, buf.at[j % slots], sems.at[j % slots])

    for j in range(slots):
        copy(j).start()
    x_ref[:rows, :] = near_ref[...]
    x_ref[rows:, :] = far_ref[...]
    for j in range(2 * n):
        copy(j).wait()
        at = slice((j % n) * depth, (j % n + 1) * depth)
        y = jnp.dot(x_ref[:, at], buf[j % slots], preferred_element_type=F32)
        if j % n == 0:
            acc[j // n] = y
        elif j < 2 * n - 1:
            acc[j // n] += y
        else:
            g = acc[0]
            act_ref[...] = (g * (acc[1] + y) / (1.0 + jnp.exp(-g))).astype(BF16)
        if j + slots < 2 * n:
            copy(j + slots).start()


def down_kernel(ks, where_ref, act_ref, d_ref, near_out, far_out, buf, sems):
    exp = where_ref[1]
    rows = near_out.shape[0]
    width = buf.shape[2]
    copies = []
    for j, k in enumerate(ks):
        at = pl.ds(pl.multiple_of((exp ^ k) * width, width), width)
        copies.append(pltpu.make_async_copy(d_ref.at[0, :, at], buf.at[j], sems.at[j]))
    for copy in copies:
        copy.start()
    for j in range(len(ks)):
        copies[j].wait()
        y = jnp.dot(act_ref[...], buf[j], preferred_element_type=F32).astype(BF16)
        near_out[:, j * width : (j + 1) * width] = y[:rows]
        far_out[:, j * width : (j + 1) * width] = y[rows:]


def scale_kernel(n, near_ref, back_ref, mix_ref, *outs):
    width = outs[0].shape[1]
    mix = mix_ref[:, :1]
    for j in range(n):
        at = slice(j * width, (j + 1) * width)
        both = near_ref[:, at].astype(F32) + back_ref[:, at].astype(F32)
        outs[j][...] = (both * mix).astype(BF16)


def spread_kernel(n_exp, n, *refs):
    takes, parts, outs = refs[:n], refs[n : n + n_exp], refs[n + n_exp :]
    slots = takes[0].shape[1]
    for i in range(n):
        total = None
        for k in range(n_exp):
            rows = parts[k][...].astype(F32)[i * slots : (i + 1) * slots].astype(BF16)
            one = lax.dot_general(
                takes[i][k], rows, (((0,), (0,)), ((), ())), preferred_element_type=F32
            )
            total = one if total is None else total + one
        outs[i][...] = total.astype(outs[i].dtype)


def body(
    queries,
    rotated_keys,
    values,
    residual,
    span_order,
    norm_gain,
    router_weight,
    expert_ids,
    gate_weight,
    up_weight,
    down_weight,
):
    tok, width = queries.shape
    n_ctx, n_exp = lax.axis_size("ctx"), lax.axis_size("exp")
    n_chip = n_ctx // 2
    kv = rotated_keys.shape[1]
    sub = tok // n_exp
    experts = n_exp * gate_weight.shape[0]
    cap = max(2, min(sub, 3 * sub // experts))
    slots = n_exp * cap
    d_model = norm_gain.shape[0]
    where = jnp.concatenate(
        [jnp.stack([lax.axis_index("ctx"), lax.axis_index("exp")]).astype(jnp.int32), span_order]
    )

    def from_chip(x, d):
        pairs = [(2 * ((i // 2 + d) % n_chip) + i % 2, i) for i in range(n_ctx)]
        return lax.ppermute(x, "ctx", pairs) if d else x

    def from_core(x):
        return lax.ppermute(x, "ctx", [(i ^ 1, i) for i in range(n_ctx)])

    def from_peer(x, k):
        return lax.ppermute(x, "exp", [(i ^ k, i) for i in range(n_exp)]) if k else x

    packed, id_row, q_near, res_near = call(
        pack_kernel,
        (
            where,
            *[
                pltpu.with_memory_space_constraint(x, pltpu.HBM)
                for x in (expert_ids.T, rotated_keys, values, queries, residual)
            ],
        ),
        [SMEM] + [ANY] * 5,
        [((tok, 2 * kv), BF16), ((TILE, LANES), BF16)] + [((tok, width), BF16)] * 2,
        4,
        [pltpu.VMEM((2, sub), jnp.int32), pltpu.SemaphoreType.DMA((5,))],
    )
    near = [from_chip(packed, d) for d in range(n_chip)]
    id_rows = [from_peer(id_row, k) for k in range(n_exp)]
    joined, id_all = call(
        functools.partial(join_kernel, n_chip),
        (*near, *id_rows),
        [VMEM] * (n_chip + n_exp),
        [((n_chip * tok, 2 * kv), BF16), ((TILE, LANES), BF16)],
        4,
    )
    score_mib = 4 * width // HEAD_WIDTH * tok * n_ctx * tok // (kv // HEAD_WIDTH) // MIB
    (hidden,) = call(
        functools.partial(attention_kernel, n_chip),
        (where, q_near, res_near, joined, from_core(joined), id_all),
        [SMEM] + [VMEM] * 5,
        [((tok + TILE, width), BF16)],
        8 + 4 * score_mib,
    )
    hidden_units = gate_weight.shape[2]
    gain = norm_gain.reshape(1, d_model)
    router = router_weight.T

    half = n_chip // 2
    forward = list(range(half)) + list(range(n_chip - 1, half - 1, -1))
    groups = [forward[:half], forward[half:]]
    takes, others, pieces = {}, {}, {}

    def pick(ds, blocks, after=()):
        n = len(ds)
        got = call(
            functools.partial(pick_kernel, n_exp, slots, tok, n),
            (where, *blocks),
            [SMEM] + [VMEM] * n,
            [((n * slots, width), BF16)] * n_exp
            + [((n_exp, slots, tok), BF16)] * n
            + [((slots, LANES), F32)] * n,
            10,
            after=after,
        )
        for i, d in enumerate(ds):
            takes[d], others[d] = got[n_exp + i], got[n_exp + n + i]
        pieces[ds[0]] = [from_peer(got[k], k) for k in range(n_exp)]

    messages = [m for m in (groups[0][:1], groups[0][1:], groups[1]) if m]
    pick(messages[0], [hidden])
    arriving = {1: from_chip(hidden, 1)}
    for d in range(2, half):
        arriving[d] = from_chip(arriving[d - 1], 1)
    for d in range(n_chip - 1, half, -1):
        arriving[d] = from_chip(hidden if d == n_chip - 1 else arriving[d + 1], n_chip - 1)
    if half > 1:
        pick(
            messages[1],
            [arriving[d] for d in messages[1]],
            (*pieces[0][1:], arriving[n_chip - 1]),
        )
        arriving[half] = from_chip(arriving[half - 1], 1)
    pick(messages[-1], [arriving[d] for d in messages[-1]])
    picked_all = (others[messages[-1][0]],)

    def take_in(ds, after=()):
        sets = [pieces[d] for d in ds if d in pieces]
        parts = [p for part in sets for p in part]
        rows = len(ds) * slots
        return call(
            functools.partial(norm_kernel, n_exp, len(ds), len(sets)),
            (where, gain, router, *[others[d] for d in ds], *parts),
            [SMEM] + [VMEM] * (2 + len(ds) + len(parts)),
            [((rows, d_model), BF16), ((rows, LANES), F32)],
            12,
            after=after,
        )

    gate_hbm, up_hbm, down_hbm = (
        pltpu.with_memory_space_constraint(w, pltpu.HBM)
        for w in (gate_weight, up_weight, down_weight)
    )

    def run_up(normed, after=()):
        rows = normed.shape[0]
        (act,) = call(
            functools.partial(up_kernel, 4),
            (normed, from_core(normed), gate_hbm, up_hbm),
            [VMEM, VMEM, ANY, ANY],
            [((2 * rows, hidden_units), BF16)],
            26,
            [
                pltpu.VMEM((2 * rows, d_model), BF16),
                pltpu.VMEM((2, 2 * rows, hidden_units), F32),
                pltpu.VMEM((4, d_model // 4, hidden_units), BF16),
                pltpu.SemaphoreType.DMA((4,)),
            ],
            after=after,
        )
        return act

    order = list(range(n_exp))[::-1]
    halves = [order[: n_exp // 2], order[n_exp // 2 :]]

    def run_down(act, ks, after=()):
        return call(
            functools.partial(down_kernel, ks),
            (where, act, down_hbm),
            [SMEM, VMEM, ANY],
            [((act.shape[0] // 2, len(ks) * width), BF16)] * 2,
            12,
            [
                pltpu.VMEM((len(ks), hidden_units, width), BF16),
                pltpu.SemaphoreType.DMA((len(ks),)),
            ],
            after=after,
        )

    def give_back(ks, near_out, far_out, mix, after=()):
        scaled = call(
            functools.partial(scale_kernel, len(ks)),
            (near_out, from_core(far_out), mix),
            [VMEM] * 3,
            [((near_out.shape[0], width), BF16)] * len(ks),
            10,
            after=after,
        )
        return scaled, {k: from_peer(p, k) for k, p in zip(ks, scaled)}

    def lay_out(ds, returned, after=()):
        return call(
            functools.partial(spread_kernel, n_exp, len(ds)),
            (*[takes[d] for d in ds], *[returned[k] for k in range(n_exp)]),
            [VMEM] * (len(ds) + n_exp),
            [((tok, width), F32 if d == 0 else BF16) for d in ds],
            10,
            after=after,
        )

    spread = [None] * n_chip
    normed_a, mix_a = take_in(groups[0], picked_all)
    act_a = run_up(normed_a)
    first_a = run_down(act_a, halves[0])
    normed_b, mix_b = take_in(groups[1], first_a[:1])
    second_a = run_down(act_a, halves[1], (normed_b,))
    scaled, returned_a = give_back(halves[0], *first_a, mix_a)
    more, rest = give_back(halves[1], *second_a, mix_a, scaled[:1])
    returned_a |= rest
    act_b = run_up(normed_b, more[:1])
    first_b = run_down(act_b, halves[0])
    waits = [returned_a[k] for k in range(1, n_exp)]
    second_b = run_down(act_b, halves[1], (first_b[0], *waits))
    scaled, returned_b = give_back(halves[0], *first_b, mix_b)
    more, rest = give_back(halves[1], *second_b, mix_b, scaled[:1])
    returned_b |= rest
    for d, m in zip(groups[0], lay_out(groups[0], returned_a, more[:1])):
        spread[d] = m
    for d, m in zip(groups[1], lay_out(groups[1], returned_b)):
        spread[d] = m
    total = hidden[:tok].astype(F32) + spread[0]
    for d in range(1, n_chip):
        total += from_chip(spread[d], n_chip - d).astype(F32)
    return total.astype(BF16)


def solution(mesh):
    return jax.shard_map(
        body,
        mesh=mesh,
        in_specs=(
            P("ctx", "exp"),
            P("ctx", "exp"),
            P("ctx", "exp"),
            P("ctx", "exp"),
            P(),
            P(),
            P(),
            P(("ctx", "exp"), None),
            P("exp", None, "ctx"),
            P("exp", None, "ctx"),
            P("exp", "ctx", None),
        ),
        out_specs=P("ctx", "exp"),
        check_vma=False,
    )
```

time: 298 us -> 164 us (0.55)
  waiting for transfers between devices: 167 us -> 66.6 us
  blocking collectives: 53.9 us -> 0 us
  Pallas kernels: 0 us -> 53.6 us
  matrix products: 37.6 us -> 0 us
  starting transfers between devices: 7.25 us -> 41.5 us
  between operations: 14.4 us -> 0.22 us
  local copies, waits for them, and re-layouts: 7.79 us -> 0.03 us
  other arithmetic: 8.44 us -> 1.61 us
    reduce_scatter x1 -> x0, waiting for transfers between devices: 76.5 us -> none  [body(): lax.psum_scatter(jnp.dot(activation, down_local, preferred_element_type=j...]
    all_gather x1 -> x0, waiting for transfers between devices: 70.8 us -> none  [body(): row_piece = lax.all_gather(flat_rows, 'ctx', axis=0, tiled=True)]
    ppermute x0 -> x34, waiting for transfers between devices: none -> 66.6 us  [the longest x18 36.6 us: from_peer(): lax.ppermute(x, 'exp', [(i ^ k, i) for i in range(n_exp)])]
    pallas_call x0 -> x20, Pallas kernels: none -> 53.6 us  [call(): pl.pallas_call(ordered, in_specs=list(specs) + [ANY] * len(after), out_sp...]
    ppermute x0 -> x34, starting transfers between devices: none -> 41.5 us  [the longest x18 18.1 us: from_peer(): lax.ppermute(x, 'exp', [(i ^ k, i) for i in range(n_exp)])]
    dot_general x8 -> x0, matrix products: 37.6 us -> none  [the longest x1 12.6 us: body(): up_val = jnp.dot(row_piece, up_local, preferred_element_type=jnp.float32)]
    all_gather x2 -> x0, blocking collectives: 29.9 us -> none  [the longest x1 15.5 us: body(): key_piece = lax.all_gather(rotated_keys, 'ctx', axis=0, tiled=True)]
    all_to_all x2 -> x0, blocking collectives: 24 us -> none  [the longest x1 16 us: body(): lax.all_to_all(buffer, 'exp', split_axis=0, concat_axis=0, tiled=True)]
  transfers between devices with their start and end apart: 4 -> 34, of which waited for: 4 -> 20; matrix products, arithmetic and copies ran while one was open for 0% -> 0% of each run, Pallas kernels for 0% -> 28%
where the time goes in v1:
time: 164 us
  waiting for transfers between devices  66.6 us (41%)
  Pallas kernels  53.6 us (33%)
  starting transfers between devices  41.5 us (25%)
    pallas_call x20, Pallas kernels, call(): pl.pallas_call(ordered, in_specs=list(specs) + [ANY] * len(after), out_sp...  53.6 us
    ppermute x18, waiting for transfers between devices, from_peer(): lax.ppermute(x, 'exp', [(i ^ k, i) for i in range(n_exp)])  36.6 us
    ppermute x9, waiting for transfers between devices, from_chip(): return lax.ppermute(x, 'ctx', pairs) if d else x  24.9 us
    ppermute x18, starting transfers between devices, from_peer(): lax.ppermute(x, 'exp', [(i ^ k, i) for i in range(n_exp)])  18.1 us
    ppermute x9, starting transfers between devices, from_chip(): return lax.ppermute(x, 'ctx', pairs) if d else x  12.1 us
    ppermute x7, starting transfers between devices, from_core(): return lax.ppermute(x, 'ctx', [(i ^ 1, i) for i in range(n_ctx)])  11.3 us
    ppermute x7, waiting for transfers between devices, from_core(): return lax.ppermute(x, 'ctx', [(i ^ 1, i) for i in range(n_ctx)])  5.03 us
  transfers between devices with their start and end apart: 34, of which 20 were waited for; matrix products, arithmetic and copies ran while one was open for 0% of the time, Pallas kernels for 28%

profile of v1, /device:TPU:9, one launch (start us, length us, event | category | flops | bytes accessed | tf_op | source)
XLA Modules:
  0.0 163.6 jit_solution(17516543112055467367)
XLA Ops:
  0.7 1.7 %shard_map.109 = (bf16[96,512]{1,0:T(8,128)(2,1)S(1)}, bf16[16,128]{1,0:T(8,128)(2,1)S(1)}, bf16[96,1536]{1,0:T(8,128)(2,1)S(1)}, bf16[96,1536]{1,0:T(8,128)(2,1)S(1)}) custom-call(s32[10]{0:T(128)S(1)} %pad_add_fusion.refs_0_, s32[2,24]{1,0:T(2,128)} %bitcast.6, bf16[96,256]{1,0:T(8,128)(2,1)} %refs_2_.7, bf16[96,256]{1,0:T(8,128)(2,1)} %refs_3_.3, ...), custom_call_target="tpu_custom_call" | custom-call | tf_op jit(solution)/shard_map/pallas_call | solution.py:27
  2.5 2.5 %collective-permute-start.1 = (bf16[96,512]{1,0:T(8,128)(2,1)S(1)}, bf16[96,512]{1,0:T(8,128)(2,1)S(1)}, u32[]{:S(2)}, u32[]{:S(2)}) collective-permute-start(bf16[96,512]{1,0:T(8,128)(2,1)S(1)} %get-tuple-element.57.refs_0_), channel_id=1, source_target_pairs={{16,0},{20,4},{24,8},{28,12},{0,16},{4,20},{8,24},{12,28},{17,1},{... | collective-permute-start | bytes 294920 | tf_op jit(solution)/shard_map/ppermute | solution.py:277
  5.0 2.2 %collective-permute-start.2 = (bf16[96,512]{1,0:T(8,128)(2,1)S(1)}, bf16[96,512]{1,0:T(8,128)(2,1)S(1)}, u32[]{:S(2)}, u32[]{:S(2)}) collective-permute-start(bf16[96,512]{1,0:T(8,128)(2,1)S(1)} %get-tuple-element.57.refs_0_), channel_id=1, source_target_pairs={{24,0},{28,4},{0,8},{4,12},{8,16},{12,20},{16,24},{20,28},{25,1},{... | collective-permute-start | bytes 294920 | tf_op jit(solution)/shard_map/ppermute | solution.py:277
  7.2 1.2 collective-permute-start.3
  8.4 1.2 collective-permute-start.4
  9.9 2.2 %collective-permute-start.5 = (bf16[16,128]{1,0:T(8,128)(2,1)S(1)}, bf16[16,128]{1,0:T(8,128)(2,1)S(1)}, u32[]{:S(2)}, u32[]{:S(2)}) collective-permute-start(bf16[16,128]{1,0:T(8,128)(2,1)S(1)} %get-tuple-element.58.refs_4_), channel_id=1, source_target_pairs={{3,0},{2,1},{1,2},{0,3},{7,4},{6,5},{5,6},{4,7},{11,8},{10,9},{9,1... | collective-permute-start | bytes 12296 | tf_op jit(solution)/shard_map/ppermute | solution.py:283
  12.1 1.2 collective-permute-done.5.refs_7_
  13.4 3.6 %collective-permute-start.6 = (bf16[384,512]{1,0:T(8,128)(2,1)S(1)}, bf16[384,512]{1,0:T(8,128)(2,1)S(1)}, u32[]{:S(2)}, u32[]{:S(2)}) collective-permute-start(bf16[384,512]{1,0:T(8,128)(2,1)S(1)} %get-tuple-element.59.refs_3_), channel_id=1, source_target_pairs={{4,0},{0,4},{12,8},{8,12},{20,16},{16,20},{28,24},{24,28},{5,1},{1... | collective-permute-start | bytes 1179656 | tf_op jit(solution)/shard_map/ppermute | solution.py:280
  16.9 1.3 collective-permute-done.6.refs_4_
  18.3 2.5 %shard_map.111.refs_1_ = bf16[112,1536]{1,0:T(8,128)(2,1)S(1)} custom-call(s32[10]{0:T(128)S(1)} %pad_add_fusion.refs_0_, bf16[96,1536]{1,0:T(8,128)(2,1)S(1)} %get-tuple-element.55.refs_1_, bf16[96,1536]{1,0:T(8,128)(2,1)S(1)} %get-tuple-element.56.refs_2_, bf16[384,512]{1,0:T(8,128)(2,1)S(1)} %get-tuple-element.59.refs_3_, ...), custom_call_target="tpu_custom_call" | custom-call | tf_op jit(solution)/shard_map/pallas_call | solution.py:27
  20.9 1.5 collective-permute-start.11
  22.3 1.1 shard_map.112
  23.4 2.2 %collective-permute-start.10 = (bf16[72,1536]{1,0:T(8,128)(2,1)S(1)}, bf16[72,1536]{1,0:T(8,128)(2,1)S(1)}, u32[]{:S(2)}, u32[]{:S(2)}) collective-permute-start(bf16[72,1536]{1,0:T(8,128)(2,1)S(1)} %get-tuple-element.64), channel_id=1, source_target_pairs={{3,0},{2,1},{1,2},{0,3},{7,4},{6,5},{5,6},{4,7},{11,8},{10,9},{9,1... | collective-permute-start | bytes 663560 | tf_op jit(solution)/shard_map/ppermute | solution.py:283
  26.1 4.6 %collective-permute-done.7.refs_1_ = bf16[112,1536]{1,0:T(8,128)(2,1)S(1)} collective-permute-done((bf16[112,1536]{1,0:T(8,128)(2,1)S(1)}, bf16[112,1536]{1,0:T(8,128)(2,1)S(1)}, u32[]{:S(2)}, u32[]{:S(2)}) %collective-permute-start.7) | collective-permute-done | bytes 344096 | tf_op jit(solution)/shard_map/ppermute | solution.py:277
  30.7 4.5 %collective-permute-done.8.refs_2_.refs_6_ = bf16[72,1536]{1,0:T(8,128)(2,1)S(1)} collective-permute-done((bf16[72,1536]{1,0:T(8,128)(2,1)S(1)}, bf16[72,1536]{1,0:T(8,128)(2,1)S(1)}, u32[]{:S(2)}, u32[]{:S(2)}) %collective-permute-start.8) | collective-permute-done | bytes 221216 | tf_op jit(solution)/shard_map/ppermute | solution.py:283
  35.2 1.2 collective-permute-done.9.refs_3_.refs_7_
  36.4 1.5 collective-permute-done.11.refs_5_.refs_1_
  37.9 1.1 shard_map.113
  39.0 1.3 collective-permute-start.12
  40.2 1.2 collective-permute-start.13
  41.7 1.3 shard_map.114
  43.0 1.1 collective-permute-done.12.refs_10_
  44.1 1.9 %collective-permute-done.13.refs_11_ = bf16[72,1536]{1,0:T(8,128)(2,1)S(1)} collective-permute-done((bf16[72,1536]{1,0:T(8,128)(2,1)S(1)}, bf16[72,1536]{1,0:T(8,128)(2,1)S(1)}, u32[]{:S(2)}, u32[]{:S(2)}) %collective-permute-start.13) | collective-permute-done | bytes 221216 | tf_op jit(solution)/shard_map/ppermute | solution.py:283
  46.0 3.5 %collective-permute-done.14.refs_12_ = bf16[72,1536]{1,0:T(8,128)(2,1)S(1)} collective-permute-done((bf16[72,1536]{1,0:T(8,128)(2,1)S(1)}, bf16[72,1536]{1,0:T(8,128)(2,1)S(1)}, u32[]{:S(2)}, u32[]{:S(2)}) %collective-permute-start.14) | collective-permute-done | bytes 221216 | tf_op jit(solution)/shard_map/ppermute | solution.py:283
  49.5 1.8 %shard_map.115 = (bf16[144,6144]{1,0:T(8,128)(2,1)S(1)}, f32[144,128]{1,0:T(8,128)S(1)}) custom-call(s32[10]{0:T(128)S(1)} %pad_add_fusion.refs_0_, bf16[1,6144]{1,0:T(2,128)(2,1)S(1)} %reshape.3.refs_1_, bf16[4,6144]{1,0:T(4,128)(2,1)S(1)} %bitcast.4, f32[72,128]{1,0:T(8,128)S(1)} %get-tuple-element.66.refs_3_, f32[72,128]{1,0:T(8,128)S(1)} %get-tuple-element.67.refs_4_, ...), custom_call_target="tpu_custom_call" | custom-call | tf_op jit(solution)/shard_map/pallas_call | solution.py:27
  51.3 3.5 %collective-permute-start.16 = (bf16[144,6144]{1,0:T(8,128)(2,1)S(1)}, bf16[144,6144]{1,0:T(8,128)(2,1)S(1)}, u32[]{:S(2)}, u32[]{:S(2)}) collective-permute-start(bf16[144,6144]{1,0:T(8,128)(2,1)S(1)} %get-tuple-element.74.refs_0_), channel_id=1, source_target_pairs={{4,0},{0,4},{12,8},{8,12},{20,16},{16,20},{28,24},{24,28},{5,1},{1... | collective-permute-start | bytes 5308424 | tf_op jit(solution)/shard_map/ppermute | solution.py:280
  56.2 1.2 collective-permute-start.19
  58.1 9.9 %shard_map.116.refs_1_ = bf16[288,1024]{1,0:T(8,128)(2,1)S(1)} custom-call(bf16[144,6144]{1,0:T(8,128)(2,1)S(1)} %get-tuple-element.74.refs_0_, bf16[144,6144]{1,0:T(8,128)(2,1)S(1)} %collective-permute-done.16.refs_1_, bf16[1,6144,1024]{2,1,0:T(8,128)(2,1)} %refs_2_.11, bf16[1,6144,1024]{2,1,0:T(8,128)(2,1)} %refs_3_.5), custom_call_target="tpu_custom_call" | custom-call | tf_op jit(solution)/shard_map/pallas_call | solution.py:27
  68.0 4.6 %shard_map.117 = (bf16[144,3072]{1,0:T(8,128)(2,1)S(1)}, bf16[144,3072]{1,0:T(8,128)(2,1)S(1)}) custom-call(s32[10]{0:T(128)S(1)} %pad_add_fusion.refs_0_, bf16[288,1024]{1,0:T(8,128)(2,1)S(1)} %shard_map.116.refs_1_, bf16[1,1024,6144]{2,1,0:T(8,128)(2,1)} %refs_2_.13), custom_call_target="tpu_custom_call" | custom-call | tf_op jit(solution)/shard_map/pallas_call | solution.py:27
  72.7 4.2 %collective-permute-done.19.refs_8_ = bf16[144,1536]{1,0:T(8,128)(2,1)S(1)} collective-permute-done((bf16[144,1536]{1,0:T(8,128)(2,1)S(1)}, bf16[144,1536]{1,0:T(8,128)(2,1)S(1)}, u32[]{:S(2)}, u32[]{:S(2)}) %collective-permute-start.19) | collective-permute-done | bytes 442400 | tf_op jit(solution)/shard_map/ppermute | solution.py:283
  76.9 1.8 %shard_map.118 = (bf16[144,6144]{1,0:T(8,128)(2,1)S(1)}, f32[144,128]{1,0:T(8,128)S(1)}) custom-call(s32[10]{0:T(128)S(1)} %pad_add_fusion.refs_0_, bf16[1,6144]{1,0:T(2,128)(2,1)S(1)} %reshape.3.refs_1_, bf16[4,6144]{1,0:T(4,128)(2,1)S(1)} %bitcast.5, f32[72,128]{1,0:T(8,128)S(1)} %get-tuple-element.73.refs_13_.refs_3_, ...), custom_call_target="tpu_custom_call" | custom-call | tf_op jit(solution)/shard_map/pallas_call | solution.py:27
  79.7 4.8 %shard_map.119 = (bf16[144,3072]{1,0:T(8,128)(2,1)S(1)}, bf16[144,3072]{1,0:T(8,128)(2,1)S(1)}) custom-call(s32[10]{0:T(128)S(1)} %pad_add_fusion.refs_0_, bf16[288,1024]{1,0:T(8,128)(2,1)S(1)} %shard_map.116.refs_1_, bf16[1,1024,6144]{2,1,0:T(8,128)(2,1)} %refs_2_.13, bf16[144,6144]{1,0:T(8,128)(2,1)S(1)} %get-tuple-element.81.refs_3_.refs_0_), custom_call_target="tpu_custom_call" | custom-call | tf_op jit(solution)/shard_map/pallas_call | solution.py:27
  85.6 1.5 collective-permute-done.20.refs_1_
  88.3 1.2 collective-permute-start.23
  90.3 9.9 %shard_map.122.refs_1_ = bf16[288,1024]{1,0:T(8,128)(2,1)S(1)} custom-call(bf16[144,6144]{1,0:T(8,128)(2,1)S(1)} %get-tuple-element.81.refs_3_.refs_0_, bf16[144,6144]{1,0:T(8,128)(2,1)S(1)} %collective-permute-done.25.refs_1_, bf16[1,6144,1024]{2,1,0:T(8,128)(2,1)} %refs_2_.11, bf16[1,6144,1024]{2,1,0:T(8,128)(2,1)} %refs_3_.5, ...), custom_call_target="tpu_custom_call" | custom-call | tf_op jit(solution)/shard_map/pallas_call | solution.py:27
  100.3 4.6 %shard_map.123 = (bf16[144,3072]{1,0:T(8,128)(2,1)S(1)}, bf16[144,3072]{1,0:T(8,128)(2,1)S(1)}) custom-call(s32[10]{0:T(128)S(1)} %pad_add_fusion.refs_0_, bf16[288,1024]{1,0:T(8,128)(2,1)S(1)} %shard_map.122.refs_1_, bf16[1,1024,6144]{2,1,0:T(8,128)(2,1)} %refs_2_.13), custom_call_target="tpu_custom_call" | custom-call | tf_op jit(solution)/shard_map/pallas_call | solution.py:27
  104.9 1.3 collective-permute-start.27
  106.2 2.7 %collective-permute-done.24.refs_6_.refs_5_ = bf16[144,1536]{1,0:T(8,128)(2,1)S(1)} collective-permute-done((bf16[144,1536]{1,0:T(8,128)(2,1)S(1)}, bf16[144,1536]{1,0:T(8,128)(2,1)S(1)}, u32[]{:S(2)}, u32[]{:S(2)}) %collective-permute-start.24) | collective-permute-done | bytes 442400 | tf_op jit(solution)/shard_map/ppermute | solution.py:283
  108.9 4.6 %shard_map.124 = (bf16[144,3072]{1,0:T(8,128)(2,1)S(1)}, bf16[144,3072]{1,0:T(8,128)(2,1)S(1)}) custom-call(s32[10]{0:T(128)S(1)} %pad_add_fusion.refs_0_, bf16[288,1024]{1,0:T(8,128)(2,1)S(1)} %shard_map.122.refs_1_, bf16[1,1024,6144]{2,1,0:T(8,128)(2,1)} %refs_2_.13, bf16[144,3072]{1,0:T(8,128)(2,1)S(1)} %get-tuple-element.90.refs_3_.refs_0_, ...), custom_call_target="tpu_custom_call" | custom-call | tf_op jit(solution)/shard_map/pallas_call | solution.py:27
  113.5 1.5 collective-permute-start.26
  115.6 1.5 collective-permute-done.26.refs_1_
  119.1 1.2 collective-permute-start.31
  121.1 2.3 %collective-permute-start.28 = (bf16[96,1536]{1,0:T(8,128)(2,1)S(1)}, bf16[96,1536]{1,0:T(8,128)(2,1)S(1)}, u32[]{:S(2)}, u32[]{:S(2)}) collective-permute-start(bf16[96,1536]{1,0:T(8,128)(2,1)S(1)} %get-tuple-element.98), channel_id=1, source_target_pairs={{24,0},{28,4},{0,8},{4,12},{8,16},{12,20},{16,24},{20,28},{25,1},{... | collective-permute-start | bytes 884744 | tf_op jit(solution)/shard_map/ppermute | solution.py:277
  123.4 5.6 %collective-permute-done.29.refs_3_ = bf16[144,1536]{1,0:T(8,128)(2,1)S(1)} collective-permute-done((bf16[144,1536]{1,0:T(8,128)(2,1)S(1)}, bf16[144,1536]{1,0:T(8,128)(2,1)S(1)}, u32[]{:S(2)}, u32[]{:S(2)}) %collective-permute-start.29) | collective-permute-done | bytes 442400 | tf_op jit(solution)/shard_map/ppermute | solution.py:283
  129.6 9.8 %collective-permute-done.31.refs_5_ = bf16[144,1536]{1,0:T(8,128)(2,1)S(1)} collective-permute-done((bf16[144,1536]{1,0:T(8,128)(2,1)S(1)}, bf16[144,1536]{1,0:T(8,128)(2,1)S(1)}, u32[]{:S(2)}, u32[]{:S(2)}) %collective-permute-start.31) | collective-permute-done | bytes 442400 | tf_op jit(solution)/shard_map/ppermute | solution.py:283
  141.3 2.5 %collective-permute-start.33 = (bf16[96,1536]{1,0:T(8,128)(2,1)S(1)}, bf16[96,1536]{1,0:T(8,128)(2,1)S(1)}, u32[]{:S(2)}, u32[]{:S(2)}) collective-permute-start(bf16[96,1536]{1,0:T(8,128)(2,1)S(1)} %get-tuple-element.104), channel_id=1, source_target_pairs={{8,0},{12,4},{16,8},{20,12},{24,16},{28,20},{0,24},{4,28},{9,1},{1... | collective-permute-start | bytes 884744 | tf_op jit(solution)/shard_map/ppermute | solution.py:277
  143.8 15.3 %collective-permute-done.32 = bf16[96,1536]{1,0:T(8,128)(2,1)S(1)} collective-permute-done((bf16[96,1536]{1,0:T(8,128)(2,1)S(1)}, bf16[96,1536]{1,0:T(8,128)(2,1)S(1)}, u32[]{:S(2)}, u32[]{:S(2)}) %collective-permute-start.32) | collective-permute-done | bytes 294944 | tf_op jit(solution)/shard_map/ppermute | solution.py:277
  159.0 3.6 %collective-permute-done.33 = bf16[96,1536]{1,0:T(8,128)(2,1)S(1)} collective-permute-done((bf16[96,1536]{1,0:T(8,128)(2,1)S(1)}, bf16[96,1536]{1,0:T(8,128)(2,1)S(1)}, u32[]{:S(2)}, u32[]{:S(2)}) %collective-permute-start.33) | collective-permute-done | bytes 294944 | tf_op jit(solution)/shard_map/ppermute | solution.py:277
  (47 shorter events, 14.9 us)
Async XLA Ops:
  2.4 10.8 %collective-permute-start = (bf16[96,512]{1,0:T(8,128)(2,1)S(1)}, bf16[96,512]{1,0:T(8,128)(2,1)S(1)}, u32[]{:S(2)}, u32[]{:S(2)}) collective-permute-start(bf16[96,512]{1,0:T(8,128)(2,1)S(1)} %get-tuple-element.57.refs_0_), channel_id=1, source_target_pairs={{8,0},{12,4},{16,8},{20,12},{24,16},{28,20},{0,24},{4,28},{9,1},{1... | collective-permute-start | bytes 294920 | tf_op jit(solution)/shard_map/ppermute | solution.py:277
  2.5 10.8 %collective-permute-start.1 = (bf16[96,512]{1,0:T(8,128)(2,1)S(1)}, bf16[96,512]{1,0:T(8,128)(2,1)S(1)}, u32[]{:S(2)}, u32[]{:S(2)}) collective-permute-start(bf16[96,512]{1,0:T(8,128)(2,1)S(1)} %get-tuple-element.57.refs_0_), channel_id=1, source_target_pairs={{16,0},{20,4},{24,8},{28,12},{0,16},{4,20},{8,24},{12,28},{17,1},{... | collective-permute-start | bytes 294920 | tf_op jit(solution)/shard_map/ppermute | solution.py:277
  5.0 8.3 %collective-permute-start.2 = (bf16[96,512]{1,0:T(8,128)(2,1)S(1)}, bf16[96,512]{1,0:T(8,128)(2,1)S(1)}, u32[]{:S(2)}, u32[]{:S(2)}) collective-permute-start(bf16[96,512]{1,0:T(8,128)(2,1)S(1)} %get-tuple-element.57.refs_0_), channel_id=1, source_target_pairs={{24,0},{28,4},{0,8},{4,12},{8,16},{12,20},{16,24},{20,28},{25,1},{... | collective-permute-start | bytes 294920 | tf_op jit(solution)/shard_map/ppermute | solution.py:277
  7.2 2.8 %collective-permute-start.3 = (bf16[16,128]{1,0:T(8,128)(2,1)S(1)}, bf16[16,128]{1,0:T(8,128)(2,1)S(1)}, u32[]{:S(2)}, u32[]{:S(2)}) collective-permute-start(bf16[16,128]{1,0:T(8,128)(2,1)S(1)} %get-tuple-element.58.refs_4_), channel_id=1, source_target_pairs={{1,0},{0,1},{3,2},{2,3},{5,4},{4,5},{7,6},{6,7},{9,8},{8,9},{11,10... | collective-permute-start | bytes 12296 | tf_op jit(solution)/shard_map/ppermute | solution.py:283
  8.4 3.7 %collective-permute-start.4 = (bf16[16,128]{1,0:T(8,128)(2,1)S(1)}, bf16[16,128]{1,0:T(8,128)(2,1)S(1)}, u32[]{:S(2)}, u32[]{:S(2)}) collective-permute-start(bf16[16,128]{1,0:T(8,128)(2,1)S(1)} %get-tuple-element.58.refs_4_), channel_id=1, source_target_pairs={{2,0},{3,1},{0,2},{1,3},{6,4},{7,5},{4,6},{5,7},{10,8},{11,9},{8,1... | collective-permute-start | bytes 12296 | tf_op jit(solution)/shard_map/ppermute | solution.py:283
  9.9 3.4 %collective-permute-start.5 = (bf16[16,128]{1,0:T(8,128)(2,1)S(1)}, bf16[16,128]{1,0:T(8,128)(2,1)S(1)}, u32[]{:S(2)}, u32[]{:S(2)}) collective-permute-start(bf16[16,128]{1,0:T(8,128)(2,1)S(1)} %get-tuple-element.58.refs_4_), channel_id=1, source_target_pairs={{3,0},{2,1},{1,2},{0,3},{7,4},{6,5},{5,6},{4,7},{11,8},{10,9},{9,1... | collective-permute-start | bytes 12296 | tf_op jit(solution)/shard_map/ppermute | solution.py:283
  13.3 28.3 %copy-start.1 = (bf16[6144]{0:T(1024)(128)(2,1)S(1)}, bf16[6144]{0:T(1024)(128)(2,1)}, u32[]{:S(2)}) copy-start(bf16[6144]{0:T(1024)(128)(2,1)} %param.16) | copy-start | bytes 36868
  13.4 4.9 %collective-permute-start.6 = (bf16[384,512]{1,0:T(8,128)(2,1)S(1)}, bf16[384,512]{1,0:T(8,128)(2,1)S(1)}, u32[]{:S(2)}, u32[]{:S(2)}) collective-permute-start(bf16[384,512]{1,0:T(8,128)(2,1)S(1)} %get-tuple-element.59.refs_3_), channel_id=1, source_target_pairs={{4,0},{0,4},{12,8},{8,12},{20,16},{16,20},{28,24},{24,28},{5,1},{1... | collective-permute-start | bytes 1179656 | tf_op jit(solution)/shard_map/ppermute | solution.py:280
  18.3 31.2 %copy-start = (bf16[6144,4]{0,1:T(4,128)(2,1)S(1)}, bf16[6144,4]{0,1:T(4,128)(2,1)}, u32[]{:S(2)}) copy-start(bf16[6144,4]{0,1:T(4,128)(2,1)} %param.17) | copy-start | bytes 147460
  20.8 9.9 %collective-permute-start.7 = (bf16[112,1536]{1,0:T(8,128)(2,1)S(1)}, bf16[112,1536]{1,0:T(8,128)(2,1)S(1)}, u32[]{:S(2)}, u32[]{:S(2)}) collective-permute-start(bf16[112,1536]{1,0:T(8,128)(2,1)S(1)} %shard_map.111.refs_1_), channel_id=1, source_target_pairs={{8,0},{12,4},{16,8},{20,12},{24,16},{28,20},{0,24},{4,28},{9,1},{1... | collective-permute-start | bytes 1032200 | tf_op jit(solution)/shard_map/ppermute | solution.py:277
  20.9 17.0 %collective-permute-start.11 = (bf16[112,1536]{1,0:T(8,128)(2,1)S(1)}, bf16[112,1536]{1,0:T(8,128)(2,1)S(1)}, u32[]{:S(2)}, u32[]{:S(2)}) collective-permute-start(bf16[112,1536]{1,0:T(8,128)(2,1)S(1)} %shard_map.111.refs_1_), channel_id=1, source_target_pairs={{24,0},{28,4},{0,8},{4,12},{8,16},{12,20},{16,24},{20,28},{25,1},{... | collective-permute-start | bytes 1032200 | tf_op jit(solution)/shard_map/ppermute | solution.py:277
  23.4 7.3 %collective-permute-start.10 = (bf16[72,1536]{1,0:T(8,128)(2,1)S(1)}, bf16[72,1536]{1,0:T(8,128)(2,1)S(1)}, u32[]{:S(2)}, u32[]{:S(2)}) collective-permute-start(bf16[72,1536]{1,0:T(8,128)(2,1)S(1)} %get-tuple-element.64), channel_id=1, source_target_pairs={{3,0},{2,1},{1,2},{0,3},{7,4},{6,5},{5,6},{4,7},{11,8},{10,9},{9,1... | collective-permute-start | bytes 663560 | tf_op jit(solution)/shard_map/ppermute | solution.py:283
  25.6 9.6 %collective-permute-start.8 = (bf16[72,1536]{1,0:T(8,128)(2,1)S(1)}, bf16[72,1536]{1,0:T(8,128)(2,1)S(1)}, u32[]{:S(2)}, u32[]{:S(2)}) collective-permute-start(bf16[72,1536]{1,0:T(8,128)(2,1)S(1)} %get-tuple-element.62), channel_id=1, source_target_pairs={{1,0},{0,1},{3,2},{2,3},{5,4},{4,5},{7,6},{6,7},{9,8},{8,9},{11,10... | collective-permute-start | bytes 663560 | tf_op jit(solution)/shard_map/ppermute | solution.py:283
  25.9 10.5 %collective-permute-start.9 = (bf16[72,1536]{1,0:T(8,128)(2,1)S(1)}, bf16[72,1536]{1,0:T(8,128)(2,1)S(1)}, u32[]{:S(2)}, u32[]{:S(2)}) collective-permute-start(bf16[72,1536]{1,0:T(8,128)(2,1)S(1)} %get-tuple-element.63), channel_id=1, source_target_pairs={{2,0},{3,1},{0,2},{1,3},{6,4},{7,5},{4,6},{5,7},{10,8},{11,9},{8,1... | collective-permute-start | bytes 663560 | tf_op jit(solution)/shard_map/ppermute | solution.py:283
  30.7 11.0 %collective-permute-start.15 = (bf16[112,1536]{1,0:T(8,128)(2,1)S(1)}, bf16[112,1536]{1,0:T(8,128)(2,1)S(1)}, u32[]{:S(2)}, u32[]{:S(2)}) collective-permute-start(bf16[112,1536]{1,0:T(8,128)(2,1)S(1)} %collective-permute-done.7.refs_1_), channel_id=1, source_target_pairs={{8,0},{12,4},{16,8},{20,12},{24,16},{28,20},{0,24},{4,28},{9,1},{1... | collective-permute-start | bytes 1032200 | tf_op jit(solution)/shard_map/ppermute | solution.py:277
  39.0 5.1 %collective-permute-start.12 = (bf16[72,1536]{1,0:T(8,128)(2,1)S(1)}, bf16[72,1536]{1,0:T(8,128)(2,1)S(1)}, u32[]{:S(2)}, u32[]{:S(2)}) collective-permute-start(bf16[72,1536]{1,0:T(8,128)(2,1)S(1)} %get-tuple-element.70), channel_id=1, source_target_pairs={{1,0},{0,1},{3,2},{2,3},{5,4},{4,5},{7,6},{6,7},{9,8},{8,9},{11,10... | collective-permute-start | bytes 663560 | tf_op jit(solution)/shard_map/ppermute | solution.py:283
  40.2 5.7 %collective-permute-start.13 = (bf16[72,1536]{1,0:T(8,128)(2,1)S(1)}, bf16[72,1536]{1,0:T(8,128)(2,1)S(1)}, u32[]{:S(2)}, u32[]{:S(2)}) collective-permute-start(bf16[72,1536]{1,0:T(8,128)(2,1)S(1)} %get-tuple-element.71), channel_id=1, source_target_pairs={{2,0},{3,1},{0,2},{1,3},{6,4},{7,5},{4,6},{5,7},{10,8},{11,9},{8,1... | collective-permute-start | bytes 663560 | tf_op jit(solution)/shard_map/ppermute | solution.py:283
  41.5 8.0 %collective-permute-start.14 = (bf16[72,1536]{1,0:T(8,128)(2,1)S(1)}, bf16[72,1536]{1,0:T(8,128)(2,1)S(1)}, u32[]{:S(2)}, u32[]{:S(2)}) collective-permute-start(bf16[72,1536]{1,0:T(8,128)(2,1)S(1)} %get-tuple-element.72), channel_id=1, source_target_pairs={{3,0},{2,1},{1,2},{0,3},{7,4},{6,5},{5,6},{4,7},{11,8},{10,9},{9,1... | collective-permute-start | bytes 663560 | tf_op jit(solution)/shard_map/ppermute | solution.py:283
  51.3 6.8 %collective-permute-start.16 = (bf16[144,6144]{1,0:T(8,128)(2,1)S(1)}, bf16[144,6144]{1,0:T(8,128)(2,1)S(1)}, u32[]{:S(2)}, u32[]{:S(2)}) collective-permute-start(bf16[144,6144]{1,0:T(8,128)(2,1)S(1)} %get-tuple-element.74.refs_0_), channel_id=1, source_target_pairs={{4,0},{0,4},{12,8},{8,12},{20,16},{16,20},{28,24},{24,28},{5,1},{1... | collective-permute-start | bytes 5308424 | tf_op jit(solution)/shard_map/ppermute | solution.py:280
  54.8 17.9 %collective-permute-start.17 = (bf16[144,1536]{1,0:T(8,128)(2,1)S(1)}, bf16[144,1536]{1,0:T(8,128)(2,1)S(1)}, u32[]{:S(2)}, u32[]{:S(2)}) collective-permute-start(bf16[144,1536]{1,0:T(8,128)(2,1)S(1)} %get-tuple-element.77), channel_id=1, source_target_pairs={{1,0},{0,1},{3,2},{2,3},{5,4},{4,5},{7,6},{6,7},{9,8},{8,9},{11,10... | collective-permute-start | bytes 1327112 | tf_op jit(solution)/shard_map/ppermute | solution.py:283
  55.7 17.0 %collective-permute-start.18 = (bf16[144,1536]{1,0:T(8,128)(2,1)S(1)}, bf16[144,1536]{1,0:T(8,128)(2,1)S(1)}, u32[]{:S(2)}, u32[]{:S(2)}) collective-permute-start(bf16[144,1536]{1,0:T(8,128)(2,1)S(1)} %get-tuple-element.78), channel_id=1, source_target_pairs={{2,0},{3,1},{0,2},{1,3},{6,4},{7,5},{4,6},{5,7},{10,8},{11,9},{8,1... | collective-permute-start | bytes 1327112 | tf_op jit(solution)/shard_map/ppermute | solution.py:283
  56.2 20.7 %collective-permute-start.19 = (bf16[144,1536]{1,0:T(8,128)(2,1)S(1)}, bf16[144,1536]{1,0:T(8,128)(2,1)S(1)}, u32[]{:S(2)}, u32[]{:S(2)}) collective-permute-start(bf16[144,1536]{1,0:T(8,128)(2,1)S(1)} %get-tuple-element.79), channel_id=1, source_target_pairs={{3,0},{2,1},{1,2},{0,3},{7,4},{6,5},{5,6},{4,7},{11,8},{10,9},{9,1... | collective-permute-start | bytes 1327112 | tf_op jit(solution)/shard_map/ppermute | solution.py:283
  78.7 11.6 %collective-permute-start.25 = (bf16[144,6144]{1,0:T(8,128)(2,1)S(1)}, bf16[144,6144]{1,0:T(8,128)(2,1)S(1)}, u32[]{:S(2)}, u32[]{:S(2)}) collective-permute-start(bf16[144,6144]{1,0:T(8,128)(2,1)S(1)} %get-tuple-element.81.refs_3_.refs_0_), channel_id=1, source_target_pairs={{4,0},{0,4},{12,8},{8,12},{20,16},{16,20},{28,24},{24,28},{5,1},{1... | collective-permute-start | bytes 5308424 | tf_op jit(solution)/shard_map/ppermute | solution.py:280
  79.6 5.4 %collective-permute-start.21 = (bf16[144,3072]{1,0:T(8,128)(2,1)S(1)}, bf16[144,3072]{1,0:T(8,128)(2,1)S(1)}, u32[]{:S(2)}, u32[]{:S(2)}) collective-permute-start(bf16[144,3072]{1,0:T(8,128)(2,1)S(1)} %get-tuple-element.85), channel_id=1, source_target_pairs={{4,0},{0,4},{12,8},{8,12},{20,16},{16,20},{28,24},{24,28},{5,1},{1... | collective-permute-start | bytes 2654216 | tf_op jit(solution)/shard_map/ppermute | solution.py:280
  84.5 2.5 %collective-permute-start.20 = (bf16[144,3072]{1,0:T(8,128)(2,1)S(1)}, bf16[144,3072]{1,0:T(8,128)(2,1)S(1)}, u32[]{:S(2)}, u32[]{:S(2)}) collective-permute-start(bf16[144,3072]{1,0:T(8,128)(2,1)S(1)} %get-tuple-element.83), channel_id=1, source_target_pairs={{4,0},{0,4},{12,8},{8,12},{20,16},{16,20},{28,24},{24,28},{5,1},{1... | collective-permute-start | bytes 2654216 | tf_op jit(solution)/shard_map/ppermute | solution.py:280
  87.6 18.6 %collective-permute-start.22 = (bf16[144,1536]{1,0:T(8,128)(2,1)S(1)}, bf16[144,1536]{1,0:T(8,128)(2,1)S(1)}, u32[]{:S(2)}, u32[]{:S(2)}) collective-permute-start(bf16[144,1536]{1,0:T(8,128)(2,1)S(1)} %get-tuple-element.88.refs_4_), channel_id=1, source_target_pairs={{1,0},{0,1},{3,2},{2,3},{5,4},{4,5},{7,6},{6,7},{9,8},{8,9},{11,10... | collective-permute-start | bytes 1327112 | tf_op jit(solution)/shard_map/ppermute | solution.py:283
  88.3 17.9 %collective-permute-start.23 = (bf16[144,1536]{1,0:T(8,128)(2,1)S(1)}, bf16[144,1536]{1,0:T(8,128)(2,1)S(1)}, u32[]{:S(2)}, u32[]{:S(2)}) collective-permute-start(bf16[144,1536]{1,0:T(8,128)(2,1)S(1)} %get-tuple-element.89), channel_id=1, source_target_pairs={{2,0},{3,1},{0,2},{1,3},{6,4},{7,5},{4,6},{5,7},{10,8},{11,9},{8,1... | collective-permute-start | bytes 1327112 | tf_op jit(solution)/shard_map/ppermute | solution.py:283
  89.4 19.4 %collective-permute-start.24 = (bf16[144,1536]{1,0:T(8,128)(2,1)S(1)}, bf16[144,1536]{1,0:T(8,128)(2,1)S(1)}, u32[]{:S(2)}, u32[]{:S(2)}) collective-permute-start(bf16[144,1536]{1,0:T(8,128)(2,1)S(1)} %get-tuple-element.86.refs_3_), channel_id=1, source_target_pairs={{3,0},{2,1},{1,2},{0,3},{7,4},{6,5},{5,6},{4,7},{11,8},{10,9},{9,1... | collective-permute-start | bytes 1327112 | tf_op jit(solution)/shard_map/ppermute | solution.py:283
  104.9 10.1 %collective-permute-start.27 = (bf16[144,3072]{1,0:T(8,128)(2,1)S(1)}, bf16[144,3072]{1,0:T(8,128)(2,1)S(1)}, u32[]{:S(2)}, u32[]{:S(2)}) collective-permute-start(bf16[144,3072]{1,0:T(8,128)(2,1)S(1)} %get-tuple-element.94), channel_id=1, source_target_pairs={{4,0},{0,4},{12,8},{8,12},{20,16},{16,20},{28,24},{24,28},{5,1},{1... | collective-permute-start | bytes 2654216 | tf_op jit(solution)/shard_map/ppermute | solution.py:280
  113.5 3.6 %collective-permute-start.26 = (bf16[144,3072]{1,0:T(8,128)(2,1)S(1)}, bf16[144,3072]{1,0:T(8,128)(2,1)S(1)}, u32[]{:S(2)}, u32[]{:S(2)}) collective-permute-start(bf16[144,3072]{1,0:T(8,128)(2,1)S(1)} %get-tuple-element.92), channel_id=1, source_target_pairs={{4,0},{0,4},{12,8},{8,12},{20,16},{16,20},{28,24},{24,28},{5,1},{1... | collective-permute-start | bytes 2654216 | tf_op jit(solution)/shard_map/ppermute | solution.py:280
  117.6 11.4 %collective-permute-start.29 = (bf16[144,1536]{1,0:T(8,128)(2,1)S(1)}, bf16[144,1536]{1,0:T(8,128)(2,1)S(1)}, u32[]{:S(2)}, u32[]{:S(2)}) collective-permute-start(bf16[144,1536]{1,0:T(8,128)(2,1)S(1)} %get-tuple-element.96.refs_6_), channel_id=1, source_target_pairs={{1,0},{0,1},{3,2},{2,3},{5,4},{4,5},{7,6},{6,7},{9,8},{8,9},{11,10... | collective-permute-start | bytes 1327112 | tf_op jit(solution)/shard_map/ppermute | solution.py:283
  118.6 11.1 %collective-permute-start.30 = (bf16[144,1536]{1,0:T(8,128)(2,1)S(1)}, bf16[144,1536]{1,0:T(8,128)(2,1)S(1)}, u32[]{:S(2)}, u32[]{:S(2)}) collective-permute-start(bf16[144,1536]{1,0:T(8,128)(2,1)S(1)} %get-tuple-element.102), channel_id=1, source_target_pairs={{2,0},{3,1},{0,2},{1,3},{6,4},{7,5},{4,6},{5,7},{10,8},{11,9},{8,1... | collective-permute-start | bytes 1327112 | tf_op jit(solution)/shard_map/ppermute | solution.py:283
  119.1 20.3 %collective-permute-start.31 = (bf16[144,1536]{1,0:T(8,128)(2,1)S(1)}, bf16[144,1536]{1,0:T(8,128)(2,1)S(1)}, u32[]{:S(2)}, u32[]{:S(2)}) collective-permute-start(bf16[144,1536]{1,0:T(8,128)(2,1)S(1)} %get-tuple-element.95.refs_3_), channel_id=1, source_target_pairs={{3,0},{2,1},{1,2},{0,3},{7,4},{6,5},{5,6},{4,7},{11,8},{10,9},{9,1... | collective-permute-start | bytes 1327112 | tf_op jit(solution)/shard_map/ppermute | solution.py:283
  121.1 22.7 %collective-permute-start.28 = (bf16[96,1536]{1,0:T(8,128)(2,1)S(1)}, bf16[96,1536]{1,0:T(8,128)(2,1)S(1)}, u32[]{:S(2)}, u32[]{:S(2)}) collective-permute-start(bf16[96,1536]{1,0:T(8,128)(2,1)S(1)} %get-tuple-element.98), channel_id=1, source_target_pairs={{24,0},{28,4},{0,8},{4,12},{8,16},{12,20},{16,24},{20,28},{25,1},{... | collective-permute-start | bytes 884744 | tf_op jit(solution)/shard_map/ppermute | solution.py:277
  140.3 18.8 %collective-permute-start.32 = (bf16[96,1536]{1,0:T(8,128)(2,1)S(1)}, bf16[96,1536]{1,0:T(8,128)(2,1)S(1)}, u32[]{:S(2)}, u32[]{:S(2)}) collective-permute-start(bf16[96,1536]{1,0:T(8,128)(2,1)S(1)} %get-tuple-element.103), channel_id=1, source_target_pairs={{16,0},{20,4},{24,8},{28,12},{0,16},{4,20},{8,24},{12,28},{17,1},{... | collective-permute-start | bytes 884744 | tf_op jit(solution)/shard_map/ppermute | solution.py:277
  141.3 21.4 %collective-permute-start.33 = (bf16[96,1536]{1,0:T(8,128)(2,1)S(1)}, bf16[96,1536]{1,0:T(8,128)(2,1)S(1)}, u32[]{:S(2)}, u32[]{:S(2)}) collective-permute-start(bf16[96,1536]{1,0:T(8,128)(2,1)S(1)} %get-tuple-element.104), channel_id=1, source_target_pairs={{8,0},{12,4},{16,8},{20,12},{24,16},{28,20},{0,24},{4,28},{9,1},{1... | collective-permute-start | bytes 884744 | tf_op jit(solution)/shard_map/ppermute | solution.py:277

commit v2 on v1

--- a/solution.py
+++ b/solution.py
@@ -18,7 +18,7 @@
 SMEM = pl.BlockSpec(memory_space=pltpu.SMEM)
 
 
-def call(kernel, inputs, specs, shapes, limit, scratch=(), flops=0, moved=0, after=()):
+def call(kernel, inputs, specs, shapes, limit, scratch=(), after=(), kept=()):
     n = len(inputs)
 
     def ordered(*refs):
@@ -27,11 +27,10 @@
     return pl.pallas_call(
         ordered,
         in_specs=list(specs) + [ANY] * len(after),
-        out_specs=[VMEM] * len(shapes),
-        out_shape=[jax.ShapeDtypeStruct(s, d) for s, d in shapes],
+        out_specs=[VMEM] * (len(shapes) + len(kept)),
+        out_shape=[jax.ShapeDtypeStruct(s, d) for s, d in shapes] + list(kept),
         scratch_shapes=list(scratch),
         compiler_params=pltpu.CompilerParams(vmem_limit_bytes=limit * MIB),
-        cost_estimate=pl.CostEstimate(flops=flops, bytes_accessed=moved, transcendentals=0),
     )(*inputs, *after)
 
 
@@ -55,7 +54,10 @@
     token = lax.broadcasted_iota(jnp.int32, (sub, LANES), 0) + where_ref[1] * sub
     lane = lax.broadcasted_iota(jnp.int32, (sub, LANES), 1)
     place = (token == lane).astype(F32)
-    row_ref[...] = jnp.dot(two.astype(F32), place, preferred_element_type=F32).astype(BF16)
+    row_ref[...] = jnp.zeros(row_ref.shape, BF16)
+    row_ref[:TILE, :LANES] = jnp.dot(
+        two.astype(F32), place, preferred_element_type=F32
+    ).astype(BF16)
     for copy in copies[1:]:
         copy.wait()
 
@@ -65,9 +67,9 @@
     tok = spans[0].shape[0]
     for d in range(n):
         out_ref[d * tok : (d + 1) * tok, :] = spans[d][...]
-    total = rows[0][...].astype(F32)
+    total = rows[0][:TILE, :LANES].astype(F32)
     for other in rows[1:]:
-        total += other[...].astype(F32)
+        total += other[:TILE, :LANES].astype(F32)
     row_ref[...] = total.astype(BF16)
 
 
@@ -178,23 +180,28 @@
     mix_ref[...] = jnp.broadcast_to(mix, (rows, LANES))
 
 
-def up_kernel(n, near_ref, far_ref, g_ref, u_ref, act_ref, x_ref, acc, buf, sems):
+def up_kernel(n, fetch, near_ref, far_ref, g_ref, u_ref, act_ref, *refs):
+    kept, (x_ref, acc, sems) = refs[:-3], refs[-3:]
+    held = kept if fetch else (g_ref, u_ref)
     rows = near_ref.shape[0]
-    depth = g_ref.shape[1] // n
-    slots = buf.shape[0]
-
-    def copy(j):
-        part = (g_ref, u_ref)[j // n].at[0, (j % n) * depth : (j % n + 1) * depth, :]
-        return pltpu.make_async_copy(part, buf.at[j % slots], sems.at[j % slots])
-
-    for j in range(slots):
-        copy(j).start()
+    depth = held[0].shape[0] // n
+    at = [slice(j * depth, (j + 1) * depth) for j in range(n)]
+    copies = []
+    if fetch:
+        copies = [
+            pltpu.make_async_copy(w.at[0, part], v.at[part], sems.at[i * n + j])
+            for i, (w, v) in enumerate(((g_ref, kept[0]), (u_ref, kept[1])))
+            for j, part in enumerate(at)
+        ]
+    for copy in copies:
+        copy.start()
     x_ref[:rows, :] = near_ref[...]
     x_ref[rows:, :] = far_ref[...]
     for j in range(2 * n):
-        copy(j).wait()
-        at = slice((j % n) * depth, (j % n + 1) * depth)
-        y = jnp.dot(x_ref[:, at], buf[j % slots], preferred_element_type=F32)
+        if fetch:
+            copies[j].wait()
+        part = at[j % n]
+        y = jnp.dot(x_ref[:, part], held[j // n][part, :], preferred_element_type=F32)
         if j % n == 0:
             acc[j // n] = y
         elif j < 2 * n - 1:
@@ -202,23 +209,25 @@
         else:
             g = acc[0]
             act_ref[...] = (g * (acc[1] + y) / (1.0 + jnp.exp(-g))).astype(BF16)
-        if j + slots < 2 * n:
-            copy(j + slots).start()
-
-
-def down_kernel(ks, where_ref, act_ref, d_ref, near_out, far_out, buf, sems):
+
+
+def down_kernel(ks, fetch, where_ref, act_ref, d_ref, near_out, far_out, *refs):
+    kept, sems = refs[:-1], refs[-1]
+    held = kept[0] if fetch else d_ref
     exp = where_ref[1]
     rows = near_out.shape[0]
-    width = buf.shape[2]
+    width = held.shape[2]
     copies = []
-    for j, k in enumerate(ks):
-        at = pl.ds(pl.multiple_of((exp ^ k) * width, width), width)
-        copies.append(pltpu.make_async_copy(d_ref.at[0, :, at], buf.at[j], sems.at[j]))
+    if fetch:
+        for j, k in enumerate(ks):
+            at = pl.ds(pl.multiple_of((exp ^ k) * width, width), width)
+            copies.append(pltpu.make_async_copy(d_ref.at[0, :, at], held.at[j], sems.at[j]))
     for copy in copies:
         copy.start()
     for j in range(len(ks)):
-        copies[j].wait()
-        y = jnp.dot(act_ref[...], buf[j], preferred_element_type=F32).astype(BF16)
+        if fetch:
+            copies[j].wait()
+        y = jnp.dot(act_ref[...], held[j], preferred_element_type=F32).astype(BF16)
         near_out[:, j * width : (j + 1) * width] = y[:rows]
         far_out[:, j * width : (j + 1) * width] = y[rows:]
 
@@ -292,7 +301,7 @@
             ],
         ),
         [SMEM] + [ANY] * 5,
-        [((tok, 2 * kv), BF16), ((TILE, LANES), BF16)] + [((tok, width), BF16)] * 2,
+        [((tok, 2 * kv), BF16)] * 2 + [((tok, width), BF16)] * 2,
         4,
         [pltpu.VMEM((2, sub), jnp.int32), pltpu.SemaphoreType.DMA((5,))],
     )
@@ -364,7 +373,7 @@
             (where, gain, router, *[others[d] for d in ds], *parts),
             [SMEM] + [VMEM] * (2 + len(ds) + len(parts)),
             [((rows, d_model), BF16), ((rows, LANES), F32)],
-            12,
+            8,
             after=after,
         )
 
@@ -373,40 +382,49 @@
         for w in (gate_weight, up_weight, down_weight)
     )
 
+    n_part = 4
+    weights = {}
+
     def run_up(normed, after=()):
         rows = normed.shape[0]
-        (act,) = call(
-            functools.partial(up_kernel, 4),
-            (normed, from_core(normed), gate_hbm, up_hbm),
-            [VMEM, VMEM, ANY, ANY],
+        fetch = "up" not in weights
+        spec = ANY if fetch else VMEM
+        act, *kept = call(
+            functools.partial(up_kernel, n_part, fetch),
+            (normed, from_core(normed), *(weights["up"] if not fetch else (gate_hbm, up_hbm))),
+            [VMEM, VMEM, spec, spec],
             [((2 * rows, hidden_units), BF16)],
-            26,
+            10,
             [
                 pltpu.VMEM((2 * rows, d_model), BF16),
                 pltpu.VMEM((2, 2 * rows, hidden_units), F32),
-                pltpu.VMEM((4, d_model // 4, hidden_units), BF16),
-                pltpu.SemaphoreType.DMA((4,)),
+                pltpu.SemaphoreType.DMA((2 * n_part,)),
             ],
             after=after,
-        )
+            kept=[pltpu.VMEM((d_model, hidden_units), BF16)] * (2 * fetch),
+        )
+        if fetch:
+            weights["up"] = kept
         return act
 
     order = list(range(n_exp))[::-1]
     halves = [order[: n_exp // 2], order[n_exp // 2 :]]
 
     def run_down(act, ks, after=()):
-        return call(
-            functools.partial(down_kernel, ks),
-            (where, act, down_hbm),
-            [SMEM, VMEM, ANY],
+        fetch = ks[0] not in weights
+        near_out, far_out, *kept = call(
+            functools.partial(down_kernel, ks, fetch),
+            (where, act, down_hbm if fetch else weights[ks[0]]),
+            [SMEM, VMEM, ANY if fetch else VMEM],
             [((act.shape[0] // 2, len(ks) * width), BF16)] * 2,
-            12,
-            [
-                pltpu.VMEM((len(ks), hidden_units, width), BF16),
-                pltpu.SemaphoreType.DMA((len(ks),)),
-            ],
-            after=after,
-        )
+            6,
+            [pltpu.SemaphoreType.DMA((len(ks),))],
+            after=after,
+            kept=[pltpu.VMEM((len(ks), hidden_units, width), BF16)] * fetch,
+        )
+        if fetch:
+            weights[ks[0]] = kept[0]
+        return near_out, far_out
 
     def give_back(ks, near_out, far_out, mix, after=()):
         scaled = call(
@@ -440,7 +458,7 @@
     returned_a |= rest
     act_b = run_up(normed_b, more[:1])
     first_b = run_down(act_b, halves[0])
-    waits = [returned_a[k] for k in range(1, n_exp)]
+    waits = [returned_a[n_exp - 1]]
     second_b = run_down(act_b, halves[1], (first_b[0], *waits))
     scaled, returned_b = give_back(halves[0], *first_b, mix_b)
     more, rest = give_back(halves[1], *second_b, mix_b, scaled[:1])

time: 164 us -> 158 us (0.963)
  starting transfers between devices: 41.5 us -> 33.1 us
  waiting for transfers between devices: 66.6 us -> 73.1 us
  Pallas kernels: 53.6 us -> 47.5 us
    pallas_call x20, Pallas kernels: 53.6 us -> 47.5 us  [call(): pl.pallas_call(ordered, in_specs=list(specs) + [ANY] * len(after), out_sp...]
    ppermute x18, waiting for transfers between devices: 36.6 us -> 42.1 us  [from_peer(): lax.ppermute(x, 'exp', [(i ^ k, i) for i in range(n_exp)])]
    ppermute x9, starting transfers between devices: 12.1 us -> 7.66 us  [from_chip(): return lax.ppermute(x, 'ctx', pairs) if d else x]
    ppermute x9, waiting for transfers between devices: 24.9 us -> 29 us  [from_chip(): return lax.ppermute(x, 'ctx', pairs) if d else x]
    ppermute x7, waiting for transfers between devices: 5.03 us -> 2.02 us  [from_core(): return lax.ppermute(x, 'ctx', [(i ^ 1, i) for i in range(n_ctx)])]
    ppermute x7, starting transfers between devices: 11.3 us -> 8.73 us  [from_core(): return lax.ppermute(x, 'ctx', [(i ^ 1, i) for i in range(n_ctx)])]
  transfers between devices with their start and end apart: 34 -> 34, of which waited for: 20 -> 19; matrix products, arithmetic and copies ran while one was open for 0% -> 0% of each run, Pallas kernels for 28% -> 25%
where the time goes in v2:
time: 158 us; the launch traced here: 157 us
  waiting for transfers between devices  73.1 us (46%)
  Pallas kernels  47.5 us (30%)
  starting transfers between devices  33.1 us (21%)
  other arithmetic  1.61 us (1%)
    pallas_call x20, Pallas kernels, call(): pl.pallas_call(ordered, in_specs=list(specs) + [ANY] * len(after), out_sp...  47.5 us
    ppermute x18, waiting for transfers between devices, from_peer(): lax.ppermute(x, 'exp', [(i ^ k, i) for i in range(n_exp)])  42.1 us
    ppermute x9, waiting for transfers between devices, from_chip(): return lax.ppermute(x, 'ctx', pairs) if d else x  29 us
    ppermute x18, starting transfers between devices, from_peer(): lax.ppermute(x, 'exp', [(i ^ k, i) for i in range(n_exp)])  16.7 us
    ppermute x7, starting transfers between devices, from_core(): return lax.ppermute(x, 'ctx', [(i ^ 1, i) for i in range(n_ctx)])  8.73 us
    ppermute x9, starting transfers between devices, from_chip(): return lax.ppermute(x, 'ctx', pairs) if d else x  7.66 us
  transfers between devices with their start and end apart: 34, of which 19 were waited for; matrix products, arithmetic and copies ran while one was open for 0% of the time, Pallas kernels for 25%

profile of v2, /device:TPU:9, one launch (start us, length us, event | category | flops | bytes accessed | tf_op | source)
XLA Modules:
  0.0 157.1 jit_solution(9469434552110898491)
XLA Ops:
  0.7 1.7 %shard_map.109 = (bf16[96,512]{1,0:T(8,128)(2,1)S(1)}, bf16[96,512]{1,0:T(8,128)(2,1)S(1)}, bf16[96,1536]{1,0:T(8,128)(2,1)S(1)}, bf16[96,1536]{1,0:T(8,128)(2,1)S(1)}) custom-call(s32[10]{0:T(128)S(1)} %pad_add_fusion.refs_0_, s32[2,24]{1,0:T(2,128)} %bitcast.6, bf16[96,256]{1,0:T(8,128)(2,1)} %refs_2_.4, bf16[96,256]{1,0:T(8,128)(2,1)} %refs_3_.2, ...), custom_call_target="tpu_custom_call" | custom-call | tf_op jit(solution)/shard_map/pallas_call | solution.py:27
  2.5 2.5 %collective-permute-start.1 = (bf16[96,512]{1,0:T(8,128)(2,1)S(1)}, bf16[96,512]{1,0:T(8,128)(2,1)S(1)}, u32[]{:S(2)}, u32[]{:S(2)}) collective-permute-start(bf16[96,512]{1,0:T(8,128)(2,1)S(1)} %get-tuple-element.62.refs_0_), channel_id=1, source_target_pairs={{16,0},{20,4},{24,8},{28,12},{0,16},{4,20},{8,24},{12,28},{17,1},{... | collective-permute-start | bytes 294920 | tf_op jit(solution)/shard_map/ppermute | solution.py:286
  5.0 2.2 %collective-permute-start.2 = (bf16[96,512]{1,0:T(8,128)(2,1)S(1)}, bf16[96,512]{1,0:T(8,128)(2,1)S(1)}, u32[]{:S(2)}, u32[]{:S(2)}) collective-permute-start(bf16[96,512]{1,0:T(8,128)(2,1)S(1)} %get-tuple-element.62.refs_0_), channel_id=1, source_target_pairs={{24,0},{28,4},{0,8},{4,12},{8,16},{12,20},{16,24},{20,28},{25,1},{... | collective-permute-start | bytes 294920 | tf_op jit(solution)/shard_map/ppermute | solution.py:286
  7.2 1.2 collective-permute-start.3
  8.4 1.2 collective-permute-start.4
  9.8 3.2 %collective-permute-done.2.refs_3_ = bf16[96,512]{1,0:T(8,128)(2,1)S(1)} collective-permute-done((bf16[96,512]{1,0:T(8,128)(2,1)S(1)}, bf16[96,512]{1,0:T(8,128)(2,1)S(1)}, u32[]{:S(2)}, u32[]{:S(2)}) %collective-permute-start.2) | collective-permute-done | bytes 98336 | tf_op jit(solution)/shard_map/ppermute | solution.py:286
  13.0 1.7 %collective-permute-done.5.refs_7_ = bf16[96,512]{1,0:T(8,128)(2,1)S(1)} collective-permute-done((bf16[96,512]{1,0:T(8,128)(2,1)S(1)}, bf16[96,512]{1,0:T(8,128)(2,1)S(1)}, u32[]{:S(2)}, u32[]{:S(2)}) %collective-permute-start.5) | collective-permute-done | bytes 98336 | tf_op jit(solution)/shard_map/ppermute | solution.py:292
  14.8 2.6 %collective-permute-start.6 = (bf16[384,512]{1,0:T(8,128)(2,1)S(1)}, bf16[384,512]{1,0:T(8,128)(2,1)S(1)}, u32[]{:S(2)}, u32[]{:S(2)}) collective-permute-start(bf16[384,512]{1,0:T(8,128)(2,1)S(1)} %get-tuple-element.64.refs_3_), channel_id=1, source_target_pairs={{4,0},{0,4},{12,8},{8,12},{20,16},{16,20},{28,24},{24,28},{5,1},{1... | collective-permute-start | bytes 1179656 | tf_op jit(solution)/shard_map/ppermute | solution.py:289
  17.3 1.3 collective-permute-done.6.refs_4_
  18.7 2.5 %shard_map.111.refs_1_ = bf16[112,1536]{1,0:T(8,128)(2,1)S(1)} custom-call(s32[10]{0:T(128)S(1)} %pad_add_fusion.refs_0_, bf16[96,1536]{1,0:T(8,128)(2,1)S(1)} %get-tuple-element.60.refs_1_, bf16[96,1536]{1,0:T(8,128)(2,1)S(1)} %get-tuple-element.61.refs_2_, bf16[384,512]{1,0:T(8,128)(2,1)S(1)} %get-tuple-element.64.refs_3_, ...), custom_call_target="tpu_custom_call" | custom-call | tf_op jit(solution)/shard_map/pallas_call | solution.py:27
  21.2 1.5 collective-permute-start.11
  22.7 1.1 shard_map.112
  24.0 1.3 collective-permute-start.8
  25.3 1.1 collective-permute-start.9
  26.5 4.0 %collective-permute-done.7.refs_1_ = bf16[112,1536]{1,0:T(8,128)(2,1)S(1)} collective-permute-done((bf16[112,1536]{1,0:T(8,128)(2,1)S(1)}, bf16[112,1536]{1,0:T(8,128)(2,1)S(1)}, u32[]{:S(2)}, u32[]{:S(2)}) %collective-permute-start.7) | collective-permute-done | bytes 344096 | tf_op jit(solution)/shard_map/ppermute | solution.py:286
  30.8 3.8 %collective-permute-done.8.refs_2_.refs_6_ = bf16[72,1536]{1,0:T(8,128)(2,1)S(1)} collective-permute-done((bf16[72,1536]{1,0:T(8,128)(2,1)S(1)}, bf16[72,1536]{1,0:T(8,128)(2,1)S(1)}, u32[]{:S(2)}, u32[]{:S(2)}) %collective-permute-start.8) | collective-permute-done | bytes 221216 | tf_op jit(solution)/shard_map/ppermute | solution.py:292
  34.7 2.2 %collective-permute-done.9.refs_3_.refs_7_ = bf16[72,1536]{1,0:T(8,128)(2,1)S(1)} collective-permute-done((bf16[72,1536]{1,0:T(8,128)(2,1)S(1)}, bf16[72,1536]{1,0:T(8,128)(2,1)S(1)}, u32[]{:S(2)}, u32[]{:S(2)}) %collective-permute-start.9) | collective-permute-done | bytes 221216 | tf_op jit(solution)/shard_map/ppermute | solution.py:292
  36.8 2.1 %collective-permute-done.11.refs_5_.refs_1_ = bf16[112,1536]{1,0:T(8,128)(2,1)S(1)} collective-permute-done((bf16[112,1536]{1,0:T(8,128)(2,1)S(1)}, bf16[112,1536]{1,0:T(8,128)(2,1)S(1)}, u32[]{:S(2)}, u32[]{:S(2)}) %collective-permute-start.11) | collective-permute-done | bytes 344096 | tf_op jit(solution)/shard_map/ppermute | solution.py:286
  38.9 1.1 shard_map.113
  40.0 1.3 collective-permute-start.12
  41.3 1.2 collective-permute-start.13
  43.4 1.3 shard_map.114
  45.1 1.9 %collective-permute-done.13.refs_11_ = bf16[72,1536]{1,0:T(8,128)(2,1)S(1)} collective-permute-done((bf16[72,1536]{1,0:T(8,128)(2,1)S(1)}, bf16[72,1536]{1,0:T(8,128)(2,1)S(1)}, u32[]{:S(2)}, u32[]{:S(2)}) %collective-permute-start.13) | collective-permute-done | bytes 221216 | tf_op jit(solution)/shard_map/ppermute | solution.py:292
  47.0 3.5 %collective-permute-done.14.refs_12_ = bf16[72,1536]{1,0:T(8,128)(2,1)S(1)} collective-permute-done((bf16[72,1536]{1,0:T(8,128)(2,1)S(1)}, bf16[72,1536]{1,0:T(8,128)(2,1)S(1)}, u32[]{:S(2)}, u32[]{:S(2)}) %collective-permute-start.14) | collective-permute-done | bytes 221216 | tf_op jit(solution)/shard_map/ppermute | solution.py:292
  51.3 1.8 %shard_map.115 = (bf16[144,6144]{1,0:T(8,128)(2,1)S(1)}, f32[144,128]{1,0:T(8,128)S(1)}) custom-call(s32[10]{0:T(128)S(1)} %pad_add_fusion.refs_0_, bf16[1,6144]{1,0:T(2,128)(2,1)S(1)} %reshape.3.refs_1_, bf16[4,6144]{1,0:T(4,128)(2,1)S(1)} %bitcast.4, f32[72,128]{1,0:T(8,128)S(1)} %get-tuple-element.71.refs_3_, f32[72,128]{1,0:T(8,128)S(1)} %get-tuple-element.72.refs_4_, ...), custom_call_target="tpu_custom_call" | custom-call | tf_op jit(solution)/shard_map/pallas_call | solution.py:27
  53.1 3.5 %collective-permute-start.16 = (bf16[144,6144]{1,0:T(8,128)(2,1)S(1)}, bf16[144,6144]{1,0:T(8,128)(2,1)S(1)}, u32[]{:S(2)}, u32[]{:S(2)}) collective-permute-start(bf16[144,6144]{1,0:T(8,128)(2,1)S(1)} %get-tuple-element.79.refs_0_), channel_id=1, source_target_pairs={{4,0},{0,4},{12,8},{8,12},{20,16},{16,20},{28,24},{24,28},{5,1},{1... | collective-permute-start | bytes 5308424 | tf_op jit(solution)/shard_map/ppermute | solution.py:289
  56.6 0.9 collective-permute-start.17
  58.1 1.2 collective-permute-start.19
  59.9 10.1 %shard_map.116 = (bf16[288,1024]{1,0:T(8,128)(2,1)S(1)}, bf16[6144,1024]{1,0:T(8,128)(2,1)S(1)}, bf16[6144,1024]{1,0:T(8,128)(2,1)S(1)}) custom-call(bf16[144,6144]{1,0:T(8,128)(2,1)S(1)} %get-tuple-element.79.refs_0_, bf16[144,6144]{1,0:T(8,128)(2,1)S(1)} %collective-permute-done.16.refs_1_, bf16[1,6144,1024]{2,1,0:T(8,128)(2,1)} %refs_2_.5, ...), custom_call_target="tpu_custom_call" | custom-call | tf_op jit(solution)/shard_map/pallas_call | solution.py:27
  70.0 4.6 %shard_map.117 = (bf16[144,3072]{1,0:T(8,128)(2,1)S(1)}, bf16[144,3072]{1,0:T(8,128)(2,1)S(1)}, bf16[2,1024,1536]{2,1,0:T(8,128)(2,1)S(1)}) custom-call(s32[10]{0:T(128)S(1)} %pad_add_fusion.refs_0_, bf16[288,1024]{1,0:T(8,128)(2,1)S(1)} %get-tuple-element.80.refs_1_, bf16[1,1024,6144]{2,1,0:T(8,128)(2,1)} %refs_2_.7), custom_call_target="tpu_custom_call" | custom-call | tf_op jit(solution)/shard_map/pallas_call | solution.py:27
  74.7 4.1 %collective-permute-done.19.refs_8_ = bf16[144,1536]{1,0:T(8,128)(2,1)S(1)} collective-permute-done((bf16[144,1536]{1,0:T(8,128)(2,1)S(1)}, bf16[144,1536]{1,0:T(8,128)(2,1)S(1)}, u32[]{:S(2)}, u32[]{:S(2)}) %collective-permute-start.19) | collective-permute-done | bytes 442400 | tf_op jit(solution)/shard_map/ppermute | solution.py:292
  78.7 1.8 %shard_map.118 = (bf16[144,6144]{1,0:T(8,128)(2,1)S(1)}, f32[144,128]{1,0:T(8,128)S(1)}) custom-call(s32[10]{0:T(128)S(1)} %pad_add_fusion.refs_0_, bf16[1,6144]{1,0:T(2,128)(2,1)S(1)} %reshape.3.refs_1_, bf16[4,6144]{1,0:T(4,128)(2,1)S(1)} %bitcast.5, f32[72,128]{1,0:T(8,128)S(1)} %get-tuple-element.78.refs_13_.refs_3_, ...), custom_call_target="tpu_custom_call" | custom-call | tf_op jit(solution)/shard_map/pallas_call | solution.py:27
  80.6 0.9 collective-permute-start.25
  81.6 4.9 %shard_map.119 = (bf16[144,3072]{1,0:T(8,128)(2,1)S(1)}, bf16[144,3072]{1,0:T(8,128)(2,1)S(1)}, bf16[2,1024,1536]{2,1,0:T(8,128)(2,1)S(1)}) custom-call(s32[10]{0:T(128)S(1)} %pad_add_fusion.refs_0_, bf16[288,1024]{1,0:T(8,128)(2,1)S(1)} %get-tuple-element.80.refs_1_, bf16[1,1024,6144]{2,1,0:T(8,128)(2,1)} %refs_2_.7, ...), custom_call_target="tpu_custom_call" | custom-call | tf_op jit(solution)/shard_map/pallas_call | solution.py:27
  87.5 1.5 collective-permute-start.24
  89.6 7.7 %shard_map.122.refs_1_ = bf16[288,1024]{1,0:T(8,128)(2,1)S(1)} custom-call(bf16[144,6144]{1,0:T(8,128)(2,1)S(1)} %get-tuple-element.87.refs_3_.refs_0_, bf16[144,6144]{1,0:T(8,128)(2,1)S(1)} %collective-permute-done.25.refs_1_, bf16[6144,1024]{1,0:T(8,128)(2,1)S(1)} %get-tuple-element.96.refs_2_, bf16[6144,1024]{1,0:T(8,128)(2,1)S(1)} %get-tuple-element.97.refs_3_, ...), custom_call_target="tpu_custom_call" | custom-call | tf_op jit(solution)/shard_map/pallas_call | solution.py:27
  97.3 2.6 %shard_map.123 = (bf16[144,3072]{1,0:T(8,128)(2,1)S(1)}, bf16[144,3072]{1,0:T(8,128)(2,1)S(1)}) custom-call(s32[10]{0:T(128)S(1)} %pad_add_fusion.refs_0_, bf16[288,1024]{1,0:T(8,128)(2,1)S(1)} %shard_map.122.refs_1_, bf16[2,1024,1536]{2,1,0:T(8,128)(2,1)S(1)} %get-tuple-element.99.refs_2_), custom_call_target="tpu_custom_call" | custom-call | tf_op jit(solution)/shard_map/pallas_call | solution.py:27
  100.3 2.6 %shard_map.124 = (bf16[144,3072]{1,0:T(8,128)(2,1)S(1)}, bf16[144,3072]{1,0:T(8,128)(2,1)S(1)}) custom-call(s32[10]{0:T(128)S(1)} %pad_add_fusion.refs_0_, bf16[288,1024]{1,0:T(8,128)(2,1)S(1)} %shard_map.122.refs_1_, bf16[2,1024,1536]{2,1,0:T(8,128)(2,1)S(1)} %get-tuple-element.98.refs_2_, bf16[144,3072]{1,0:T(8,128)(2,1)S(1)} %get-tuple-element.100.refs_3_.refs_0_, ...), custom_call_target="tpu_custom_call" | custom-call | tf_op jit(solution)/shard_map/pallas_call | solution.py:27
  104.2 1.2 collective-permute-start.23
  106.9 1.2 collective-permute-start.30
  108.1 1.2 collective-permute-start.31
  109.2 6.2 %collective-permute-done.22.refs_3_ = bf16[144,1536]{1,0:T(8,128)(2,1)S(1)} collective-permute-done((bf16[144,1536]{1,0:T(8,128)(2,1)S(1)}, bf16[144,1536]{1,0:T(8,128)(2,1)S(1)}, u32[]{:S(2)}, u32[]{:S(2)}) %collective-permute-start.22) | collective-permute-done | bytes 442400 | tf_op jit(solution)/shard_map/ppermute | solution.py:292
  116.5 8.4 %collective-permute-done.29.refs_3_ = bf16[144,1536]{1,0:T(8,128)(2,1)S(1)} collective-permute-done((bf16[144,1536]{1,0:T(8,128)(2,1)S(1)}, bf16[144,1536]{1,0:T(8,128)(2,1)S(1)}, u32[]{:S(2)}, u32[]{:S(2)}) %collective-permute-start.29) | collective-permute-done | bytes 442400 | tf_op jit(solution)/shard_map/ppermute | solution.py:292
  125.1 9.6 %collective-permute-done.31.refs_5_ = bf16[144,1536]{1,0:T(8,128)(2,1)S(1)} collective-permute-done((bf16[144,1536]{1,0:T(8,128)(2,1)S(1)}, bf16[144,1536]{1,0:T(8,128)(2,1)S(1)}, u32[]{:S(2)}, u32[]{:S(2)}) %collective-permute-start.31) | collective-permute-done | bytes 442400 | tf_op jit(solution)/shard_map/ppermute | solution.py:292
  135.5 1.0 collective-permute-start.32
  136.6 18.5 %collective-permute-done.32 = bf16[96,1536]{1,0:T(8,128)(2,1)S(1)} collective-permute-done((bf16[96,1536]{1,0:T(8,128)(2,1)S(1)}, bf16[96,1536]{1,0:T(8,128)(2,1)S(1)}, u32[]{:S(2)}, u32[]{:S(2)}) %collective-permute-start.32) | collective-permute-done | bytes 294944 | tf_op jit(solution)/shard_map/ppermute | solution.py:286
  155.0 1.2 collective-permute-done.33
  156.2 0.9 add_convert_fusion
  (47 shorter events, 11.9 us)
Async XLA Ops:
  2.4 7.2 %collective-permute-start = (bf16[96,512]{1,0:T(8,128)(2,1)S(1)}, bf16[96,512]{1,0:T(8,128)(2,1)S(1)}, u32[]{:S(2)}, u32[]{:S(2)}) collective-permute-start(bf16[96,512]{1,0:T(8,128)(2,1)S(1)} %get-tuple-element.62.refs_0_), channel_id=1, source_target_pairs={{8,0},{12,4},{16,8},{20,12},{24,16},{28,20},{0,24},{4,28},{9,1},{1... | collective-permute-start | bytes 294920 | tf_op jit(solution)/shard_map/ppermute | solution.py:286
  2.5 7.3 %collective-permute-start.1 = (bf16[96,512]{1,0:T(8,128)(2,1)S(1)}, bf16[96,512]{1,0:T(8,128)(2,1)S(1)}, u32[]{:S(2)}, u32[]{:S(2)}) collective-permute-start(bf16[96,512]{1,0:T(8,128)(2,1)S(1)} %get-tuple-element.62.refs_0_), channel_id=1, source_target_pairs={{16,0},{20,4},{24,8},{28,12},{0,16},{4,20},{8,24},{12,28},{17,1},{... | collective-permute-start | bytes 294920 | tf_op jit(solution)/shard_map/ppermute | solution.py:286
  5.0 8.1 %collective-permute-start.2 = (bf16[96,512]{1,0:T(8,128)(2,1)S(1)}, bf16[96,512]{1,0:T(8,128)(2,1)S(1)}, u32[]{:S(2)}, u32[]{:S(2)}) collective-permute-start(bf16[96,512]{1,0:T(8,128)(2,1)S(1)} %get-tuple-element.62.refs_0_), channel_id=1, source_target_pairs={{24,0},{28,4},{0,8},{4,12},{8,16},{12,20},{16,24},{20,28},{25,1},{... | collective-permute-start | bytes 294920 | tf_op jit(solution)/shard_map/ppermute | solution.py:286
  7.2 5.9 %collective-permute-start.3 = (bf16[96,512]{1,0:T(8,128)(2,1)S(1)}, bf16[96,512]{1,0:T(8,128)(2,1)S(1)}, u32[]{:S(2)}, u32[]{:S(2)}) collective-permute-start(bf16[96,512]{1,0:T(8,128)(2,1)S(1)} %get-tuple-element.63.refs_4_), channel_id=1, source_target_pairs={{1,0},{0,1},{3,2},{2,3},{5,4},{4,5},{7,6},{6,7},{9,8},{8,9},{11,10... | collective-permute-start | bytes 294920 | tf_op jit(solution)/shard_map/ppermute | solution.py:292
  8.4 4.7 %collective-permute-start.4 = (bf16[96,512]{1,0:T(8,128)(2,1)S(1)}, bf16[96,512]{1,0:T(8,128)(2,1)S(1)}, u32[]{:S(2)}, u32[]{:S(2)}) collective-permute-start(bf16[96,512]{1,0:T(8,128)(2,1)S(1)} %get-tuple-element.63.refs_4_), channel_id=1, source_target_pairs={{2,0},{3,1},{0,2},{1,3},{6,4},{7,5},{4,6},{5,7},{10,8},{11,9},{8,1... | collective-permute-start | bytes 294920 | tf_op jit(solution)/shard_map/ppermute | solution.py:292
  9.6 5.1 %collective-permute-start.5 = (bf16[96,512]{1,0:T(8,128)(2,1)S(1)}, bf16[96,512]{1,0:T(8,128)(2,1)S(1)}, u32[]{:S(2)}, u32[]{:S(2)}) collective-permute-start(bf16[96,512]{1,0:T(8,128)(2,1)S(1)} %get-tuple-element.63.refs_4_), channel_id=1, source_target_pairs={{3,0},{2,1},{1,2},{0,3},{7,4},{6,5},{5,6},{4,7},{11,8},{10,9},{9,1... | collective-permute-start | bytes 294920 | tf_op jit(solution)/shard_map/ppermute | solution.py:292
  14.8 3.9 %collective-permute-start.6 = (bf16[384,512]{1,0:T(8,128)(2,1)S(1)}, bf16[384,512]{1,0:T(8,128)(2,1)S(1)}, u32[]{:S(2)}, u32[]{:S(2)}) collective-permute-start(bf16[384,512]{1,0:T(8,128)(2,1)S(1)} %get-tuple-element.64.refs_3_), channel_id=1, source_target_pairs={{4,0},{0,4},{12,8},{8,12},{20,16},{16,20},{28,24},{24,28},{5,1},{1... | collective-permute-start | bytes 1179656 | tf_op jit(solution)/shard_map/ppermute | solution.py:289
  21.2 9.3 %collective-permute-start.7 = (bf16[112,1536]{1,0:T(8,128)(2,1)S(1)}, bf16[112,1536]{1,0:T(8,128)(2,1)S(1)}, u32[]{:S(2)}, u32[]{:S(2)}) collective-permute-start(bf16[112,1536]{1,0:T(8,128)(2,1)S(1)} %shard_map.111.refs_1_), channel_id=1, source_target_pairs={{8,0},{12,4},{16,8},{20,12},{24,16},{28,20},{0,24},{4,28},{9,1},{1... | collective-permute-start | bytes 1032200 | tf_op jit(solution)/shard_map/ppermute | solution.py:286
  21.2 17.7 %collective-permute-start.11 = (bf16[112,1536]{1,0:T(8,128)(2,1)S(1)}, bf16[112,1536]{1,0:T(8,128)(2,1)S(1)}, u32[]{:S(2)}, u32[]{:S(2)}) collective-permute-start(bf16[112,1536]{1,0:T(8,128)(2,1)S(1)} %shard_map.111.refs_1_), channel_id=1, source_target_pairs={{24,0},{28,4},{0,8},{4,12},{8,16},{12,20},{16,24},{20,28},{25,1},{... | collective-permute-start | bytes 1032200 | tf_op jit(solution)/shard_map/ppermute | solution.py:286
  23.8 7.1 %collective-permute-start.10 = (bf16[72,1536]{1,0:T(8,128)(2,1)S(1)}, bf16[72,1536]{1,0:T(8,128)(2,1)S(1)}, u32[]{:S(2)}, u32[]{:S(2)}) collective-permute-start(bf16[72,1536]{1,0:T(8,128)(2,1)S(1)} %get-tuple-element.69), channel_id=1, source_target_pairs={{3,0},{2,1},{1,2},{0,3},{7,4},{6,5},{5,6},{4,7},{11,8},{10,9},{9,1... | collective-permute-start | bytes 663560 | tf_op jit(solution)/shard_map/ppermute | solution.py:292
  24.0 10.6 %collective-permute-start.8 = (bf16[72,1536]{1,0:T(8,128)(2,1)S(1)}, bf16[72,1536]{1,0:T(8,128)(2,1)S(1)}, u32[]{:S(2)}, u32[]{:S(2)}) collective-permute-start(bf16[72,1536]{1,0:T(8,128)(2,1)S(1)} %get-tuple-element.67), channel_id=1, source_target_pairs={{1,0},{0,1},{3,2},{2,3},{5,4},{4,5},{7,6},{6,7},{9,8},{8,9},{11,10... | collective-permute-start | bytes 663560 | tf_op jit(solution)/shard_map/ppermute | solution.py:292
  25.3 11.5 %collective-permute-start.9 = (bf16[72,1536]{1,0:T(8,128)(2,1)S(1)}, bf16[72,1536]{1,0:T(8,128)(2,1)S(1)}, u32[]{:S(2)}, u32[]{:S(2)}) collective-permute-start(bf16[72,1536]{1,0:T(8,128)(2,1)S(1)} %get-tuple-element.68), channel_id=1, source_target_pairs={{2,0},{3,1},{0,2},{1,3},{6,4},{7,5},{4,6},{5,7},{10,8},{11,9},{8,1... | collective-permute-start | bytes 663560 | tf_op jit(solution)/shard_map/ppermute | solution.py:292
  30.5 12.9 %collective-permute-start.15 = (bf16[112,1536]{1,0:T(8,128)(2,1)S(1)}, bf16[112,1536]{1,0:T(8,128)(2,1)S(1)}, u32[]{:S(2)}, u32[]{:S(2)}) collective-permute-start(bf16[112,1536]{1,0:T(8,128)(2,1)S(1)} %collective-permute-done.7.refs_1_), channel_id=1, source_target_pairs={{8,0},{12,4},{16,8},{20,12},{24,16},{28,20},{0,24},{4,28},{9,1},{1... | collective-permute-start | bytes 1032200 | tf_op jit(solution)/shard_map/ppermute | solution.py:286
  40.0 5.1 %collective-permute-start.12 = (bf16[72,1536]{1,0:T(8,128)(2,1)S(1)}, bf16[72,1536]{1,0:T(8,128)(2,1)S(1)}, u32[]{:S(2)}, u32[]{:S(2)}) collective-permute-start(bf16[72,1536]{1,0:T(8,128)(2,1)S(1)} %get-tuple-element.75), channel_id=1, source_target_pairs={{1,0},{0,1},{3,2},{2,3},{5,4},{4,5},{7,6},{6,7},{9,8},{8,9},{11,10... | collective-permute-start | bytes 663560 | tf_op jit(solution)/shard_map/ppermute | solution.py:292
  41.3 5.8 %collective-permute-start.13 = (bf16[72,1536]{1,0:T(8,128)(2,1)S(1)}, bf16[72,1536]{1,0:T(8,128)(2,1)S(1)}, u32[]{:S(2)}, u32[]{:S(2)}) collective-permute-start(bf16[72,1536]{1,0:T(8,128)(2,1)S(1)} %get-tuple-element.76), channel_id=1, source_target_pairs={{2,0},{3,1},{0,2},{1,3},{6,4},{7,5},{4,6},{5,7},{10,8},{11,9},{8,1... | collective-permute-start | bytes 663560 | tf_op jit(solution)/shard_map/ppermute | solution.py:292
  42.5 8.0 %collective-permute-start.14 = (bf16[72,1536]{1,0:T(8,128)(2,1)S(1)}, bf16[72,1536]{1,0:T(8,128)(2,1)S(1)}, u32[]{:S(2)}, u32[]{:S(2)}) collective-permute-start(bf16[72,1536]{1,0:T(8,128)(2,1)S(1)} %get-tuple-element.77), channel_id=1, source_target_pairs={{3,0},{2,1},{1,2},{0,3},{7,4},{6,5},{5,6},{4,7},{11,8},{10,9},{9,1... | collective-permute-start | bytes 663560 | tf_op jit(solution)/shard_map/ppermute | solution.py:292
  50.5 0.8 copy-start
  53.1 6.8 %collective-permute-start.16 = (bf16[144,6144]{1,0:T(8,128)(2,1)S(1)}, bf16[144,6144]{1,0:T(8,128)(2,1)S(1)}, u32[]{:S(2)}, u32[]{:S(2)}) collective-permute-start(bf16[144,6144]{1,0:T(8,128)(2,1)S(1)} %get-tuple-element.79.refs_0_), channel_id=1, source_target_pairs={{4,0},{0,4},{12,8},{8,12},{20,16},{16,20},{28,24},{24,28},{5,1},{1... | collective-permute-start | bytes 5308424 | tf_op jit(solution)/shard_map/ppermute | solution.py:289
  56.6 18.0 %collective-permute-start.17 = (bf16[144,1536]{1,0:T(8,128)(2,1)S(1)}, bf16[144,1536]{1,0:T(8,128)(2,1)S(1)}, u32[]{:S(2)}, u32[]{:S(2)}) collective-permute-start(bf16[144,1536]{1,0:T(8,128)(2,1)S(1)} %get-tuple-element.83), channel_id=1, source_target_pairs={{1,0},{0,1},{3,2},{2,3},{5,4},{4,5},{7,6},{6,7},{9,8},{8,9},{11,10... | collective-permute-start | bytes 1327112 | tf_op jit(solution)/shard_map/ppermute | solution.py:292
  57.5 17.1 %collective-permute-start.18 = (bf16[144,1536]{1,0:T(8,128)(2,1)S(1)}, bf16[144,1536]{1,0:T(8,128)(2,1)S(1)}, u32[]{:S(2)}, u32[]{:S(2)}) collective-permute-start(bf16[144,1536]{1,0:T(8,128)(2,1)S(1)} %get-tuple-element.84), channel_id=1, source_target_pairs={{2,0},{3,1},{0,2},{1,3},{6,4},{7,5},{4,6},{5,7},{10,8},{11,9},{8,1... | collective-permute-start | bytes 1327112 | tf_op jit(solution)/shard_map/ppermute | solution.py:292
  58.1 20.7 %collective-permute-start.19 = (bf16[144,1536]{1,0:T(8,128)(2,1)S(1)}, bf16[144,1536]{1,0:T(8,128)(2,1)S(1)}, u32[]{:S(2)}, u32[]{:S(2)}) collective-permute-start(bf16[144,1536]{1,0:T(8,128)(2,1)S(1)} %get-tuple-element.85), channel_id=1, source_target_pairs={{3,0},{2,1},{1,2},{0,3},{7,4},{6,5},{5,6},{4,7},{11,8},{10,9},{9,1... | collective-permute-start | bytes 1327112 | tf_op jit(solution)/shard_map/ppermute | solution.py:292
  70.0 8.8 %copy-start.1 = (bf16[6144,4]{0,1:T(4,128)(2,1)S(1)}, bf16[6144,4]{0,1:T(4,128)(2,1)}, u32[]{:S(2)}) copy-start(bf16[6144,4]{0,1:T(4,128)(2,1)} %param.17) | copy-start | bytes 147460
  80.6 9.0 %collective-permute-start.25 = (bf16[144,6144]{1,0:T(8,128)(2,1)S(1)}, bf16[144,6144]{1,0:T(8,128)(2,1)S(1)}, u32[]{:S(2)}, u32[]{:S(2)}) collective-permute-start(bf16[144,6144]{1,0:T(8,128)(2,1)S(1)} %get-tuple-element.87.refs_3_.refs_0_), channel_id=1, source_target_pairs={{4,0},{0,4},{12,8},{8,12},{20,16},{16,20},{28,24},{24,28},{5,1},{1... | collective-permute-start | bytes 5308424 | tf_op jit(solution)/shard_map/ppermute | solution.py:289
  81.5 5.5 %collective-permute-start.21 = (bf16[144,3072]{1,0:T(8,128)(2,1)S(1)}, bf16[144,3072]{1,0:T(8,128)(2,1)S(1)}, u32[]{:S(2)}, u32[]{:S(2)}) collective-permute-start(bf16[144,3072]{1,0:T(8,128)(2,1)S(1)} %get-tuple-element.91), channel_id=1, source_target_pairs={{4,0},{0,4},{12,8},{8,12},{20,16},{16,20},{28,24},{24,28},{5,1},{1... | collective-permute-start | bytes 2654216 | tf_op jit(solution)/shard_map/ppermute | solution.py:289
  86.5 2.6 %collective-permute-start.20 = (bf16[144,3072]{1,0:T(8,128)(2,1)S(1)}, bf16[144,3072]{1,0:T(8,128)(2,1)S(1)}, u32[]{:S(2)}, u32[]{:S(2)}) collective-permute-start(bf16[144,3072]{1,0:T(8,128)(2,1)S(1)} %get-tuple-element.89), channel_id=1, source_target_pairs={{4,0},{0,4},{12,8},{8,12},{20,16},{16,20},{28,24},{24,28},{5,1},{1... | collective-permute-start | bytes 2654216 | tf_op jit(solution)/shard_map/ppermute | solution.py:289
  87.5 12.8 %collective-permute-start.24 = (bf16[144,1536]{1,0:T(8,128)(2,1)S(1)}, bf16[144,1536]{1,0:T(8,128)(2,1)S(1)}, u32[]{:S(2)}, u32[]{:S(2)}) collective-permute-start(bf16[144,1536]{1,0:T(8,128)(2,1)S(1)} %get-tuple-element.92.refs_3_), channel_id=1, source_target_pairs={{3,0},{2,1},{1,2},{0,3},{7,4},{6,5},{5,6},{4,7},{11,8},{10,9},{9,1... | collective-permute-start | bytes 1327112 | tf_op jit(solution)/shard_map/ppermute | solution.py:292
  99.9 5.5 %collective-permute-start.27 = (bf16[144,3072]{1,0:T(8,128)(2,1)S(1)}, bf16[144,3072]{1,0:T(8,128)(2,1)S(1)}, u32[]{:S(2)}, u32[]{:S(2)}) collective-permute-start(bf16[144,3072]{1,0:T(8,128)(2,1)S(1)} %get-tuple-element.104), channel_id=1, source_target_pairs={{4,0},{0,4},{12,8},{8,12},{20,16},{16,20},{28,24},{24,28},{5,1},{1... | collective-permute-start | bytes 2654216 | tf_op jit(solution)/shard_map/ppermute | solution.py:289
  102.9 3.1 %collective-permute-start.26 = (bf16[144,3072]{1,0:T(8,128)(2,1)S(1)}, bf16[144,3072]{1,0:T(8,128)(2,1)S(1)}, u32[]{:S(2)}, u32[]{:S(2)}) collective-permute-start(bf16[144,3072]{1,0:T(8,128)(2,1)S(1)} %get-tuple-element.102), channel_id=1, source_target_pairs={{4,0},{0,4},{12,8},{8,12},{20,16},{16,20},{28,24},{24,28},{5,1},{1... | collective-permute-start | bytes 2654216 | tf_op jit(solution)/shard_map/ppermute | solution.py:289
  103.7 11.7 %collective-permute-start.22 = (bf16[144,1536]{1,0:T(8,128)(2,1)S(1)}, bf16[144,1536]{1,0:T(8,128)(2,1)S(1)}, u32[]{:S(2)}, u32[]{:S(2)}) collective-permute-start(bf16[144,1536]{1,0:T(8,128)(2,1)S(1)} %get-tuple-element.94.refs_4_), channel_id=1, source_target_pairs={{1,0},{0,1},{3,2},{2,3},{5,4},{4,5},{7,6},{6,7},{9,8},{8,9},{11,10... | collective-permute-start | bytes 1327112 | tf_op jit(solution)/shard_map/ppermute | solution.py:292
  104.2 11.4 %collective-permute-start.23 = (bf16[144,1536]{1,0:T(8,128)(2,1)S(1)}, bf16[144,1536]{1,0:T(8,128)(2,1)S(1)}, u32[]{:S(2)}, u32[]{:S(2)}) collective-permute-start(bf16[144,1536]{1,0:T(8,128)(2,1)S(1)} %get-tuple-element.95), channel_id=1, source_target_pairs={{2,0},{3,1},{0,2},{1,3},{6,4},{7,5},{4,6},{5,7},{10,8},{11,9},{8,1... | collective-permute-start | bytes 1327112 | tf_op jit(solution)/shard_map/ppermute | solution.py:292
  106.5 18.4 %collective-permute-start.29 = (bf16[144,1536]{1,0:T(8,128)(2,1)S(1)}, bf16[144,1536]{1,0:T(8,128)(2,1)S(1)}, u32[]{:S(2)}, u32[]{:S(2)}) collective-permute-start(bf16[144,1536]{1,0:T(8,128)(2,1)S(1)} %get-tuple-element.106.refs_6_), channel_id=1, source_target_pairs={{1,0},{0,1},{3,2},{2,3},{5,4},{4,5},{7,6},{6,7},{9,8},{8,9},{11,10... | collective-permute-start | bytes 1327112 | tf_op jit(solution)/shard_map/ppermute | solution.py:292
  106.9 18.2 %collective-permute-start.30 = (bf16[144,1536]{1,0:T(8,128)(2,1)S(1)}, bf16[144,1536]{1,0:T(8,128)(2,1)S(1)}, u32[]{:S(2)}, u32[]{:S(2)}) collective-permute-start(bf16[144,1536]{1,0:T(8,128)(2,1)S(1)} %get-tuple-element.112), channel_id=1, source_target_pairs={{2,0},{3,1},{0,2},{1,3},{6,4},{7,5},{4,6},{5,7},{10,8},{11,9},{8,1... | collective-permute-start | bytes 1327112 | tf_op jit(solution)/shard_map/ppermute | solution.py:292
  108.1 26.6 %collective-permute-start.31 = (bf16[144,1536]{1,0:T(8,128)(2,1)S(1)}, bf16[144,1536]{1,0:T(8,128)(2,1)S(1)}, u32[]{:S(2)}, u32[]{:S(2)}) collective-permute-start(bf16[144,1536]{1,0:T(8,128)(2,1)S(1)} %get-tuple-element.105.refs_3_), channel_id=1, source_target_pairs={{3,0},{2,1},{1,2},{0,3},{7,4},{6,5},{5,6},{4,7},{11,8},{10,9},{9,1... | collective-permute-start | bytes 1327112 | tf_op jit(solution)/shard_map/ppermute | solution.py:292
  116.5 20.1 %collective-permute-start.28 = (bf16[96,1536]{1,0:T(8,128)(2,1)S(1)}, bf16[96,1536]{1,0:T(8,128)(2,1)S(1)}, u32[]{:S(2)}, u32[]{:S(2)}) collective-permute-start(bf16[96,1536]{1,0:T(8,128)(2,1)S(1)} %get-tuple-element.108), channel_id=1, source_target_pairs={{24,0},{28,4},{0,8},{4,12},{8,16},{12,20},{16,24},{20,28},{25,1},{... | collective-permute-start | bytes 884744 | tf_op jit(solution)/shard_map/ppermute | solution.py:286
  135.5 19.5 %collective-permute-start.32 = (bf16[96,1536]{1,0:T(8,128)(2,1)S(1)}, bf16[96,1536]{1,0:T(8,128)(2,1)S(1)}, u32[]{:S(2)}, u32[]{:S(2)}) collective-permute-start(bf16[96,1536]{1,0:T(8,128)(2,1)S(1)} %get-tuple-element.113), channel_id=1, source_target_pairs={{16,0},{20,4},{24,8},{28,12},{0,16},{4,20},{8,24},{12,28},{17,1},{... | collective-permute-start | bytes 884744 | tf_op jit(solution)/shard_map/ppermute | solution.py:286
  136.5 19.7 %collective-permute-start.33 = (bf16[96,1536]{1,0:T(8,128)(2,1)S(1)}, bf16[96,1536]{1,0:T(8,128)(2,1)S(1)}, u32[]{:S(2)}, u32[]{:S(2)}) collective-permute-start(bf16[96,1536]{1,0:T(8,128)(2,1)S(1)} %get-tuple-element.114), channel_id=1, source_target_pairs={{8,0},{12,4},{16,8},{20,12},{24,16},{28,20},{0,24},{4,28},{9,1},{1... | collective-permute-start | bytes 884744 | tf_op jit(solution)/shard_map/ppermute | solution.py:286

commit v3 on v2

--- a/solution.py
+++ b/solution.py
@@ -358,7 +358,7 @@
         pick(
             messages[1],
             [arriving[d] for d in messages[1]],
-            (*pieces[0][1:], arriving[n_chip - 1]),
+            (*pieces[0][1:],),
         )
         arriving[half] = from_chip(arriving[half - 1], 1)
     pick(messages[-1], [arriving[d] for d in messages[-1]])
@@ -451,8 +451,8 @@
     normed_a, mix_a = take_in(groups[0], picked_all)
     act_a = run_up(normed_a)
     first_a = run_down(act_a, halves[0])
-    normed_b, mix_b = take_in(groups[1], first_a[:1])
-    second_a = run_down(act_a, halves[1], (normed_b,))
+    second_a = run_down(act_a, halves[1], first_a[:1])
+    normed_b, mix_b = take_in(groups[1], second_a[:1])
     scaled, returned_a = give_back(halves[0], *first_a, mix_a)
     more, rest = give_back(halves[1], *second_a, mix_a, scaled[:1])
     returned_a |= rest

time: 158 us -> 155 us (0.981)
  waiting for transfers between devices: 73.1 us -> 69.8 us
    ppermute x18, waiting for transfers between devices: 42.1 us -> 32.7 us  [from_peer(): lax.ppermute(x, 'exp', [(i ^ k, i) for i in range(n_exp)])]
    ppermute x7, waiting for transfers between devices: 2.02 us -> 6.24 us  [from_core(): return lax.ppermute(x, 'ctx', [(i ^ 1, i) for i in range(n_ctx)])]
    ppermute x9, starting transfers between devices: 7.66 us -> 10.9 us  [from_chip(): return lax.ppermute(x, 'ctx', pairs) if d else x]
    ppermute x9, waiting for transfers between devices: 29 us -> 30.9 us  [from_chip(): return lax.ppermute(x, 'ctx', pairs) if d else x]
  transfers between devices with their start and end apart: 34 -> 34, of which waited for: 19 -> 17; matrix products, arithmetic and copies ran while one was open for 0% -> 0% of each run, Pallas kernels for 25% -> 25%
where the time goes in v3:
time: 155 us
  waiting for transfers between devices  69.8 us (45%)
  Pallas kernels  47.6 us (31%)
  starting transfers between devices  34.4 us (22%)
  other arithmetic  1.62 us (1%)
    pallas_call x20, Pallas kernels, call(): pl.pallas_call(ordered, in_specs=list(specs) + [ANY] * len(after), out_sp...  47.6 us
    ppermute x18, waiting for transfers between devices, from_peer(): lax.ppermute(x, 'exp', [(i ^ k, i) for i in range(n_exp)])  32.7 us
    ppermute x9, waiting for transfers between devices, from_chip(): return lax.ppermute(x, 'ctx', pairs) if d else x  30.9 us
    ppermute x18, starting transfers between devices, from_peer(): lax.ppermute(x, 'exp', [(i ^ k, i) for i in range(n_exp)])  15.7 us
    ppermute x9, starting transfers between devices, from_chip(): return lax.ppermute(x, 'ctx', pairs) if d else x  10.9 us
    ppermute x7, starting transfers between devices, from_core(): return lax.ppermute(x, 'ctx', [(i ^ 1, i) for i in range(n_ctx)])  7.76 us
    ppermute x7, waiting for transfers between devices, from_core(): return lax.ppermute(x, 'ctx', [(i ^ 1, i) for i in range(n_ctx)])  6.24 us
  transfers between devices with their start and end apart: 34, of which 17 were waited for; matrix products, arithmetic and copies ran while one was open for 0% of the time, Pallas kernels for 25%

profile of v3, /device:TPU:9, one launch (start us, length us, event | category | flops | bytes accessed | tf_op | source)
XLA Modules:
  0.0 155.2 jit_solution(3271820155288512239)
XLA Ops:
  0.7 1.7 %shard_map.109 = (bf16[96,512]{1,0:T(8,128)(2,1)S(1)}, bf16[96,512]{1,0:T(8,128)(2,1)S(1)}, bf16[96,1536]{1,0:T(8,128)(2,1)S(1)}, bf16[96,1536]{1,0:T(8,128)(2,1)S(1)}) custom-call(s32[10]{0:T(128)S(1)} %pad_add_fusion.refs_0_, s32[2,24]{1,0:T(2,128)} %bitcast.6, bf16[96,256]{1,0:T(8,128)(2,1)} %refs_2_.4, bf16[96,256]{1,0:T(8,128)(2,1)} %refs_3_.2, ...), custom_call_target="tpu_custom_call" | custom-call | tf_op jit(solution)/shard_map/pallas_call | solution.py:27
  2.5 2.5 %collective-permute-start.1 = (bf16[96,512]{1,0:T(8,128)(2,1)S(1)}, bf16[96,512]{1,0:T(8,128)(2,1)S(1)}, u32[]{:S(2)}, u32[]{:S(2)}) collective-permute-start(bf16[96,512]{1,0:T(8,128)(2,1)S(1)} %get-tuple-element.62.refs_0_), channel_id=1, source_target_pairs={{16,0},{20,4},{24,8},{28,12},{0,16},{4,20},{8,24},{12,28},{17,1},{... | collective-permute-start | bytes 294920 | tf_op jit(solution)/shard_map/ppermute | solution.py:286
  5.0 2.2 %collective-permute-start.2 = (bf16[96,512]{1,0:T(8,128)(2,1)S(1)}, bf16[96,512]{1,0:T(8,128)(2,1)S(1)}, u32[]{:S(2)}, u32[]{:S(2)}) collective-permute-start(bf16[96,512]{1,0:T(8,128)(2,1)S(1)} %get-tuple-element.62.refs_0_), channel_id=1, source_target_pairs={{24,0},{28,4},{0,8},{4,12},{8,16},{12,20},{16,24},{20,28},{25,1},{... | collective-permute-start | bytes 294920 | tf_op jit(solution)/shard_map/ppermute | solution.py:286
  7.2 1.2 collective-permute-start.3
  8.4 1.2 collective-permute-start.4
  9.8 3.2 %collective-permute-done.2.refs_3_ = bf16[96,512]{1,0:T(8,128)(2,1)S(1)} collective-permute-done((bf16[96,512]{1,0:T(8,128)(2,1)S(1)}, bf16[96,512]{1,0:T(8,128)(2,1)S(1)}, u32[]{:S(2)}, u32[]{:S(2)}) %collective-permute-start.2) | collective-permute-done | bytes 98336 | tf_op jit(solution)/shard_map/ppermute | solution.py:286
  13.0 1.7 %collective-permute-done.5.refs_7_ = bf16[96,512]{1,0:T(8,128)(2,1)S(1)} collective-permute-done((bf16[96,512]{1,0:T(8,128)(2,1)S(1)}, bf16[96,512]{1,0:T(8,128)(2,1)S(1)}, u32[]{:S(2)}, u32[]{:S(2)}) %collective-permute-start.5) | collective-permute-done | bytes 98336 | tf_op jit(solution)/shard_map/ppermute | solution.py:292
  14.8 2.6 %collective-permute-start.6 = (bf16[384,512]{1,0:T(8,128)(2,1)S(1)}, bf16[384,512]{1,0:T(8,128)(2,1)S(1)}, u32[]{:S(2)}, u32[]{:S(2)}) collective-permute-start(bf16[384,512]{1,0:T(8,128)(2,1)S(1)} %get-tuple-element.64.refs_3_), channel_id=1, source_target_pairs={{4,0},{0,4},{12,8},{8,12},{20,16},{16,20},{28,24},{24,28},{5,1},{1... | collective-permute-start | bytes 1179656 | tf_op jit(solution)/shard_map/ppermute | solution.py:289
  17.3 1.3 collective-permute-done.6.refs_4_
  18.7 2.5 %shard_map.111.refs_1_ = bf16[112,1536]{1,0:T(8,128)(2,1)S(1)} custom-call(s32[10]{0:T(128)S(1)} %pad_add_fusion.refs_0_, bf16[96,1536]{1,0:T(8,128)(2,1)S(1)} %get-tuple-element.60.refs_1_, bf16[96,1536]{1,0:T(8,128)(2,1)S(1)} %get-tuple-element.61.refs_2_, bf16[384,512]{1,0:T(8,128)(2,1)S(1)} %get-tuple-element.64.refs_3_, ...), custom_call_target="tpu_custom_call" | custom-call | tf_op jit(solution)/shard_map/pallas_call | solution.py:27
  21.2 1.1 shard_map.112
  23.9 1.1 collective-permute-start.9
  25.0 1.4 collective-permute-start.14
  26.5 4.0 %collective-permute-done.7.refs_1_ = bf16[112,1536]{1,0:T(8,128)(2,1)S(1)} collective-permute-done((bf16[112,1536]{1,0:T(8,128)(2,1)S(1)}, bf16[112,1536]{1,0:T(8,128)(2,1)S(1)}, u32[]{:S(2)}, u32[]{:S(2)}) %collective-permute-start.7) | collective-permute-done | bytes 344096 | tf_op jit(solution)/shard_map/ppermute | solution.py:286
  30.8 3.0 %collective-permute-done.8.refs_2_.refs_6_ = bf16[72,1536]{1,0:T(8,128)(2,1)S(1)} collective-permute-done((bf16[72,1536]{1,0:T(8,128)(2,1)S(1)}, bf16[72,1536]{1,0:T(8,128)(2,1)S(1)}, u32[]{:S(2)}, u32[]{:S(2)}) %collective-permute-start.8) | collective-permute-done | bytes 221216 | tf_op jit(solution)/shard_map/ppermute | solution.py:292
  33.9 1.5 collective-permute-done.9.refs_3_.refs_7_
  35.4 1.1 shard_map.113
  37.5 1.7 %collective-permute-start.13 = (bf16[72,1536]{1,0:T(8,128)(2,1)S(1)}, bf16[72,1536]{1,0:T(8,128)(2,1)S(1)}, u32[]{:S(2)}, u32[]{:S(2)}) collective-permute-start(bf16[72,1536]{1,0:T(8,128)(2,1)S(1)} %get-tuple-element.77), channel_id=1, source_target_pairs={{3,0},{2,1},{1,2},{0,3},{7,4},{6,5},{5,6},{4,7},{11,8},{10,9},{9,1... | collective-permute-start | bytes 663560 | tf_op jit(solution)/shard_map/ppermute | solution.py:292
  39.9 4.0 %collective-permute-done.15.refs_2_ = bf16[112,1536]{1,0:T(8,128)(2,1)S(1)} collective-permute-done((bf16[112,1536]{1,0:T(8,128)(2,1)S(1)}, bf16[112,1536]{1,0:T(8,128)(2,1)S(1)}, u32[]{:S(2)}, u32[]{:S(2)}) %collective-permute-start.15) | collective-permute-done | bytes 344096 | tf_op jit(solution)/shard_map/ppermute | solution.py:286
  43.9 1.3 shard_map.114
  45.3 2.5 %collective-permute-done.13.refs_12_ = bf16[72,1536]{1,0:T(8,128)(2,1)S(1)} collective-permute-done((bf16[72,1536]{1,0:T(8,128)(2,1)S(1)}, bf16[72,1536]{1,0:T(8,128)(2,1)S(1)}, u32[]{:S(2)}, u32[]{:S(2)}) %collective-permute-start.13) | collective-permute-done | bytes 221216 | tf_op jit(solution)/shard_map/ppermute | solution.py:292
  48.6 1.8 %shard_map.115 = (bf16[144,6144]{1,0:T(8,128)(2,1)S(1)}, f32[144,128]{1,0:T(8,128)S(1)}) custom-call(s32[10]{0:T(128)S(1)} %pad_add_fusion.refs_0_, bf16[1,6144]{1,0:T(2,128)(2,1)S(1)} %reshape.3.refs_1_, bf16[4,6144]{1,0:T(4,128)(2,1)S(1)} %bitcast.4, f32[72,128]{1,0:T(8,128)S(1)} %get-tuple-element.71.refs_3_, f32[72,128]{1,0:T(8,128)S(1)} %get-tuple-element.72.refs_4_, ...), custom_call_target="tpu_custom_call" | custom-call | tf_op jit(solution)/shard_map/pallas_call | solution.py:27
  50.5 1.7 %collective-permute-start.16 = (bf16[144,6144]{1,0:T(8,128)(2,1)S(1)}, bf16[144,6144]{1,0:T(8,128)(2,1)S(1)}, u32[]{:S(2)}, u32[]{:S(2)}) collective-permute-start(bf16[144,6144]{1,0:T(8,128)(2,1)S(1)} %get-tuple-element.79.refs_0_), channel_id=1, source_target_pairs={{4,0},{0,4},{12,8},{8,12},{20,16},{16,20},{28,24},{24,28},{5,1},{1... | collective-permute-start | bytes 5308424 | tf_op jit(solution)/shard_map/ppermute | solution.py:289
  52.2 1.7 %collective-permute-start.22 = (bf16[144,1536]{1,0:T(8,128)(2,1)S(1)}, bf16[144,1536]{1,0:T(8,128)(2,1)S(1)}, u32[]{:S(2)}, u32[]{:S(2)}) collective-permute-start(bf16[144,1536]{1,0:T(8,128)(2,1)S(1)} %get-tuple-element.92), channel_id=1, source_target_pairs={{1,0},{0,1},{3,2},{2,3},{5,4},{4,5},{7,6},{6,7},{9,8},{8,9},{11,10... | collective-permute-start | bytes 1327112 | tf_op jit(solution)/shard_map/ppermute | solution.py:292
  53.9 1.2 collective-permute-start.24
  55.5 10.1 %shard_map.116 = (bf16[288,1024]{1,0:T(8,128)(2,1)S(1)}, bf16[6144,1024]{1,0:T(8,128)(2,1)S(1)}, bf16[6144,1024]{1,0:T(8,128)(2,1)S(1)}) custom-call(bf16[144,6144]{1,0:T(8,128)(2,1)S(1)} %get-tuple-element.79.refs_0_, bf16[144,6144]{1,0:T(8,128)(2,1)S(1)} %collective-permute-done.16.refs_1_, bf16[1,6144,1024]{2,1,0:T(8,128)(2,1)} %refs_2_.5, ...), custom_call_target="tpu_custom_call" | custom-call | tf_op jit(solution)/shard_map/pallas_call | solution.py:27
  65.6 4.7 %shard_map.117 = (bf16[144,3072]{1,0:T(8,128)(2,1)S(1)}, bf16[144,3072]{1,0:T(8,128)(2,1)S(1)}, bf16[2,1024,1536]{2,1,0:T(8,128)(2,1)S(1)}) custom-call(s32[10]{0:T(128)S(1)} %pad_add_fusion.refs_0_, bf16[288,1024]{1,0:T(8,128)(2,1)S(1)} %get-tuple-element.80.refs_1_, bf16[1,1024,6144]{2,1,0:T(8,128)(2,1)} %refs_2_.7), custom_call_target="tpu_custom_call" | custom-call | tf_op jit(solution)/shard_map/pallas_call | solution.py:27
  70.3 4.6 %shard_map.118 = (bf16[144,3072]{1,0:T(8,128)(2,1)S(1)}, bf16[144,3072]{1,0:T(8,128)(2,1)S(1)}, bf16[2,1024,1536]{2,1,0:T(8,128)(2,1)S(1)}) custom-call(s32[10]{0:T(128)S(1)} %pad_add_fusion.refs_0_, bf16[288,1024]{1,0:T(8,128)(2,1)S(1)} %get-tuple-element.80.refs_1_, bf16[1,1024,6144]{2,1,0:T(8,128)(2,1)} %refs_2_.7, ...), custom_call_target="tpu_custom_call" | custom-call | tf_op jit(solution)/shard_map/pallas_call | solution.py:27
  75.0 2.1 %shard_map.121 = (bf16[144,6144]{1,0:T(8,128)(2,1)S(1)}, f32[144,128]{1,0:T(8,128)S(1)}) custom-call(s32[10]{0:T(128)S(1)} %pad_add_fusion.refs_0_, bf16[1,6144]{1,0:T(2,128)(2,1)S(1)} %reshape.3.refs_1_, bf16[4,6144]{1,0:T(4,128)(2,1)S(1)} %bitcast.5, f32[72,128]{1,0:T(8,128)S(1)} %get-tuple-element.78.refs_13_.refs_3_, ...), custom_call_target="tpu_custom_call" | custom-call | tf_op jit(solution)/shard_map/pallas_call | solution.py:27
  77.0 1.1 collective-permute-start.25
  78.6 4.1 %collective-permute-done.18.refs_1_ = bf16[144,3072]{1,0:T(8,128)(2,1)S(1)} collective-permute-done((bf16[144,3072]{1,0:T(8,128)(2,1)S(1)}, bf16[144,3072]{1,0:T(8,128)(2,1)S(1)}, u32[]{:S(2)}, u32[]{:S(2)}) %collective-permute-start.18) | collective-permute-done | bytes 884768 | tf_op jit(solution)/shard_map/ppermute | solution.py:289
  83.2 0.9 collective-permute-start.21
  84.7 7.7 %shard_map.122.refs_1_ = bf16[288,1024]{1,0:T(8,128)(2,1)S(1)} custom-call(bf16[144,6144]{1,0:T(8,128)(2,1)S(1)} %get-tuple-element.95.refs_0_, bf16[144,6144]{1,0:T(8,128)(2,1)S(1)} %collective-permute-done.25.refs_1_, bf16[6144,1024]{1,0:T(8,128)(2,1)S(1)} %get-tuple-element.96.refs_2_, bf16[6144,1024]{1,0:T(8,128)(2,1)S(1)} %get-tuple-element.97.refs_3_, ...), custom_call_target="tpu_custom_call" | custom-call | tf_op jit(solution)/shard_map/pallas_call | solution.py:27
  92.4 2.6 %shard_map.123 = (bf16[144,3072]{1,0:T(8,128)(2,1)S(1)}, bf16[144,3072]{1,0:T(8,128)(2,1)S(1)}) custom-call(s32[10]{0:T(128)S(1)} %pad_add_fusion.refs_0_, bf16[288,1024]{1,0:T(8,128)(2,1)S(1)} %shard_map.122.refs_1_, bf16[2,1024,1536]{2,1,0:T(8,128)(2,1)S(1)} %get-tuple-element.99.refs_2_), custom_call_target="tpu_custom_call" | custom-call | tf_op jit(solution)/shard_map/pallas_call | solution.py:27
  95.7 2.6 %shard_map.124 = (bf16[144,3072]{1,0:T(8,128)(2,1)S(1)}, bf16[144,3072]{1,0:T(8,128)(2,1)S(1)}) custom-call(s32[10]{0:T(128)S(1)} %pad_add_fusion.refs_0_, bf16[288,1024]{1,0:T(8,128)(2,1)S(1)} %shard_map.122.refs_1_, bf16[2,1024,1536]{2,1,0:T(8,128)(2,1)S(1)} %get-tuple-element.98.refs_2_, bf16[144,3072]{1,0:T(8,128)(2,1)S(1)} %get-tuple-element.100.refs_3_.refs_0_, ...), custom_call_target="tpu_custom_call" | custom-call | tf_op jit(solution)/shard_map/pallas_call | solution.py:27
  98.3 1.2 collective-permute-start.26
  99.5 1.0 collective-permute-start.19
  102.1 1.1 collective-permute-start.29
  103.6 1.2 collective-permute-start.31
  104.8 6.4 %collective-permute-done.19.refs_3_ = bf16[144,1536]{1,0:T(8,128)(2,1)S(1)} collective-permute-done((bf16[144,1536]{1,0:T(8,128)(2,1)S(1)}, bf16[144,1536]{1,0:T(8,128)(2,1)S(1)}, u32[]{:S(2)}, u32[]{:S(2)}) %collective-permute-start.19) | collective-permute-done | bytes 442400 | tf_op jit(solution)/shard_map/ppermute | solution.py:292
  112.7 1.4 collective-permute-start.28
  114.1 6.6 %collective-permute-done.29.refs_3_ = bf16[144,1536]{1,0:T(8,128)(2,1)S(1)} collective-permute-done((bf16[144,1536]{1,0:T(8,128)(2,1)S(1)}, bf16[144,1536]{1,0:T(8,128)(2,1)S(1)}, u32[]{:S(2)}, u32[]{:S(2)}) %collective-permute-start.29) | collective-permute-done | bytes 442400 | tf_op jit(solution)/shard_map/ppermute | solution.py:292
  120.7 10.2 %collective-permute-done.30.refs_4_ = bf16[144,1536]{1,0:T(8,128)(2,1)S(1)} collective-permute-done((bf16[144,1536]{1,0:T(8,128)(2,1)S(1)}, bf16[144,1536]{1,0:T(8,128)(2,1)S(1)}, u32[]{:S(2)}, u32[]{:S(2)}) %collective-permute-start.30) | collective-permute-done | bytes 442400 | tf_op jit(solution)/shard_map/ppermute | solution.py:292
  131.7 1.7 %collective-permute-start.32 = (bf16[96,1536]{1,0:T(8,128)(2,1)S(1)}, bf16[96,1536]{1,0:T(8,128)(2,1)S(1)}, u32[]{:S(2)}, u32[]{:S(2)}) collective-permute-start(bf16[96,1536]{1,0:T(8,128)(2,1)S(1)} %get-tuple-element.113), channel_id=1, source_target_pairs={{16,0},{20,4},{24,8},{28,12},{0,16},{4,20},{8,24},{12,28},{17,1},{... | collective-permute-start | bytes 884744 | tf_op jit(solution)/shard_map/ppermute | solution.py:286
  133.5 1.2 collective-permute-start.33
  134.7 17.2 %collective-permute-done.32 = bf16[96,1536]{1,0:T(8,128)(2,1)S(1)} collective-permute-done((bf16[96,1536]{1,0:T(8,128)(2,1)S(1)}, bf16[96,1536]{1,0:T(8,128)(2,1)S(1)}, u32[]{:S(2)}, u32[]{:S(2)}) %collective-permute-start.32) | collective-permute-done | bytes 294944 | tf_op jit(solution)/shard_map/ppermute | solution.py:286
  151.9 2.4 %collective-permute-done.33 = bf16[96,1536]{1,0:T(8,128)(2,1)S(1)} collective-permute-done((bf16[96,1536]{1,0:T(8,128)(2,1)S(1)}, bf16[96,1536]{1,0:T(8,128)(2,1)S(1)}, u32[]{:S(2)}, u32[]{:S(2)}) %collective-permute-start.33) | collective-permute-done | bytes 294944 | tf_op jit(solution)/shard_map/ppermute | solution.py:286
  154.3 0.9 add_convert_fusion
  (47 shorter events, 12.6 us)
Async XLA Ops:
  2.4 7.2 %collective-permute-start = (bf16[96,512]{1,0:T(8,128)(2,1)S(1)}, bf16[96,512]{1,0:T(8,128)(2,1)S(1)}, u32[]{:S(2)}, u32[]{:S(2)}) collective-permute-start(bf16[96,512]{1,0:T(8,128)(2,1)S(1)} %get-tuple-element.62.refs_0_), channel_id=1, source_target_pairs={{8,0},{12,4},{16,8},{20,12},{24,16},{28,20},{0,24},{4,28},{9,1},{1... | collective-permute-start | bytes 294920 | tf_op jit(solution)/shard_map/ppermute | solution.py:286
  2.5 7.3 %collective-permute-start.1 = (bf16[96,512]{1,0:T(8,128)(2,1)S(1)}, bf16[96,512]{1,0:T(8,128)(2,1)S(1)}, u32[]{:S(2)}, u32[]{:S(2)}) collective-permute-start(bf16[96,512]{1,0:T(8,128)(2,1)S(1)} %get-tuple-element.62.refs_0_), channel_id=1, source_target_pairs={{16,0},{20,4},{24,8},{28,12},{0,16},{4,20},{8,24},{12,28},{17,1},{... | collective-permute-start | bytes 294920 | tf_op jit(solution)/shard_map/ppermute | solution.py:286
  5.0 8.1 %collective-permute-start.2 = (bf16[96,512]{1,0:T(8,128)(2,1)S(1)}, bf16[96,512]{1,0:T(8,128)(2,1)S(1)}, u32[]{:S(2)}, u32[]{:S(2)}) collective-permute-start(bf16[96,512]{1,0:T(8,128)(2,1)S(1)} %get-tuple-element.62.refs_0_), channel_id=1, source_target_pairs={{24,0},{28,4},{0,8},{4,12},{8,16},{12,20},{16,24},{20,28},{25,1},{... | collective-permute-start | bytes 294920 | tf_op jit(solution)/shard_map/ppermute | solution.py:286
  7.2 5.9 %collective-permute-start.3 = (bf16[96,512]{1,0:T(8,128)(2,1)S(1)}, bf16[96,512]{1,0:T(8,128)(2,1)S(1)}, u32[]{:S(2)}, u32[]{:S(2)}) collective-permute-start(bf16[96,512]{1,0:T(8,128)(2,1)S(1)} %get-tuple-element.63.refs_4_), channel_id=1, source_target_pairs={{1,0},{0,1},{3,2},{2,3},{5,4},{4,5},{7,6},{6,7},{9,8},{8,9},{11,10... | collective-permute-start | bytes 294920 | tf_op jit(solution)/shard_map/ppermute | solution.py:292
  8.4 4.7 %collective-permute-start.4 = (bf16[96,512]{1,0:T(8,128)(2,1)S(1)}, bf16[96,512]{1,0:T(8,128)(2,1)S(1)}, u32[]{:S(2)}, u32[]{:S(2)}) collective-permute-start(bf16[96,512]{1,0:T(8,128)(2,1)S(1)} %get-tuple-element.63.refs_4_), channel_id=1, source_target_pairs={{2,0},{3,1},{0,2},{1,3},{6,4},{7,5},{4,6},{5,7},{10,8},{11,9},{8,1... | collective-permute-start | bytes 294920 | tf_op jit(solution)/shard_map/ppermute | solution.py:292
  9.6 5.1 %collective-permute-start.5 = (bf16[96,512]{1,0:T(8,128)(2,1)S(1)}, bf16[96,512]{1,0:T(8,128)(2,1)S(1)}, u32[]{:S(2)}, u32[]{:S(2)}) collective-permute-start(bf16[96,512]{1,0:T(8,128)(2,1)S(1)} %get-tuple-element.63.refs_4_), channel_id=1, source_target_pairs={{3,0},{2,1},{1,2},{0,3},{7,4},{6,5},{5,6},{4,7},{11,8},{10,9},{9,1... | collective-permute-start | bytes 294920 | tf_op jit(solution)/shard_map/ppermute | solution.py:292
  14.8 3.9 %collective-permute-start.6 = (bf16[384,512]{1,0:T(8,128)(2,1)S(1)}, bf16[384,512]{1,0:T(8,128)(2,1)S(1)}, u32[]{:S(2)}, u32[]{:S(2)}) collective-permute-start(bf16[384,512]{1,0:T(8,128)(2,1)S(1)} %get-tuple-element.64.refs_3_), channel_id=1, source_target_pairs={{4,0},{0,4},{12,8},{8,12},{20,16},{16,20},{28,24},{24,28},{5,1},{1... | collective-permute-start | bytes 1179656 | tf_op jit(solution)/shard_map/ppermute | solution.py:289
  21.2 9.3 %collective-permute-start.7 = (bf16[112,1536]{1,0:T(8,128)(2,1)S(1)}, bf16[112,1536]{1,0:T(8,128)(2,1)S(1)}, u32[]{:S(2)}, u32[]{:S(2)}) collective-permute-start(bf16[112,1536]{1,0:T(8,128)(2,1)S(1)} %shard_map.111.refs_1_), channel_id=1, source_target_pairs={{8,0},{12,4},{16,8},{20,12},{24,16},{28,20},{0,24},{4,28},{9,1},{1... | collective-permute-start | bytes 1032200 | tf_op jit(solution)/shard_map/ppermute | solution.py:286
  22.3 8.5 %collective-permute-start.10 = (bf16[72,1536]{1,0:T(8,128)(2,1)S(1)}, bf16[72,1536]{1,0:T(8,128)(2,1)S(1)}, u32[]{:S(2)}, u32[]{:S(2)}) collective-permute-start(bf16[72,1536]{1,0:T(8,128)(2,1)S(1)} %get-tuple-element.69), channel_id=1, source_target_pairs={{3,0},{2,1},{1,2},{0,3},{7,4},{6,5},{5,6},{4,7},{11,8},{10,9},{9,1... | collective-permute-start | bytes 663560 | tf_op jit(solution)/shard_map/ppermute | solution.py:292
  23.0 10.8 %collective-permute-start.8 = (bf16[72,1536]{1,0:T(8,128)(2,1)S(1)}, bf16[72,1536]{1,0:T(8,128)(2,1)S(1)}, u32[]{:S(2)}, u32[]{:S(2)}) collective-permute-start(bf16[72,1536]{1,0:T(8,128)(2,1)S(1)} %get-tuple-element.67), channel_id=1, source_target_pairs={{1,0},{0,1},{3,2},{2,3},{5,4},{4,5},{7,6},{6,7},{9,8},{8,9},{11,10... | collective-permute-start | bytes 663560 | tf_op jit(solution)/shard_map/ppermute | solution.py:292
  23.9 11.5 %collective-permute-start.9 = (bf16[72,1536]{1,0:T(8,128)(2,1)S(1)}, bf16[72,1536]{1,0:T(8,128)(2,1)S(1)}, u32[]{:S(2)}, u32[]{:S(2)}) collective-permute-start(bf16[72,1536]{1,0:T(8,128)(2,1)S(1)} %get-tuple-element.68), channel_id=1, source_target_pairs={{2,0},{3,1},{0,2},{1,3},{6,4},{7,5},{4,6},{5,7},{10,8},{11,9},{8,1... | collective-permute-start | bytes 663560 | tf_op jit(solution)/shard_map/ppermute | solution.py:292
  25.0 14.9 %collective-permute-start.14 = (bf16[112,1536]{1,0:T(8,128)(2,1)S(1)}, bf16[112,1536]{1,0:T(8,128)(2,1)S(1)}, u32[]{:S(2)}, u32[]{:S(2)}) collective-permute-start(bf16[112,1536]{1,0:T(8,128)(2,1)S(1)} %shard_map.111.refs_1_), channel_id=1, source_target_pairs={{24,0},{28,4},{0,8},{4,12},{8,16},{12,20},{16,24},{20,28},{25,1},{... | collective-permute-start | bytes 1032200 | tf_op jit(solution)/shard_map/ppermute | solution.py:286
  30.5 13.4 %collective-permute-start.15 = (bf16[112,1536]{1,0:T(8,128)(2,1)S(1)}, bf16[112,1536]{1,0:T(8,128)(2,1)S(1)}, u32[]{:S(2)}, u32[]{:S(2)}) collective-permute-start(bf16[112,1536]{1,0:T(8,128)(2,1)S(1)} %collective-permute-done.7.refs_1_), channel_id=1, source_target_pairs={{8,0},{12,4},{16,8},{20,12},{24,16},{28,20},{0,24},{4,28},{9,1},{1... | collective-permute-start | bytes 1032200 | tf_op jit(solution)/shard_map/ppermute | solution.py:286
  36.5 8.8 %collective-permute-start.11 = (bf16[72,1536]{1,0:T(8,128)(2,1)S(1)}, bf16[72,1536]{1,0:T(8,128)(2,1)S(1)}, u32[]{:S(2)}, u32[]{:S(2)}) collective-permute-start(bf16[72,1536]{1,0:T(8,128)(2,1)S(1)} %get-tuple-element.75), channel_id=1, source_target_pairs={{1,0},{0,1},{3,2},{2,3},{5,4},{4,5},{7,6},{6,7},{9,8},{8,9},{11,10... | collective-permute-start | bytes 663560 | tf_op jit(solution)/shard_map/ppermute | solution.py:292
  36.8 8.5 %collective-permute-start.12 = (bf16[72,1536]{1,0:T(8,128)(2,1)S(1)}, bf16[72,1536]{1,0:T(8,128)(2,1)S(1)}, u32[]{:S(2)}, u32[]{:S(2)}) collective-permute-start(bf16[72,1536]{1,0:T(8,128)(2,1)S(1)} %get-tuple-element.76), channel_id=1, source_target_pairs={{2,0},{3,1},{0,2},{1,3},{6,4},{7,5},{4,6},{5,7},{10,8},{11,9},{8,1... | collective-permute-start | bytes 663560 | tf_op jit(solution)/shard_map/ppermute | solution.py:292
  37.5 10.4 %collective-permute-start.13 = (bf16[72,1536]{1,0:T(8,128)(2,1)S(1)}, bf16[72,1536]{1,0:T(8,128)(2,1)S(1)}, u32[]{:S(2)}, u32[]{:S(2)}) collective-permute-start(bf16[72,1536]{1,0:T(8,128)(2,1)S(1)} %get-tuple-element.77), channel_id=1, source_target_pairs={{3,0},{2,1},{1,2},{0,3},{7,4},{6,5},{5,6},{4,7},{11,8},{10,9},{9,1... | collective-permute-start | bytes 663560 | tf_op jit(solution)/shard_map/ppermute | solution.py:292
  47.8 0.8 copy-start
  50.5 5.1 %collective-permute-start.16 = (bf16[144,6144]{1,0:T(8,128)(2,1)S(1)}, bf16[144,6144]{1,0:T(8,128)(2,1)S(1)}, u32[]{:S(2)}, u32[]{:S(2)}) collective-permute-start(bf16[144,6144]{1,0:T(8,128)(2,1)S(1)} %get-tuple-element.79.refs_0_), channel_id=1, source_target_pairs={{4,0},{0,4},{12,8},{8,12},{20,16},{16,20},{28,24},{24,28},{5,1},{1... | collective-permute-start | bytes 5308424 | tf_op jit(solution)/shard_map/ppermute | solution.py:289
  52.2 22.7 %collective-permute-start.22 = (bf16[144,1536]{1,0:T(8,128)(2,1)S(1)}, bf16[144,1536]{1,0:T(8,128)(2,1)S(1)}, u32[]{:S(2)}, u32[]{:S(2)}) collective-permute-start(bf16[144,1536]{1,0:T(8,128)(2,1)S(1)} %get-tuple-element.92), channel_id=1, source_target_pairs={{1,0},{0,1},{3,2},{2,3},{5,4},{4,5},{7,6},{6,7},{9,8},{8,9},{11,10... | collective-permute-start | bytes 1327112 | tf_op jit(solution)/shard_map/ppermute | solution.py:292
  53.9 21.1 %collective-permute-start.23 = (bf16[144,1536]{1,0:T(8,128)(2,1)S(1)}, bf16[144,1536]{1,0:T(8,128)(2,1)S(1)}, u32[]{:S(2)}, u32[]{:S(2)}) collective-permute-start(bf16[144,1536]{1,0:T(8,128)(2,1)S(1)} %get-tuple-element.93), channel_id=1, source_target_pairs={{2,0},{3,1},{0,2},{1,3},{6,4},{7,5},{4,6},{5,7},{10,8},{11,9},{8,1... | collective-permute-start | bytes 1327112 | tf_op jit(solution)/shard_map/ppermute | solution.py:292
  53.9 21.1 %collective-permute-start.24 = (bf16[144,1536]{1,0:T(8,128)(2,1)S(1)}, bf16[144,1536]{1,0:T(8,128)(2,1)S(1)}, u32[]{:S(2)}, u32[]{:S(2)}) collective-permute-start(bf16[144,1536]{1,0:T(8,128)(2,1)S(1)} %get-tuple-element.94), channel_id=1, source_target_pairs={{3,0},{2,1},{1,2},{0,3},{7,4},{6,5},{5,6},{4,7},{11,8},{10,9},{9,1... | collective-permute-start | bytes 1327112 | tf_op jit(solution)/shard_map/ppermute | solution.py:292
  70.3 4.7 %copy-start.1 = (bf16[6144,4]{0,1:T(4,128)(2,1)S(1)}, bf16[6144,4]{0,1:T(4,128)(2,1)}, u32[]{:S(2)}) copy-start(bf16[6144,4]{0,1:T(4,128)(2,1)} %param.17) | copy-start | bytes 147460
  77.0 7.7 %collective-permute-start.25 = (bf16[144,6144]{1,0:T(8,128)(2,1)S(1)}, bf16[144,6144]{1,0:T(8,128)(2,1)S(1)}, u32[]{:S(2)}, u32[]{:S(2)}) collective-permute-start(bf16[144,6144]{1,0:T(8,128)(2,1)S(1)} %get-tuple-element.95.refs_0_), channel_id=1, source_target_pairs={{4,0},{0,4},{12,8},{8,12},{20,16},{16,20},{28,24},{24,28},{5,1},{1... | collective-permute-start | bytes 5308424 | tf_op jit(solution)/shard_map/ppermute | solution.py:289
  78.1 4.6 %collective-permute-start.18 = (bf16[144,3072]{1,0:T(8,128)(2,1)S(1)}, bf16[144,3072]{1,0:T(8,128)(2,1)S(1)}, u32[]{:S(2)}, u32[]{:S(2)}) collective-permute-start(bf16[144,3072]{1,0:T(8,128)(2,1)S(1)} %get-tuple-element.85), channel_id=1, source_target_pairs={{4,0},{0,4},{12,8},{8,12},{20,16},{16,20},{28,24},{24,28},{5,1},{1... | collective-permute-start | bytes 2654216 | tf_op jit(solution)/shard_map/ppermute | solution.py:289
  78.2 6.0 %collective-permute-start.17 = (bf16[144,3072]{1,0:T(8,128)(2,1)S(1)}, bf16[144,3072]{1,0:T(8,128)(2,1)S(1)}, u32[]{:S(2)}, u32[]{:S(2)}) collective-permute-start(bf16[144,3072]{1,0:T(8,128)(2,1)S(1)} %get-tuple-element.83), channel_id=1, source_target_pairs={{4,0},{0,4},{12,8},{8,12},{20,16},{16,20},{28,24},{24,28},{5,1},{1... | collective-permute-start | bytes 2654216 | tf_op jit(solution)/shard_map/ppermute | solution.py:289
  83.2 12.4 %collective-permute-start.21 = (bf16[144,1536]{1,0:T(8,128)(2,1)S(1)}, bf16[144,1536]{1,0:T(8,128)(2,1)S(1)}, u32[]{:S(2)}, u32[]{:S(2)}) collective-permute-start(bf16[144,1536]{1,0:T(8,128)(2,1)S(1)} %get-tuple-element.86.refs_3_), channel_id=1, source_target_pairs={{3,0},{2,1},{1,2},{0,3},{7,4},{6,5},{5,6},{4,7},{11,8},{10,9},{9,1... | collective-permute-start | bytes 1327112 | tf_op jit(solution)/shard_map/ppermute | solution.py:292
  94.9 5.7 %collective-permute-start.27 = (bf16[144,3072]{1,0:T(8,128)(2,1)S(1)}, bf16[144,3072]{1,0:T(8,128)(2,1)S(1)}, u32[]{:S(2)}, u32[]{:S(2)}) collective-permute-start(bf16[144,3072]{1,0:T(8,128)(2,1)S(1)} %get-tuple-element.104), channel_id=1, source_target_pairs={{4,0},{0,4},{12,8},{8,12},{20,16},{16,20},{28,24},{24,28},{5,1},{1... | collective-permute-start | bytes 2654216 | tf_op jit(solution)/shard_map/ppermute | solution.py:289
  98.3 3.2 %collective-permute-start.26 = (bf16[144,3072]{1,0:T(8,128)(2,1)S(1)}, bf16[144,3072]{1,0:T(8,128)(2,1)S(1)}, u32[]{:S(2)}, u32[]{:S(2)}) collective-permute-start(bf16[144,3072]{1,0:T(8,128)(2,1)S(1)} %get-tuple-element.102), channel_id=1, source_target_pairs={{4,0},{0,4},{12,8},{8,12},{20,16},{16,20},{28,24},{24,28},{5,1},{1... | collective-permute-start | bytes 2654216 | tf_op jit(solution)/shard_map/ppermute | solution.py:289
  99.5 11.7 %collective-permute-start.19 = (bf16[144,1536]{1,0:T(8,128)(2,1)S(1)}, bf16[144,1536]{1,0:T(8,128)(2,1)S(1)}, u32[]{:S(2)}, u32[]{:S(2)}) collective-permute-start(bf16[144,1536]{1,0:T(8,128)(2,1)S(1)} %get-tuple-element.88.refs_4_), channel_id=1, source_target_pairs={{1,0},{0,1},{3,2},{2,3},{5,4},{4,5},{7,6},{6,7},{9,8},{8,9},{11,10... | collective-permute-start | bytes 1327112 | tf_op jit(solution)/shard_map/ppermute | solution.py:292
  100.5 11.4 %collective-permute-start.20 = (bf16[144,1536]{1,0:T(8,128)(2,1)S(1)}, bf16[144,1536]{1,0:T(8,128)(2,1)S(1)}, u32[]{:S(2)}, u32[]{:S(2)}) collective-permute-start(bf16[144,1536]{1,0:T(8,128)(2,1)S(1)} %get-tuple-element.89), channel_id=1, source_target_pairs={{2,0},{3,1},{0,2},{1,3},{6,4},{7,5},{4,6},{5,7},{10,8},{11,9},{8,1... | collective-permute-start | bytes 1327112 | tf_op jit(solution)/shard_map/ppermute | solution.py:292
  102.1 18.6 %collective-permute-start.29 = (bf16[144,1536]{1,0:T(8,128)(2,1)S(1)}, bf16[144,1536]{1,0:T(8,128)(2,1)S(1)}, u32[]{:S(2)}, u32[]{:S(2)}) collective-permute-start(bf16[144,1536]{1,0:T(8,128)(2,1)S(1)} %get-tuple-element.106.refs_6_), channel_id=1, source_target_pairs={{1,0},{0,1},{3,2},{2,3},{5,4},{4,5},{7,6},{6,7},{9,8},{8,9},{11,10... | collective-permute-start | bytes 1327112 | tf_op jit(solution)/shard_map/ppermute | solution.py:292
  103.2 27.7 %collective-permute-start.30 = (bf16[144,1536]{1,0:T(8,128)(2,1)S(1)}, bf16[144,1536]{1,0:T(8,128)(2,1)S(1)}, u32[]{:S(2)}, u32[]{:S(2)}) collective-permute-start(bf16[144,1536]{1,0:T(8,128)(2,1)S(1)} %get-tuple-element.112), channel_id=1, source_target_pairs={{2,0},{3,1},{0,2},{1,3},{6,4},{7,5},{4,6},{5,7},{10,8},{11,9},{8,1... | collective-permute-start | bytes 1327112 | tf_op jit(solution)/shard_map/ppermute | solution.py:292
  103.6 27.3 %collective-permute-start.31 = (bf16[144,1536]{1,0:T(8,128)(2,1)S(1)}, bf16[144,1536]{1,0:T(8,128)(2,1)S(1)}, u32[]{:S(2)}, u32[]{:S(2)}) collective-permute-start(bf16[144,1536]{1,0:T(8,128)(2,1)S(1)} %get-tuple-element.105.refs_3_), channel_id=1, source_target_pairs={{3,0},{2,1},{1,2},{0,3},{7,4},{6,5},{5,6},{4,7},{11,8},{10,9},{9,1... | collective-permute-start | bytes 1327112 | tf_op jit(solution)/shard_map/ppermute | solution.py:292
  112.7 22.0 %collective-permute-start.28 = (bf16[96,1536]{1,0:T(8,128)(2,1)S(1)}, bf16[96,1536]{1,0:T(8,128)(2,1)S(1)}, u32[]{:S(2)}, u32[]{:S(2)}) collective-permute-start(bf16[96,1536]{1,0:T(8,128)(2,1)S(1)} %get-tuple-element.108), channel_id=1, source_target_pairs={{24,0},{28,4},{0,8},{4,12},{8,16},{12,20},{16,24},{20,28},{25,1},{... | collective-permute-start | bytes 884744 | tf_op jit(solution)/shard_map/ppermute | solution.py:286
  131.7 20.2 %collective-permute-start.32 = (bf16[96,1536]{1,0:T(8,128)(2,1)S(1)}, bf16[96,1536]{1,0:T(8,128)(2,1)S(1)}, u32[]{:S(2)}, u32[]{:S(2)}) collective-permute-start(bf16[96,1536]{1,0:T(8,128)(2,1)S(1)} %get-tuple-element.113), channel_id=1, source_target_pairs={{16,0},{20,4},{24,8},{28,12},{0,16},{4,20},{8,24},{12,28},{17,1},{... | collective-permute-start | bytes 884744 | tf_op jit(solution)/shard_map/ppermute | solution.py:286
  133.5 20.8 %collective-permute-start.33 = (bf16[96,1536]{1,0:T(8,128)(2,1)S(1)}, bf16[96,1536]{1,0:T(8,128)(2,1)S(1)}, u32[]{:S(2)}, u32[]{:S(2)}) collective-permute-start(bf16[96,1536]{1,0:T(8,128)(2,1)S(1)} %get-tuple-element.114), channel_id=1, source_target_pairs={{8,0},{12,4},{16,8},{20,12},{24,16},{28,20},{0,24},{4,28},{9,1},{1... | collective-permute-start | bytes 884744 | tf_op jit(solution)/shard_map/ppermute | solution.py:286

commit v4 on v3

--- a/solution.py
+++ b/solution.py
@@ -35,7 +35,8 @@
 
 
 def pack_kernel(
-    where_ref, ids_ref, k_ref, v_ref, q_ref, res_ref, out_ref, row_ref, q_out, res_out, ids_vmem, sems
+    where_ref, ids_ref, k_ref, v_ref, q_ref, res_ref, w_ref,
+    out_ref, row_ref, q_out, res_out, w_out, ids_vmem, sems,
 ):
     kv = k_ref.shape[1]
     sub = ids_ref.shape[1]
@@ -45,6 +46,7 @@
         pltpu.make_async_copy(v_ref, out_ref.at[:, kv:], sems.at[2]),
         pltpu.make_async_copy(q_ref, q_out, sems.at[3]),
         pltpu.make_async_copy(res_ref, res_out, sems.at[4]),
+        pltpu.make_async_copy(w_ref, w_out, sems.at[5]),
     ]
     for copy in copies:
         copy.start()
@@ -291,19 +293,20 @@
     def from_peer(x, k):
         return lax.ppermute(x, "exp", [(i ^ k, i) for i in range(n_exp)]) if k else x
 
-    packed, id_row, q_near, res_near = call(
+    packed, id_row, q_near, res_near, router = call(
         pack_kernel,
         (
             where,
             *[
                 pltpu.with_memory_space_constraint(x, pltpu.HBM)
-                for x in (expert_ids.T, rotated_keys, values, queries, residual)
+                for x in (expert_ids.T, rotated_keys, values, queries, residual, router_weight.T)
             ],
         ),
-        [SMEM] + [ANY] * 5,
-        [((tok, 2 * kv), BF16)] * 2 + [((tok, width), BF16)] * 2,
+        [SMEM] + [ANY] * 6,
+        [((tok, 2 * kv), BF16)] * 2 + [((tok, width), BF16)] * 2
+        + [((experts, d_model), BF16)],
         4,
-        [pltpu.VMEM((2, sub), jnp.int32), pltpu.SemaphoreType.DMA((5,))],
+        [pltpu.VMEM((2, sub), jnp.int32), pltpu.SemaphoreType.DMA((6,))],
     )
     near = [from_chip(packed, d) for d in range(n_chip)]
     id_rows = [from_peer(id_row, k) for k in range(n_exp)]
@@ -324,7 +327,6 @@
     )
     hidden_units = gate_weight.shape[2]
     gain = norm_gain.reshape(1, d_model)
-    router = router_weight.T
 
     half = n_chip // 2
     forward = list(range(half)) + list(range(n_chip - 1, half - 1, -1))

time: 155 us -> 155 us (level)
  transfers between devices with their start and end apart: 34 -> 34, of which waited for: 17 -> 17; matrix products, arithmetic and copies ran while one was open for 0% -> 0% of each run, Pallas kernels for 25% -> 26%
where the time goes in v4:
time: 155 us; the launch traced here: 154 us
  waiting for transfers between devices  69.8 us (45%)
  Pallas kernels  47.5 us (31%)
  starting transfers between devices  34.5 us (22%)
  other arithmetic  1.62 us (1%)
    pallas_call x20, Pallas kernels, call(): pl.pallas_call(ordered, in_specs=list(specs) + [ANY] * len(after), out_sp...  47.5 us
    ppermute x18, waiting for transfers between devices, from_peer(): lax.ppermute(x, 'exp', [(i ^ k, i) for i in range(n_exp)])  32.7 us
    ppermute x9, waiting for transfers between devices, from_chip(): return lax.ppermute(x, 'ctx', pairs) if d else x  30.8 us
    ppermute x18, starting transfers between devices, from_peer(): lax.ppermute(x, 'exp', [(i ^ k, i) for i in range(n_exp)])  15.8 us
    ppermute x9, starting transfers between devices, from_chip(): return lax.ppermute(x, 'ctx', pairs) if d else x  10.9 us
    ppermute x7, starting transfers between devices, from_core(): return lax.ppermute(x, 'ctx', [(i ^ 1, i) for i in range(n_ctx)])  7.81 us
    ppermute x7, waiting for transfers between devices, from_core(): return lax.ppermute(x, 'ctx', [(i ^ 1, i) for i in range(n_ctx)])  6.22 us
  transfers between devices with their start and end apart: 34, of which 17 were waited for; matrix products, arithmetic and copies ran while one was open for 0% of the time, Pallas kernels for 26%

profile of v4, /device:TPU:9, one launch (start us, length us, event | category | flops | bytes accessed | tf_op | source)
XLA Modules:
  0.0 154.4 jit_solution(15189413752805908944)
XLA Ops:
  0.7 1.7 %shard_map.109 = (bf16[96,512]{1,0:T(8,128)(2,1)S(1)}, bf16[96,512]{1,0:T(8,128)(2,1)S(1)}, bf16[96,1536]{1,0:T(8,128)(2,1)S(1)}, bf16[96,1536]{1,0:T(8,128)(2,1)S(1)}, bf16[4,6144]{1,0:T(4,128)(2,1)S(1)}) custom-call(s32[10]{0:T(128)S(1)} %pad_add_fusion.refs_0_, s32[2,24]{1,0:T(2,128)} %bitcast.5, bf16[96,256]{1,0:T(8,128)(2,1)} %refs_2_.4, ...), custom_call_target="tpu_custom_call" | custom-call | tf_op jit(solution)/shard_map/pallas_call | solution.py:27
  2.5 2.5 %collective-permute-start.1 = (bf16[96,512]{1,0:T(8,128)(2,1)S(1)}, bf16[96,512]{1,0:T(8,128)(2,1)S(1)}, u32[]{:S(2)}, u32[]{:S(2)}) collective-permute-start(bf16[96,512]{1,0:T(8,128)(2,1)S(1)} %get-tuple-element.63.refs_0_), channel_id=1, source_target_pairs={{16,0},{20,4},{24,8},{28,12},{0,16},{4,20},{8,24},{12,28},{17,1},{... | collective-permute-start | bytes 294920 | tf_op jit(solution)/shard_map/ppermute | solution.py:288
  5.0 2.2 %collective-permute-start.2 = (bf16[96,512]{1,0:T(8,128)(2,1)S(1)}, bf16[96,512]{1,0:T(8,128)(2,1)S(1)}, u32[]{:S(2)}, u32[]{:S(2)}) collective-permute-start(bf16[96,512]{1,0:T(8,128)(2,1)S(1)} %get-tuple-element.63.refs_0_), channel_id=1, source_target_pairs={{24,0},{28,4},{0,8},{4,12},{8,16},{12,20},{16,24},{20,28},{25,1},{... | collective-permute-start | bytes 294920 | tf_op jit(solution)/shard_map/ppermute | solution.py:288
  7.2 1.2 collective-permute-start.3
  8.4 1.2 collective-permute-start.4
  9.8 3.2 %collective-permute-done.2.refs_3_ = bf16[96,512]{1,0:T(8,128)(2,1)S(1)} collective-permute-done((bf16[96,512]{1,0:T(8,128)(2,1)S(1)}, bf16[96,512]{1,0:T(8,128)(2,1)S(1)}, u32[]{:S(2)}, u32[]{:S(2)}) %collective-permute-start.2) | collective-permute-done | bytes 98336 | tf_op jit(solution)/shard_map/ppermute | solution.py:288
  13.0 1.7 %collective-permute-done.5.refs_7_ = bf16[96,512]{1,0:T(8,128)(2,1)S(1)} collective-permute-done((bf16[96,512]{1,0:T(8,128)(2,1)S(1)}, bf16[96,512]{1,0:T(8,128)(2,1)S(1)}, u32[]{:S(2)}, u32[]{:S(2)}) %collective-permute-start.5) | collective-permute-done | bytes 98336 | tf_op jit(solution)/shard_map/ppermute | solution.py:294
  14.8 2.6 %collective-permute-start.6 = (bf16[384,512]{1,0:T(8,128)(2,1)S(1)}, bf16[384,512]{1,0:T(8,128)(2,1)S(1)}, u32[]{:S(2)}, u32[]{:S(2)}) collective-permute-start(bf16[384,512]{1,0:T(8,128)(2,1)S(1)} %get-tuple-element.65.refs_3_), channel_id=1, source_target_pairs={{4,0},{0,4},{12,8},{8,12},{20,16},{16,20},{28,24},{24,28},{5,1},{1... | collective-permute-start | bytes 1179656 | tf_op jit(solution)/shard_map/ppermute | solution.py:291
  17.3 1.3 collective-permute-done.6.refs_4_
  18.7 2.5 %shard_map.111.refs_1_ = bf16[112,1536]{1,0:T(8,128)(2,1)S(1)} custom-call(s32[10]{0:T(128)S(1)} %pad_add_fusion.refs_0_, bf16[96,1536]{1,0:T(8,128)(2,1)S(1)} %get-tuple-element.61.refs_1_, bf16[96,1536]{1,0:T(8,128)(2,1)S(1)} %get-tuple-element.62.refs_2_, bf16[384,512]{1,0:T(8,128)(2,1)S(1)} %get-tuple-element.65.refs_3_, ...), custom_call_target="tpu_custom_call" | custom-call | tf_op jit(solution)/shard_map/pallas_call | solution.py:27
  21.3 1.1 shard_map.112
  23.9 1.1 collective-permute-start.9
  25.0 1.4 collective-permute-start.14
  26.5 4.0 %collective-permute-done.7.refs_1_ = bf16[112,1536]{1,0:T(8,128)(2,1)S(1)} collective-permute-done((bf16[112,1536]{1,0:T(8,128)(2,1)S(1)}, bf16[112,1536]{1,0:T(8,128)(2,1)S(1)}, u32[]{:S(2)}, u32[]{:S(2)}) %collective-permute-start.7) | collective-permute-done | bytes 344096 | tf_op jit(solution)/shard_map/ppermute | solution.py:288
  30.8 3.0 %collective-permute-done.8.refs_2_.refs_6_ = bf16[72,1536]{1,0:T(8,128)(2,1)S(1)} collective-permute-done((bf16[72,1536]{1,0:T(8,128)(2,1)S(1)}, bf16[72,1536]{1,0:T(8,128)(2,1)S(1)}, u32[]{:S(2)}, u32[]{:S(2)}) %collective-permute-start.8) | collective-permute-done | bytes 221216 | tf_op jit(solution)/shard_map/ppermute | solution.py:294
  33.9 1.5 collective-permute-done.9.refs_3_.refs_7_
  35.4 1.1 shard_map.113
  37.5 1.7 %collective-permute-start.13 = (bf16[72,1536]{1,0:T(8,128)(2,1)S(1)}, bf16[72,1536]{1,0:T(8,128)(2,1)S(1)}, u32[]{:S(2)}, u32[]{:S(2)}) collective-permute-start(bf16[72,1536]{1,0:T(8,128)(2,1)S(1)} %get-tuple-element.79), channel_id=1, source_target_pairs={{3,0},{2,1},{1,2},{0,3},{7,4},{6,5},{5,6},{4,7},{11,8},{10,9},{9,1... | collective-permute-start | bytes 663560 | tf_op jit(solution)/shard_map/ppermute | solution.py:294
  39.9 4.0 %collective-permute-done.15.refs_2_ = bf16[112,1536]{1,0:T(8,128)(2,1)S(1)} collective-permute-done((bf16[112,1536]{1,0:T(8,128)(2,1)S(1)}, bf16[112,1536]{1,0:T(8,128)(2,1)S(1)}, u32[]{:S(2)}, u32[]{:S(2)}) %collective-permute-start.15) | collective-permute-done | bytes 344096 | tf_op jit(solution)/shard_map/ppermute | solution.py:288
  43.9 1.3 shard_map.114
  45.3 2.5 %collective-permute-done.13.refs_12_ = bf16[72,1536]{1,0:T(8,128)(2,1)S(1)} collective-permute-done((bf16[72,1536]{1,0:T(8,128)(2,1)S(1)}, bf16[72,1536]{1,0:T(8,128)(2,1)S(1)}, u32[]{:S(2)}, u32[]{:S(2)}) %collective-permute-start.13) | collective-permute-done | bytes 221216 | tf_op jit(solution)/shard_map/ppermute | solution.py:294
  47.8 1.8 %shard_map.115 = (bf16[144,6144]{1,0:T(8,128)(2,1)S(1)}, f32[144,128]{1,0:T(8,128)S(1)}) custom-call(s32[10]{0:T(128)S(1)} %pad_add_fusion.refs_0_, bf16[1,6144]{1,0:T(2,128)(2,1)S(1)} %reshape.3.refs_1_, bf16[4,6144]{1,0:T(4,128)(2,1)S(1)} %get-tuple-element.72.refs_2_, f32[72,128]{1,0:T(8,128)S(1)} %get-tuple-element.73.refs_3_, ...), custom_call_target="tpu_custom_call" | custom-call | tf_op jit(solution)/shard_map/pallas_call | solution.py:27
  49.7 1.7 %collective-permute-start.16 = (bf16[144,6144]{1,0:T(8,128)(2,1)S(1)}, bf16[144,6144]{1,0:T(8,128)(2,1)S(1)}, u32[]{:S(2)}, u32[]{:S(2)}) collective-permute-start(bf16[144,6144]{1,0:T(8,128)(2,1)S(1)} %get-tuple-element.81.refs_0_), channel_id=1, source_target_pairs={{4,0},{0,4},{12,8},{8,12},{20,16},{16,20},{28,24},{24,28},{5,1},{1... | collective-permute-start | bytes 5308424 | tf_op jit(solution)/shard_map/ppermute | solution.py:291
  51.4 1.7 %collective-permute-start.22 = (bf16[144,1536]{1,0:T(8,128)(2,1)S(1)}, bf16[144,1536]{1,0:T(8,128)(2,1)S(1)}, u32[]{:S(2)}, u32[]{:S(2)}) collective-permute-start(bf16[144,1536]{1,0:T(8,128)(2,1)S(1)} %get-tuple-element.94), channel_id=1, source_target_pairs={{1,0},{0,1},{3,2},{2,3},{5,4},{4,5},{7,6},{6,7},{9,8},{8,9},{11,10... | collective-permute-start | bytes 1327112 | tf_op jit(solution)/shard_map/ppermute | solution.py:294
  53.1 1.2 collective-permute-start.24
  54.7 10.0 %shard_map.116 = (bf16[288,1024]{1,0:T(8,128)(2,1)S(1)}, bf16[6144,1024]{1,0:T(8,128)(2,1)S(1)}, bf16[6144,1024]{1,0:T(8,128)(2,1)S(1)}) custom-call(bf16[144,6144]{1,0:T(8,128)(2,1)S(1)} %get-tuple-element.81.refs_0_, bf16[144,6144]{1,0:T(8,128)(2,1)S(1)} %collective-permute-done.16.refs_1_, bf16[1,6144,1024]{2,1,0:T(8,128)(2,1)} %refs_2_.5, ...), custom_call_target="tpu_custom_call" | custom-call | tf_op jit(solution)/shard_map/pallas_call | solution.py:27
  64.8 4.7 %shard_map.117 = (bf16[144,3072]{1,0:T(8,128)(2,1)S(1)}, bf16[144,3072]{1,0:T(8,128)(2,1)S(1)}, bf16[2,1024,1536]{2,1,0:T(8,128)(2,1)S(1)}) custom-call(s32[10]{0:T(128)S(1)} %pad_add_fusion.refs_0_, bf16[288,1024]{1,0:T(8,128)(2,1)S(1)} %get-tuple-element.82.refs_1_, bf16[1,1024,6144]{2,1,0:T(8,128)(2,1)} %refs_2_.7), custom_call_target="tpu_custom_call" | custom-call | tf_op jit(solution)/shard_map/pallas_call | solution.py:27
  69.4 4.6 %shard_map.118 = (bf16[144,3072]{1,0:T(8,128)(2,1)S(1)}, bf16[144,3072]{1,0:T(8,128)(2,1)S(1)}, bf16[2,1024,1536]{2,1,0:T(8,128)(2,1)S(1)}) custom-call(s32[10]{0:T(128)S(1)} %pad_add_fusion.refs_0_, bf16[288,1024]{1,0:T(8,128)(2,1)S(1)} %get-tuple-element.82.refs_1_, bf16[1,1024,6144]{2,1,0:T(8,128)(2,1)} %refs_2_.7, ...), custom_call_target="tpu_custom_call" | custom-call | tf_op jit(solution)/shard_map/pallas_call | solution.py:27
  74.1 2.1 %shard_map.121 = (bf16[144,6144]{1,0:T(8,128)(2,1)S(1)}, f32[144,128]{1,0:T(8,128)S(1)}) custom-call(s32[10]{0:T(128)S(1)} %pad_add_fusion.refs_0_, bf16[1,6144]{1,0:T(2,128)(2,1)S(1)} %reshape.3.refs_1_, bf16[4,6144]{1,0:T(4,128)(2,1)S(1)} %get-tuple-element.72.refs_2_, f32[72,128]{1,0:T(8,128)S(1)} %get-tuple-element.80.refs_13_.refs_3_, ...), custom_call_target="tpu_custom_call" | custom-call | tf_op jit(solution)/shard_map/pallas_call | solution.py:27
  76.2 1.1 collective-permute-start.25
  77.8 4.1 %collective-permute-done.18.refs_1_ = bf16[144,3072]{1,0:T(8,128)(2,1)S(1)} collective-permute-done((bf16[144,3072]{1,0:T(8,128)(2,1)S(1)}, bf16[144,3072]{1,0:T(8,128)(2,1)S(1)}, u32[]{:S(2)}, u32[]{:S(2)}) %collective-permute-start.18) | collective-permute-done | bytes 884768 | tf_op jit(solution)/shard_map/ppermute | solution.py:291
  82.4 0.9 collective-permute-start.21
  83.9 7.7 %shard_map.122.refs_1_ = bf16[288,1024]{1,0:T(8,128)(2,1)S(1)} custom-call(bf16[144,6144]{1,0:T(8,128)(2,1)S(1)} %get-tuple-element.97.refs_0_, bf16[144,6144]{1,0:T(8,128)(2,1)S(1)} %collective-permute-done.25.refs_1_, bf16[6144,1024]{1,0:T(8,128)(2,1)S(1)} %get-tuple-element.98.refs_2_, bf16[6144,1024]{1,0:T(8,128)(2,1)S(1)} %get-tuple-element.99.refs_3_, ...), custom_call_target="tpu_custom_call" | custom-call | tf_op jit(solution)/shard_map/pallas_call | solution.py:27
  91.6 2.6 %shard_map.123 = (bf16[144,3072]{1,0:T(8,128)(2,1)S(1)}, bf16[144,3072]{1,0:T(8,128)(2,1)S(1)}) custom-call(s32[10]{0:T(128)S(1)} %pad_add_fusion.refs_0_, bf16[288,1024]{1,0:T(8,128)(2,1)S(1)} %shard_map.122.refs_1_, bf16[2,1024,1536]{2,1,0:T(8,128)(2,1)S(1)} %get-tuple-element.101.refs_2_), custom_call_target="tpu_custom_call" | custom-call | tf_op jit(solution)/shard_map/pallas_call | solution.py:27
  94.9 2.6 %shard_map.124 = (bf16[144,3072]{1,0:T(8,128)(2,1)S(1)}, bf16[144,3072]{1,0:T(8,128)(2,1)S(1)}) custom-call(s32[10]{0:T(128)S(1)} %pad_add_fusion.refs_0_, bf16[288,1024]{1,0:T(8,128)(2,1)S(1)} %shard_map.122.refs_1_, bf16[2,1024,1536]{2,1,0:T(8,128)(2,1)S(1)} %get-tuple-element.100.refs_2_, bf16[144,3072]{1,0:T(8,128)(2,1)S(1)} %get-tuple-element.102.refs_3_.refs_0_, ...), custom_call_target="tpu_custom_call" | custom-call | tf_op jit(solution)/shard_map/pallas_call | solution.py:27
  97.5 1.2 collective-permute-start.26
  98.7 1.0 collective-permute-start.19
  101.3 1.1 collective-permute-start.29
  102.8 1.2 collective-permute-start.31
  104.0 6.4 %collective-permute-done.19.refs_3_ = bf16[144,1536]{1,0:T(8,128)(2,1)S(1)} collective-permute-done((bf16[144,1536]{1,0:T(8,128)(2,1)S(1)}, bf16[144,1536]{1,0:T(8,128)(2,1)S(1)}, u32[]{:S(2)}, u32[]{:S(2)}) %collective-permute-start.19) | collective-permute-done | bytes 442400 | tf_op jit(solution)/shard_map/ppermute | solution.py:294
  111.9 1.4 collective-permute-start.28
  113.3 6.6 %collective-permute-done.29.refs_3_ = bf16[144,1536]{1,0:T(8,128)(2,1)S(1)} collective-permute-done((bf16[144,1536]{1,0:T(8,128)(2,1)S(1)}, bf16[144,1536]{1,0:T(8,128)(2,1)S(1)}, u32[]{:S(2)}, u32[]{:S(2)}) %collective-permute-start.29) | collective-permute-done | bytes 442400 | tf_op jit(solution)/shard_map/ppermute | solution.py:294
  119.9 10.2 %collective-permute-done.30.refs_4_ = bf16[144,1536]{1,0:T(8,128)(2,1)S(1)} collective-permute-done((bf16[144,1536]{1,0:T(8,128)(2,1)S(1)}, bf16[144,1536]{1,0:T(8,128)(2,1)S(1)}, u32[]{:S(2)}, u32[]{:S(2)}) %collective-permute-start.30) | collective-permute-done | bytes 442400 | tf_op jit(solution)/shard_map/ppermute | solution.py:294
  130.9 1.8 %collective-permute-start.32 = (bf16[96,1536]{1,0:T(8,128)(2,1)S(1)}, bf16[96,1536]{1,0:T(8,128)(2,1)S(1)}, u32[]{:S(2)}, u32[]{:S(2)}) collective-permute-start(bf16[96,1536]{1,0:T(8,128)(2,1)S(1)} %get-tuple-element.115), channel_id=1, source_target_pairs={{16,0},{20,4},{24,8},{28,12},{0,16},{4,20},{8,24},{12,28},{17,1},{... | collective-permute-start | bytes 884744 | tf_op jit(solution)/shard_map/ppermute | solution.py:288
  132.7 1.2 collective-permute-start.33
  133.9 17.2 %collective-permute-done.32 = bf16[96,1536]{1,0:T(8,128)(2,1)S(1)} collective-permute-done((bf16[96,1536]{1,0:T(8,128)(2,1)S(1)}, bf16[96,1536]{1,0:T(8,128)(2,1)S(1)}, u32[]{:S(2)}, u32[]{:S(2)}) %collective-permute-start.32) | collective-permute-done | bytes 294944 | tf_op jit(solution)/shard_map/ppermute | solution.py:288
  151.1 2.4 %collective-permute-done.33 = bf16[96,1536]{1,0:T(8,128)(2,1)S(1)} collective-permute-done((bf16[96,1536]{1,0:T(8,128)(2,1)S(1)}, bf16[96,1536]{1,0:T(8,128)(2,1)S(1)}, u32[]{:S(2)}, u32[]{:S(2)}) %collective-permute-start.33) | collective-permute-done | bytes 294944 | tf_op jit(solution)/shard_map/ppermute | solution.py:288
  153.5 0.9 add_convert_fusion
  (43 shorter events, 11.8 us)
Async XLA Ops:
  2.5 7.2 %collective-permute-start = (bf16[96,512]{1,0:T(8,128)(2,1)S(1)}, bf16[96,512]{1,0:T(8,128)(2,1)S(1)}, u32[]{:S(2)}, u32[]{:S(2)}) collective-permute-start(bf16[96,512]{1,0:T(8,128)(2,1)S(1)} %get-tuple-element.63.refs_0_), channel_id=1, source_target_pairs={{8,0},{12,4},{16,8},{20,12},{24,16},{28,20},{0,24},{4,28},{9,1},{1... | collective-permute-start | bytes 294920 | tf_op jit(solution)/shard_map/ppermute | solution.py:288
  2.5 7.3 %collective-permute-start.1 = (bf16[96,512]{1,0:T(8,128)(2,1)S(1)}, bf16[96,512]{1,0:T(8,128)(2,1)S(1)}, u32[]{:S(2)}, u32[]{:S(2)}) collective-permute-start(bf16[96,512]{1,0:T(8,128)(2,1)S(1)} %get-tuple-element.63.refs_0_), channel_id=1, source_target_pairs={{16,0},{20,4},{24,8},{28,12},{0,16},{4,20},{8,24},{12,28},{17,1},{... | collective-permute-start | bytes 294920 | tf_op jit(solution)/shard_map/ppermute | solution.py:288
  5.0 8.1 %collective-permute-start.2 = (bf16[96,512]{1,0:T(8,128)(2,1)S(1)}, bf16[96,512]{1,0:T(8,128)(2,1)S(1)}, u32[]{:S(2)}, u32[]{:S(2)}) collective-permute-start(bf16[96,512]{1,0:T(8,128)(2,1)S(1)} %get-tuple-element.63.refs_0_), channel_id=1, source_target_pairs={{24,0},{28,4},{0,8},{4,12},{8,16},{12,20},{16,24},{20,28},{25,1},{... | collective-permute-start | bytes 294920 | tf_op jit(solution)/shard_map/ppermute | solution.py:288
  7.2 5.9 %collective-permute-start.3 = (bf16[96,512]{1,0:T(8,128)(2,1)S(1)}, bf16[96,512]{1,0:T(8,128)(2,1)S(1)}, u32[]{:S(2)}, u32[]{:S(2)}) collective-permute-start(bf16[96,512]{1,0:T(8,128)(2,1)S(1)} %get-tuple-element.64.refs_4_), channel_id=1, source_target_pairs={{1,0},{0,1},{3,2},{2,3},{5,4},{4,5},{7,6},{6,7},{9,8},{8,9},{11,10... | collective-permute-start | bytes 294920 | tf_op jit(solution)/shard_map/ppermute | solution.py:294
  8.4 4.7 %collective-permute-start.4 = (bf16[96,512]{1,0:T(8,128)(2,1)S(1)}, bf16[96,512]{1,0:T(8,128)(2,1)S(1)}, u32[]{:S(2)}, u32[]{:S(2)}) collective-permute-start(bf16[96,512]{1,0:T(8,128)(2,1)S(1)} %get-tuple-element.64.refs_4_), channel_id=1, source_target_pairs={{2,0},{3,1},{0,2},{1,3},{6,4},{7,5},{4,6},{5,7},{10,8},{11,9},{8,1... | collective-permute-start | bytes 294920 | tf_op jit(solution)/shard_map/ppermute | solution.py:294
  9.6 5.1 %collective-permute-start.5 = (bf16[96,512]{1,0:T(8,128)(2,1)S(1)}, bf16[96,512]{1,0:T(8,128)(2,1)S(1)}, u32[]{:S(2)}, u32[]{:S(2)}) collective-permute-start(bf16[96,512]{1,0:T(8,128)(2,1)S(1)} %get-tuple-element.64.refs_4_), channel_id=1, source_target_pairs={{3,0},{2,1},{1,2},{0,3},{7,4},{6,5},{5,6},{4,7},{11,8},{10,9},{9,1... | collective-permute-start | bytes 294920 | tf_op jit(solution)/shard_map/ppermute | solution.py:294
  14.8 3.9 %collective-permute-start.6 = (bf16[384,512]{1,0:T(8,128)(2,1)S(1)}, bf16[384,512]{1,0:T(8,128)(2,1)S(1)}, u32[]{:S(2)}, u32[]{:S(2)}) collective-permute-start(bf16[384,512]{1,0:T(8,128)(2,1)S(1)} %get-tuple-element.65.refs_3_), channel_id=1, source_target_pairs={{4,0},{0,4},{12,8},{8,12},{20,16},{16,20},{28,24},{24,28},{5,1},{1... | collective-permute-start | bytes 1179656 | tf_op jit(solution)/shard_map/ppermute | solution.py:291
  21.2 9.3 %collective-permute-start.7 = (bf16[112,1536]{1,0:T(8,128)(2,1)S(1)}, bf16[112,1536]{1,0:T(8,128)(2,1)S(1)}, u32[]{:S(2)}, u32[]{:S(2)}) collective-permute-start(bf16[112,1536]{1,0:T(8,128)(2,1)S(1)} %shard_map.111.refs_1_), channel_id=1, source_target_pairs={{8,0},{12,4},{16,8},{20,12},{24,16},{28,20},{0,24},{4,28},{9,1},{1... | collective-permute-start | bytes 1032200 | tf_op jit(solution)/shard_map/ppermute | solution.py:288
  22.3 8.5 %collective-permute-start.10 = (bf16[72,1536]{1,0:T(8,128)(2,1)S(1)}, bf16[72,1536]{1,0:T(8,128)(2,1)S(1)}, u32[]{:S(2)}, u32[]{:S(2)}) collective-permute-start(bf16[72,1536]{1,0:T(8,128)(2,1)S(1)} %get-tuple-element.70), channel_id=1, source_target_pairs={{3,0},{2,1},{1,2},{0,3},{7,4},{6,5},{5,6},{4,7},{11,8},{10,9},{9,1... | collective-permute-start | bytes 663560 | tf_op jit(solution)/shard_map/ppermute | solution.py:294
  23.1 10.8 %collective-permute-start.8 = (bf16[72,1536]{1,0:T(8,128)(2,1)S(1)}, bf16[72,1536]{1,0:T(8,128)(2,1)S(1)}, u32[]{:S(2)}, u32[]{:S(2)}) collective-permute-start(bf16[72,1536]{1,0:T(8,128)(2,1)S(1)} %get-tuple-element.68), channel_id=1, source_target_pairs={{1,0},{0,1},{3,2},{2,3},{5,4},{4,5},{7,6},{6,7},{9,8},{8,9},{11,10... | collective-permute-start | bytes 663560 | tf_op jit(solution)/shard_map/ppermute | solution.py:294
  23.9 11.5 %collective-permute-start.9 = (bf16[72,1536]{1,0:T(8,128)(2,1)S(1)}, bf16[72,1536]{1,0:T(8,128)(2,1)S(1)}, u32[]{:S(2)}, u32[]{:S(2)}) collective-permute-start(bf16[72,1536]{1,0:T(8,128)(2,1)S(1)} %get-tuple-element.69), channel_id=1, source_target_pairs={{2,0},{3,1},{0,2},{1,3},{6,4},{7,5},{4,6},{5,7},{10,8},{11,9},{8,1... | collective-permute-start | bytes 663560 | tf_op jit(solution)/shard_map/ppermute | solution.py:294
  25.0 14.9 %collective-permute-start.14 = (bf16[112,1536]{1,0:T(8,128)(2,1)S(1)}, bf16[112,1536]{1,0:T(8,128)(2,1)S(1)}, u32[]{:S(2)}, u32[]{:S(2)}) collective-permute-start(bf16[112,1536]{1,0:T(8,128)(2,1)S(1)} %shard_map.111.refs_1_), channel_id=1, source_target_pairs={{24,0},{28,4},{0,8},{4,12},{8,16},{12,20},{16,24},{20,28},{25,1},{... | collective-permute-start | bytes 1032200 | tf_op jit(solution)/shard_map/ppermute | solution.py:288
  30.5 13.4 %collective-permute-start.15 = (bf16[112,1536]{1,0:T(8,128)(2,1)S(1)}, bf16[112,1536]{1,0:T(8,128)(2,1)S(1)}, u32[]{:S(2)}, u32[]{:S(2)}) collective-permute-start(bf16[112,1536]{1,0:T(8,128)(2,1)S(1)} %collective-permute-done.7.refs_1_), channel_id=1, source_target_pairs={{8,0},{12,4},{16,8},{20,12},{24,16},{28,20},{0,24},{4,28},{9,1},{1... | collective-permute-start | bytes 1032200 | tf_op jit(solution)/shard_map/ppermute | solution.py:288
  36.5 8.8 %collective-permute-start.11 = (bf16[72,1536]{1,0:T(8,128)(2,1)S(1)}, bf16[72,1536]{1,0:T(8,128)(2,1)S(1)}, u32[]{:S(2)}, u32[]{:S(2)}) collective-permute-start(bf16[72,1536]{1,0:T(8,128)(2,1)S(1)} %get-tuple-element.77), channel_id=1, source_target_pairs={{1,0},{0,1},{3,2},{2,3},{5,4},{4,5},{7,6},{6,7},{9,8},{8,9},{11,10... | collective-permute-start | bytes 663560 | tf_op jit(solution)/shard_map/ppermute | solution.py:294
  36.8 8.5 %collective-permute-start.12 = (bf16[72,1536]{1,0:T(8,128)(2,1)S(1)}, bf16[72,1536]{1,0:T(8,128)(2,1)S(1)}, u32[]{:S(2)}, u32[]{:S(2)}) collective-permute-start(bf16[72,1536]{1,0:T(8,128)(2,1)S(1)} %get-tuple-element.78), channel_id=1, source_target_pairs={{2,0},{3,1},{0,2},{1,3},{6,4},{7,5},{4,6},{5,7},{10,8},{11,9},{8,1... | collective-permute-start | bytes 663560 | tf_op jit(solution)/shard_map/ppermute | solution.py:294
  37.5 10.4 %collective-permute-start.13 = (bf16[72,1536]{1,0:T(8,128)(2,1)S(1)}, bf16[72,1536]{1,0:T(8,128)(2,1)S(1)}, u32[]{:S(2)}, u32[]{:S(2)}) collective-permute-start(bf16[72,1536]{1,0:T(8,128)(2,1)S(1)} %get-tuple-element.79), channel_id=1, source_target_pairs={{3,0},{2,1},{1,2},{0,3},{7,4},{6,5},{5,6},{4,7},{11,8},{10,9},{9,1... | collective-permute-start | bytes 663560 | tf_op jit(solution)/shard_map/ppermute | solution.py:294
  49.7 5.1 %collective-permute-start.16 = (bf16[144,6144]{1,0:T(8,128)(2,1)S(1)}, bf16[144,6144]{1,0:T(8,128)(2,1)S(1)}, u32[]{:S(2)}, u32[]{:S(2)}) collective-permute-start(bf16[144,6144]{1,0:T(8,128)(2,1)S(1)} %get-tuple-element.81.refs_0_), channel_id=1, source_target_pairs={{4,0},{0,4},{12,8},{8,12},{20,16},{16,20},{28,24},{24,28},{5,1},{1... | collective-permute-start | bytes 5308424 | tf_op jit(solution)/shard_map/ppermute | solution.py:291
  51.4 22.7 %collective-permute-start.22 = (bf16[144,1536]{1,0:T(8,128)(2,1)S(1)}, bf16[144,1536]{1,0:T(8,128)(2,1)S(1)}, u32[]{:S(2)}, u32[]{:S(2)}) collective-permute-start(bf16[144,1536]{1,0:T(8,128)(2,1)S(1)} %get-tuple-element.94), channel_id=1, source_target_pairs={{1,0},{0,1},{3,2},{2,3},{5,4},{4,5},{7,6},{6,7},{9,8},{8,9},{11,10... | collective-permute-start | bytes 1327112 | tf_op jit(solution)/shard_map/ppermute | solution.py:294
  53.1 21.0 %collective-permute-start.23 = (bf16[144,1536]{1,0:T(8,128)(2,1)S(1)}, bf16[144,1536]{1,0:T(8,128)(2,1)S(1)}, u32[]{:S(2)}, u32[]{:S(2)}) collective-permute-start(bf16[144,1536]{1,0:T(8,128)(2,1)S(1)} %get-tuple-element.95), channel_id=1, source_target_pairs={{2,0},{3,1},{0,2},{1,3},{6,4},{7,5},{4,6},{5,7},{10,8},{11,9},{8,1... | collective-permute-start | bytes 1327112 | tf_op jit(solution)/shard_map/ppermute | solution.py:294
  53.1 21.0 %collective-permute-start.24 = (bf16[144,1536]{1,0:T(8,128)(2,1)S(1)}, bf16[144,1536]{1,0:T(8,128)(2,1)S(1)}, u32[]{:S(2)}, u32[]{:S(2)}) collective-permute-start(bf16[144,1536]{1,0:T(8,128)(2,1)S(1)} %get-tuple-element.96), channel_id=1, source_target_pairs={{3,0},{2,1},{1,2},{0,3},{7,4},{6,5},{5,6},{4,7},{11,8},{10,9},{9,1... | collective-permute-start | bytes 1327112 | tf_op jit(solution)/shard_map/ppermute | solution.py:294
  76.2 7.7 %collective-permute-start.25 = (bf16[144,6144]{1,0:T(8,128)(2,1)S(1)}, bf16[144,6144]{1,0:T(8,128)(2,1)S(1)}, u32[]{:S(2)}, u32[]{:S(2)}) collective-permute-start(bf16[144,6144]{1,0:T(8,128)(2,1)S(1)} %get-tuple-element.97.refs_0_), channel_id=1, source_target_pairs={{4,0},{0,4},{12,8},{8,12},{20,16},{16,20},{28,24},{24,28},{5,1},{1... | collective-permute-start | bytes 5308424 | tf_op jit(solution)/shard_map/ppermute | solution.py:291
  77.3 4.6 %collective-permute-start.18 = (bf16[144,3072]{1,0:T(8,128)(2,1)S(1)}, bf16[144,3072]{1,0:T(8,128)(2,1)S(1)}, u32[]{:S(2)}, u32[]{:S(2)}) collective-permute-start(bf16[144,3072]{1,0:T(8,128)(2,1)S(1)} %get-tuple-element.87), channel_id=1, source_target_pairs={{4,0},{0,4},{12,8},{8,12},{20,16},{16,20},{28,24},{24,28},{5,1},{1... | collective-permute-start | bytes 2654216 | tf_op jit(solution)/shard_map/ppermute | solution.py:291
  77.4 6.0 %collective-permute-start.17 = (bf16[144,3072]{1,0:T(8,128)(2,1)S(1)}, bf16[144,3072]{1,0:T(8,128)(2,1)S(1)}, u32[]{:S(2)}, u32[]{:S(2)}) collective-permute-start(bf16[144,3072]{1,0:T(8,128)(2,1)S(1)} %get-tuple-element.85), channel_id=1, source_target_pairs={{4,0},{0,4},{12,8},{8,12},{20,16},{16,20},{28,24},{24,28},{5,1},{1... | collective-permute-start | bytes 2654216 | tf_op jit(solution)/shard_map/ppermute | solution.py:291
  82.4 12.4 %collective-permute-start.21 = (bf16[144,1536]{1,0:T(8,128)(2,1)S(1)}, bf16[144,1536]{1,0:T(8,128)(2,1)S(1)}, u32[]{:S(2)}, u32[]{:S(2)}) collective-permute-start(bf16[144,1536]{1,0:T(8,128)(2,1)S(1)} %get-tuple-element.88.refs_3_), channel_id=1, source_target_pairs={{3,0},{2,1},{1,2},{0,3},{7,4},{6,5},{5,6},{4,7},{11,8},{10,9},{9,1... | collective-permute-start | bytes 1327112 | tf_op jit(solution)/shard_map/ppermute | solution.py:294
  94.2 5.7 %collective-permute-start.27 = (bf16[144,3072]{1,0:T(8,128)(2,1)S(1)}, bf16[144,3072]{1,0:T(8,128)(2,1)S(1)}, u32[]{:S(2)}, u32[]{:S(2)}) collective-permute-start(bf16[144,3072]{1,0:T(8,128)(2,1)S(1)} %get-tuple-element.106), channel_id=1, source_target_pairs={{4,0},{0,4},{12,8},{8,12},{20,16},{16,20},{28,24},{24,28},{5,1},{1... | collective-permute-start | bytes 2654216 | tf_op jit(solution)/shard_map/ppermute | solution.py:291
  97.5 3.2 %collective-permute-start.26 = (bf16[144,3072]{1,0:T(8,128)(2,1)S(1)}, bf16[144,3072]{1,0:T(8,128)(2,1)S(1)}, u32[]{:S(2)}, u32[]{:S(2)}) collective-permute-start(bf16[144,3072]{1,0:T(8,128)(2,1)S(1)} %get-tuple-element.104), channel_id=1, source_target_pairs={{4,0},{0,4},{12,8},{8,12},{20,16},{16,20},{28,24},{24,28},{5,1},{1... | collective-permute-start | bytes 2654216 | tf_op jit(solution)/shard_map/ppermute | solution.py:291
  98.7 11.7 %collective-permute-start.19 = (bf16[144,1536]{1,0:T(8,128)(2,1)S(1)}, bf16[144,1536]{1,0:T(8,128)(2,1)S(1)}, u32[]{:S(2)}, u32[]{:S(2)}) collective-permute-start(bf16[144,1536]{1,0:T(8,128)(2,1)S(1)} %get-tuple-element.90.refs_4_), channel_id=1, source_target_pairs={{1,0},{0,1},{3,2},{2,3},{5,4},{4,5},{7,6},{6,7},{9,8},{8,9},{11,10... | collective-permute-start | bytes 1327112 | tf_op jit(solution)/shard_map/ppermute | solution.py:294
  99.7 11.4 %collective-permute-start.20 = (bf16[144,1536]{1,0:T(8,128)(2,1)S(1)}, bf16[144,1536]{1,0:T(8,128)(2,1)S(1)}, u32[]{:S(2)}, u32[]{:S(2)}) collective-permute-start(bf16[144,1536]{1,0:T(8,128)(2,1)S(1)} %get-tuple-element.91), channel_id=1, source_target_pairs={{2,0},{3,1},{0,2},{1,3},{6,4},{7,5},{4,6},{5,7},{10,8},{11,9},{8,1... | collective-permute-start | bytes 1327112 | tf_op jit(solution)/shard_map/ppermute | solution.py:294
  101.3 18.6 %collective-permute-start.29 = (bf16[144,1536]{1,0:T(8,128)(2,1)S(1)}, bf16[144,1536]{1,0:T(8,128)(2,1)S(1)}, u32[]{:S(2)}, u32[]{:S(2)}) collective-permute-start(bf16[144,1536]{1,0:T(8,128)(2,1)S(1)} %get-tuple-element.108.refs_6_), channel_id=1, source_target_pairs={{1,0},{0,1},{3,2},{2,3},{5,4},{4,5},{7,6},{6,7},{9,8},{8,9},{11,10... | collective-permute-start | bytes 1327112 | tf_op jit(solution)/shard_map/ppermute | solution.py:294
  102.3 27.7 %collective-permute-start.30 = (bf16[144,1536]{1,0:T(8,128)(2,1)S(1)}, bf16[144,1536]{1,0:T(8,128)(2,1)S(1)}, u32[]{:S(2)}, u32[]{:S(2)}) collective-permute-start(bf16[144,1536]{1,0:T(8,128)(2,1)S(1)} %get-tuple-element.114), channel_id=1, source_target_pairs={{2,0},{3,1},{0,2},{1,3},{6,4},{7,5},{4,6},{5,7},{10,8},{11,9},{8,1... | collective-permute-start | bytes 1327112 | tf_op jit(solution)/shard_map/ppermute | solution.py:294
  102.8 27.3 %collective-permute-start.31 = (bf16[144,1536]{1,0:T(8,128)(2,1)S(1)}, bf16[144,1536]{1,0:T(8,128)(2,1)S(1)}, u32[]{:S(2)}, u32[]{:S(2)}) collective-permute-start(bf16[144,1536]{1,0:T(8,128)(2,1)S(1)} %get-tuple-element.107.refs_3_), channel_id=1, source_target_pairs={{3,0},{2,1},{1,2},{0,3},{7,4},{6,5},{5,6},{4,7},{11,8},{10,9},{9,1... | collective-permute-start | bytes 1327112 | tf_op jit(solution)/shard_map/ppermute | solution.py:294
  111.9 22.0 %collective-permute-start.28 = (bf16[96,1536]{1,0:T(8,128)(2,1)S(1)}, bf16[96,1536]{1,0:T(8,128)(2,1)S(1)}, u32[]{:S(2)}, u32[]{:S(2)}) collective-permute-start(bf16[96,1536]{1,0:T(8,128)(2,1)S(1)} %get-tuple-element.110), channel_id=1, source_target_pairs={{24,0},{28,4},{0,8},{4,12},{8,16},{12,20},{16,24},{20,28},{25,1},{... | collective-permute-start | bytes 884744 | tf_op jit(solution)/shard_map/ppermute | solution.py:288
  130.9 20.2 %collective-permute-start.32 = (bf16[96,1536]{1,0:T(8,128)(2,1)S(1)}, bf16[96,1536]{1,0:T(8,128)(2,1)S(1)}, u32[]{:S(2)}, u32[]{:S(2)}) collective-permute-start(bf16[96,1536]{1,0:T(8,128)(2,1)S(1)} %get-tuple-element.115), channel_id=1, source_target_pairs={{16,0},{20,4},{24,8},{28,12},{0,16},{4,20},{8,24},{12,28},{17,1},{... | collective-permute-start | bytes 884744 | tf_op jit(solution)/shard_map/ppermute | solution.py:288
  132.7 20.8 %collective-permute-start.33 = (bf16[96,1536]{1,0:T(8,128)(2,1)S(1)}, bf16[96,1536]{1,0:T(8,128)(2,1)S(1)}, u32[]{:S(2)}, u32[]{:S(2)}) collective-permute-start(bf16[96,1536]{1,0:T(8,128)(2,1)S(1)} %get-tuple-element.116), channel_id=1, source_target_pairs={{8,0},{12,4},{16,8},{20,12},{24,16},{28,20},{0,24},{4,28},{9,1},{1... | collective-permute-start | bytes 884744 | tf_op jit(solution)/shard_map/ppermute | solution.py:288
